TPU v7x, 256 devices: a whole 4x4x8 slice. The times are simulated.
256 devices in a mesh: gx: 4 (over x), gy: 4 (over y), gz: 16 (over z, core).
Axes of the slice: x: 4, y: 4, z: 8, core: 2. Of those that a mesh axis runs over, the one named last changes fastest.
Arguments:
- positions: float32 [3, 8, 8, 2048], P(None, 'gx', 'gy', 'gz'), may hold values from -0.5 to 0.5
- velocities: float32 [3, 8, 8, 2048], P(None, 'gx', 'gy', 'gz'), may hold values from -2 to 2
- forces_in: float32 [3, 8, 8, 2048], P(None, 'gx', 'gy', 'gz'), may hold values from -6 to 6
- counts: int32 [8, 8, 64], P('gx', 'gy', 'gz'), may hold values from 0 to 32, as said below
- neighbours: int32 [24, 8, 8, 2048], P(None, 'gx', 'gy', 'gz'), may hold values from 0 to 863, as said below
- send_list: int32 [4, 4, 8192], P('gx', 'gy', 'gz'), may hold values from -1 to 511, as said below
- w_radial: float32 [8, 128], replicated, may hold values from -2 to 2
- w_env: bfloat16 [128, 128], replicated, may hold values from -0.5 to 0.5
- w_latent: bfloat16 [256, 128], replicated, may hold values from -0.375 to 0.375
- w_out: bfloat16 [128], replicated, may hold values from -0.5 to 0.5
Outputs:
- positions_out: float32 [3, 8, 8, 2048], P(None, 'gx', 'gy', 'gz')
- velocities_out: float32 [3, 8, 8, 2048], P(None, 'gx', 'gy', 'gz')
- forces_out: float32 [3, 8, 8, 2048], P(None, 'gx', 'gy', 'gz')
- work_energy: float32 [4, 4, 8192], P('gx', 'gy', 'gz')
Inputs may be any that keep to these rules, and one draw needn't show every extreme that they name: `counts`: A cell's occupied slots are its first ones. The devices of one gz group hold 4096 occupied slots together, and one of them has every slot occupied. `neighbours`: an entry never names the atom itself; entries naming unoccupied slots are padding. `send_list`: every occupied slot appears exactly once in its device's list, unoccupied ones never; each device receives exactly 256 atoms over all senders, and some sender fills all 32 rows for every receiver.
All inputs are finite; a program needn't handle non-finite values.
Results may differ from a plain program's by a relative error of at most 0.035.
Values sent between devices are 32-bit elements; how exact they have to be, the bound alone decides.
No kernel may reach another device: no remote copies, remote signals or barrier semaphores. Data moves between devices by JAX's collectives and lax.ppermute only.
A program may use at most 128 MiB of HBM per device.

v0:
```python
import functools

import jax
import jax.numpy as jnp
from jax import lax
from jax.experimental import pallas as pl
from jax.experimental.pallas import tpu as pltpu
from jax.sharding import PartitionSpec as P

STEPS = 2
TIME_STEP = 0.5
BASIS = 8
CENTRE_FIRST = 0.5
CENTRE_STEP = 1.5 / 7.0
UNOCCUPIED = 1e30
FAR = 3.0
F32 = jnp.float32
BF16 = jnp.bfloat16

CELLS = 16
ROWS = 8
USED = 6
TILES = 3


def dot(a, b):
    return lax.dot_general(a, b, (((1,), (0,)), ((), ())), preferred_element_type=F32)


def dot_nt(a, b):
    return lax.dot_general(a, b, (((1,), (1,)), ((), ())), preferred_element_type=F32)


def pair_row(block, t):
    return jnp.concatenate([block[2 * t : 2 * t + 1], block[2 * t + 1 : 2 * t + 2]], axis=1)


def lane_pick(line, place, shape):
    table = jnp.broadcast_to(line, shape)
    return jnp.take_along_axis(table, place, axis=1, mode="promise_in_bounds")


def force_kernel(blocks, layers, first, last, *refs):
    refs = list(refs)
    outer = len(layers) == 1
    base = layers[0] // 3 * 64 if outer else 32
    tab_ref, key_ref = refs[:2]
    wr_ref, wtf_ref, wtop_ref, webf_ref, web_ref, wo_ref = refs[2:8]
    refs = refs[8:]
    if outer:
        halo_ref = refs.pop(0)
    if not first:
        before_ref, site_before_ref = refs[:2]
        refs = refs[2:]
    if last:
        list_ref = refs.pop(0)
    spread_ref, site_ref, extra_ref = refs[:3]
    geo, res, acc, own_sum, table_ref = refs[3:8]
    cells = [(block, layer) for block in blocks for layer in layers]
    count = len(cells)
    works, slopes = refs[8 : 8 + count], refs[8 + count :]
    if outer:
        lane48 = lax.broadcasted_iota(jnp.int32, (48, 128), 1)
        halo = jnp.concatenate([halo_ref[...], jnp.zeros((48, 96), F32)], axis=1)
        if base == 0:
            table_ref[...] = jnp.where(lane48 < 32, halo, pltpu.roll(tab_ref[...], 32, 1))
        else:
            table_ref[...] = jnp.where(
                lane48 < 96, pltpu.roll(tab_ref[...], 96, 1), pltpu.roll(halo, 96, 1)
            )
    else:
        table_ref = tab_ref
    high = len(layers)
    shape = (high * ROWS, 128)
    lane = lax.broadcasted_iota(jnp.int32, shape, 1)
    layer_of = layers[0] + lax.broadcasted_iota(jnp.int32, shape, 0) // ROWS
    own_place = 32 * (layer_of + 1) - base + lane % 32
    for number, block in enumerate(blocks):
        cx, cy = block // 2, block % 2
        key = jnp.concatenate([key_ref[block, layer] for layer in layers], axis=0)
        col = key >> 8
        place = (key & 255) - base
        own = []
        other = []
        for a in range(3):
            found = None
            for ox in range(3):
                for oy in range(3):
                    c = (cx + ox) * 4 + cy + oy
                    line = table_ref[a * 16 + c : a * 16 + c + 1, :]
                    picked = lane_pick(line, place, shape)
                    found = picked if found is None else jnp.where(col == c, picked, found)
                    if ox == 1 and oy == 1:
                        own.append(lane_pick(line, own_place, shape))
            other.append(found)
        usable = jnp.logical_and(own[0] < 0.5 * UNOCCUPIED, other[0] < 0.5 * UNOCCUPIED)
        shift = (
            (col >> 2) - (cx + 1),
            (col & 3) - (cy + 1),
            (place + base) // 32 - (layer_of + 1),
        )
        far = (FAR, 0.0, 0.0)
        displace = [
            jnp.where(usable, other[a] - own[a] + shift[a].astype(F32), far[a]) for a in range(3)
        ]
        square = displace[0] ** 2 + displace[1] ** 2 + displace[2] ** 2
        radius = jnp.sqrt(square + 0.25)
        inverse = 1.0 / radius
        root = jnp.maximum(1.0 - 0.25 * square, 0.0)
        kept = [radius, root] + [displace[a] * inverse for a in range(3)] + displace
        kept.append(-4.0 * inverse * (root * root))
        for slot, value in enumerate(kept):
            for k in range(high):
                geo[slot, number * high + k] = value[ROWS * k : ROWS * k + ROWS]

    same = lax.broadcasted_iota(jnp.int32, (32, 256), 1) % 32 == lax.broadcasted_iota(
        jnp.int32, (32, 256), 0
    )
    centre = CENTRE_FIRST + CENTRE_STEP * lax.broadcasted_iota(jnp.int32, (BASIS, 256), 0).astype(
        F32
    )

    def one_cell(k, work, slope):
        radius8 = geo[0, k]
        root8 = geo[1, k]
        scale8 = geo[8, k]
        dir8 = [geo[2 + a, k] for a in range(3)]
        for t in range(TILES):
            lanes = slice(256 * t, 256 * t + 256)
            away = pair_row(radius8, t) - centre
            radial = jnp.exp(-4.0 * away * away)
            steep = radial * (away * pair_row(scale8, t))
            high = radial.astype(BF16).astype(F32)
            steep_high = steep.astype(BF16).astype(F32)
            zero = jnp.zeros_like(high)
            stacked = jnp.concatenate(
                [high, radial - high, high, zero, steep_high, steep - steep_high, steep_high, zero],
                axis=0,
            ).astype(BF16)
            both = dot(wr_ref[...], stacked)
            zh = both[0:128]
            th = jnp.tanh(zh)
            up = 1.0 + th
            root = pair_row(root8, t)
            work[0:128, lanes] = (zh * up * (root * root)).astype(BF16)
            slope[:, lanes] = up * (
                (1.0 + zh * (1.0 - th)) * both[128:256] - zh * (0.5 * root)
            )
            for a in range(3):
                work[128 + 32 * a : 160 + 32 * a, lanes] = jnp.where(
                    same, pair_row(dir8[a], t), 0.0
                ).astype(BF16)
            work[224:256, lanes] = jnp.zeros((32, 256), BF16)
        yield
        gathered = dot_nt(work[0:128, :], work[128:256, :])
        mixed = dot(webf_ref[...], gathered.astype(BF16))
        mixed_t = (2.0 * mixed.T).astype(BF16)
        left = jnp.concatenate([wtf_ref[...], mixed.astype(BF16)], axis=1)
        yield
        for t in range(TILES):
            lanes = slice(256 * t, 256 * t + 256)
            ph = dot(left, work[0:256, lanes])
            th = jnp.tanh(ph)
            up = 1.0 + th
            root = pair_row(root8, t)
            readout = wo_ref[...]
            energy = jnp.sum(readout * (ph * up), axis=0, keepdims=True)
            res[4, k, 2 * t : 2 * t + 1] = energy[:, 0:128]
            res[4, k, 2 * t + 1 : 2 * t + 2] = energy[:, 128:256]
            work[256:384, lanes] = (
                (readout * (0.5 * root * root)) * (up * (1.0 + ph * (1.0 - th)))
            ).astype(BF16)
        yield
        back = dot_nt(work[256:384, :], work[128:256, :])
        back = dot(web_ref[...], back.astype(BF16))
        back_t = back.T.astype(BF16)
        left = jnp.concatenate(
            [
                jnp.concatenate([back.astype(BF16), wtop_ref[...]], axis=1),
                jnp.concatenate([jnp.zeros((96, 128), BF16), mixed_t[0:96]], axis=1),
            ],
            axis=0,
        )
        yield
        for t in range(TILES):
            lanes = slice(256 * t, 256 * t + 256)
            latent = work[0:128, lanes]
            slant = dot(left, work[128:384, lanes])
            turned = slant[128:224] + dot(back_t[0:96], latent)
            outcome = [
                jnp.sum(jnp.where(same, turned[32 * a : 32 * a + 32], 0.0), axis=0, keepdims=True)
                for a in range(3)
            ]
            outcome.append(jnp.sum(slant[0:128] * slope[:, lanes], axis=0, keepdims=True))
            for value, slot in zip(outcome, (0, 1, 2, 3)):
                res[slot, k, 2 * t : 2 * t + 1] = value[:, 0:128]
                res[slot, k, 2 * t + 1 : 2 * t + 2] = value[:, 128:256]

    runs = [one_cell(k, works[k], slopes[k]) for k in range(count)]
    done = object()
    for tick in range(6 + count):
        for k in range(count):
            if tick >= k and runs[k] is not None:
                if next(runs[k], done) is done:
                    runs[k] = None

    radius, root = geo[0], geo[1]
    direction = [geo[2 + a] for a in range(3)]
    pull = [res[a] for a in range(3)]
    readout = res[4]
    inverse = 1.0 / radius
    along = pull[0] * direction[0] + pull[1] * direction[1] + pull[2] * direction[2]
    to_square = res[3] - 0.5 * (root * readout + inverse * inverse * along)
    for a in range(3):
        geo[2 + a] = pull[a] * inverse + geo[5 + a] * (2.0 * to_square)
    res[4] = root * root * readout

    acc[...] = jnp.zeros_like(acc)
    iota96 = lax.broadcasted_iota(jnp.int32, (96, 128), 0)
    iota16 = lax.broadcasted_iota(jnp.int32, (16, 128), 0)
    lane1 = lax.broadcasted_iota(jnp.int32, (1, 128), 1)
    own_sum[...] = jnp.zeros_like(own_sum)

    def spread_rows(col_row, terms):
        highs, lows = [], []
        for term in terms:
            chosen = jnp.where(col_row == iota16, term, 0.0)
            high = chosen.astype(BF16)
            highs.append(high)
            lows.append((chosen - high.astype(F32)).astype(BF16))
        return jnp.concatenate(highs + lows, axis=0)

    for k, (block, layer) in enumerate(cells):
        key = key_ref[block, layer]
        col = key >> 8
        place = (key & 255) - 32 * layer
        term = [geo[2 + a, k] for a in range(3)]
        hots, lefts = [], []
        for r in range(USED):
            hots.append(jnp.where(iota96 == place[r : r + 1], 1.0, 0.0).astype(BF16))
            lefts.append(spread_rows(col[r : r + 1], [-term[a][r : r + 1] for a in range(3)]))
        added = dot_nt(jnp.concatenate(hots, axis=1), jnp.concatenate(lefts, axis=1))
        at = 32 * layer - base
        acc[at : at + 96, 0:96] += added
        term.append(res[4, k])
        for slot in range(4):
            line = jnp.sum(term[slot][0:USED], axis=0, keepdims=True)
            line = line + pltpu.roll(line, 32, 1)
            line = line + pltpu.roll(line, 64, 1)
            own_sum[slot, block : block + 1, :] += jnp.where(lane1 // 32 == layer, line, 0.0)

    flipped = acc[...].T
    total = flipped[0:48] + flipped[48:96]
    if outer:
        extra_ref[...] = total
        turn, inside = (96, lane48 < 96) if base == 0 else (32, lane48 >= 32)
        total = jnp.where(inside, pltpu.roll(total, turn, 1), 0.0)
    elif first:
        extra_ref[...] = tab_ref[...]
    site = own_sum[3]
    if not first:
        total = total + before_ref[...]
        site = site + site_before_ref[...]
    spread_ref[...] = total
    for a in range(3):
        for block in blocks:
            line = a * 16 + (block // 2 + 1) * 4 + block % 2 + 1
            spread_ref[line : line + 1, :] += own_sum[a, block : block + 1, :]
    site_ref[...] = site
    if last:
        listed = list_ref[...]
        sent = jnp.zeros((16, 128), F32)
        for block in range(4):
            table = jnp.broadcast_to(site[block : block + 1], (16, 128))
            picked = jnp.take_along_axis(table, listed & 127, axis=1, mode="promise_in_bounds")
            sent = jnp.where(listed >> 7 == block, picked, sent)
        extra_ref[...] = sent


def force_call(tab, key, weights, blocks, layers, halo=None, before=None, listed=None):
    first, last = before is None, listed is not None
    count = len(blocks) * len(layers)
    args = [tab, key, *weights]
    if halo is not None:
        args.append(halo)
    if not first:
        args += before
    if last:
        args.append(listed)
    return pl.pallas_call(
        functools.partial(force_kernel, blocks, layers, first, last),
        out_shape=(
            jax.ShapeDtypeStruct((48, 128), F32),
            jax.ShapeDtypeStruct((8, 128), F32),
            jax.ShapeDtypeStruct((16 if last else 48, 128), F32),
        ),
        scratch_shapes=[
            pltpu.VMEM((9, count, ROWS, 128), F32),
            pltpu.VMEM((5, count, ROWS, 128), F32),
            pltpu.VMEM((128, 128), F32),
            pltpu.VMEM((4, 8, 128), F32),
            pltpu.VMEM((48, 128), F32),
        ]
        + [pltpu.VMEM((384, 768), BF16)] * count
        + [pltpu.VMEM((128, 768), F32)] * count,
        compiler_params=pltpu.CompilerParams(vmem_limit_bytes=40 * 1024 * 1024),
        cost_estimate=pl.CostEstimate(
            flops=count * 800_000_000, bytes_accessed=300_000, transcendentals=0
        ),
        name="force",
    )(*args)


def finish_kernel(
    arrived_ref, x_ref, below_ref, above_ref, pace_ref, place_ref, drift_ref, count_ref, *outs
):
    coords_ref, speed_ref, force_ref, rows_ref = outs
    lane = lax.broadcasted_iota(jnp.int32, (1, 128), 1)
    for row in range(4):
        line = arrived_ref[4 * row : 4 * row + 1, :]
        for part in range(1, 4):
            moved = pltpu.roll(arrived_ref[4 * row + part : 4 * row + part + 1, :], 32 * part, 1)
            line = jnp.where(lane // 32 == part, moved, line)
        rows_ref[row : row + 1, :] = line
    for cx in range(2):
        for cy in range(2):
            limit = jnp.zeros((1, 128), jnp.int32)
            for cz in range(4):
                limit = jnp.where(lane // 32 == cz, count_ref[cx, cy, cz], limit)
            occupied = lane % 32 < limit
            for a in range(3):
                beside = below_ref if cy == 0 else above_ref
                force = x_ref[a, cx, cy + 1 : cy + 2, :] + beside[a, cx]
                force_ref[a, cx, cy : cy + 1, :] = force
                speed = pace_ref[a, cx + 1, cy + 1 : cy + 2, :]
                speed_ref[a, cx, cy : cy + 1, :] = speed + 0.5 * TIME_STEP * force
                coords_ref[a, cx, cy : cy + 1, :] = jnp.where(
                    occupied,
                    place_ref[a, cx + 1, cy + 1 : cy + 2, :],
                    drift_ref[a, cx, cy : cy + 1, :] + TIME_STEP * speed,
                )


def prepare_weights(w_radial, w_env, w_latent, w_out):
    top = w_latent[0:128]
    both = jnp.dot(
        w_env.astype(F32), w_latent[128:256].astype(F32), precision=lax.Precision.HIGHEST
    )
    high = w_radial.astype(BF16)
    low = (w_radial - high.astype(F32)).astype(BF16)
    half = BF16(0.5)
    wr = jnp.concatenate([high, high, low, jnp.zeros_like(low)], axis=0).T * half
    wr = jnp.concatenate([jnp.pad(wr, ((0, 0), (0, 32))), jnp.pad(wr, ((0, 0), (32, 0)))], axis=0)
    wo = jnp.broadcast_to(w_out.astype(F32)[:, None], (128, 256))
    return (wr, top.T * half, top, (0.5 * both).T.astype(BF16), both.astype(BF16), wo)


def neighbour_keys(neighbours):
    code = neighbours.reshape(4, 6, 2, 2, 4, 32)
    offset = code // 32
    slot = code % 32
    grid = lambda n, dim: jnp.arange(n, dtype=jnp.int32).reshape(
        tuple(n if d == dim else 1 for d in range(6))
    )
    col = (grid(2, 2) + offset // 9) * 4 + grid(2, 3) + offset // 3 % 3
    place = (grid(4, 4) + offset % 3) * 32 + slot
    key = (col * 256 + place).transpose(2, 3, 4, 1, 0, 5).reshape(4, 4, USED, 128)
    return jnp.pad(key, ((0, 0), (0, 0), (0, ROWS - USED), (0, 0)))


def shifted(array, axis, step):
    peers = lax.axis_size(axis)
    return lax.ppermute(array, axis, [(i, (i + step) % peers) for i in range(peers)])


def both_ways(array, axis, dim, low, high):
    from_below = shifted(lax.slice_in_dim(array, *high, axis=dim), axis, 1)
    from_above = shifted(lax.slice_in_dim(array, *low, axis=dim), axis, -1)
    return from_below, from_above


def with_halo(array, axis, dim):
    below, above = both_ways(array, axis, dim, (0, 1), (1, 2))
    return jnp.concatenate([below, array, above], axis=dim)


def share(padded, axis, dim):
    below, above = both_ways(padded, axis, dim, (0, 2), (2, 4))
    return padded + jnp.concatenate([below, above], axis=dim)


def fold(padded, axis, dim):
    below, above = both_ways(padded, axis, dim, (0, 1), (3, 4))
    return lax.slice_in_dim(padded, 1, 3, axis=dim) + jnp.concatenate([below, above], axis=dim)


def on_device(
    positions,
    velocities,
    forces_in,
    counts,
    neighbours,
    send_list,
    w_radial,
    w_env,
    w_latent,
    w_out,
):
    weights = prepare_weights(w_radial, w_env, w_latent, w_out)
    key = neighbour_keys(neighbours)
    listed = jnp.pad(send_list.reshape(16, 32), ((0, 0), (0, 96)))
    occupied = jnp.arange(32, dtype=jnp.int32).reshape(1, 1, 1, 32) < counts[:, :, :, None]
    occupied = occupied.reshape(1, 2, 2, 128)
    half, quarter = TIME_STEP, 0.5 * TIME_STEP
    speed = velocities + quarter * forces_in
    coords = positions + half * speed

    def one_step(repeat, carry):
        wide_coords, wide_speed, change = carry
        change = lax.cond(
            repeat == 0, lambda part: part, lambda part: share(share(part, "gx", 1), "gy", 2), change
        )
        wide_coords = wide_coords + half * wide_speed + change[0:3]
        wide_speed = wide_speed + change[3:6]
        flat = wide_coords.reshape(48, 128)
        below = shifted(flat[:, 96:128], "gz", 1)
        *state, again = force_call(flat, key, weights, (0, 1), (1, 2))
        above = shifted(again[:, 0:32], "gz", -1)
        *state, rim = force_call(flat, key, weights, (0, 1, 2, 3), (0,), below, state)
        from_above = shifted(rim[:, 0:32], "gz", -1)
        *state, rim = force_call(flat, key, weights, (0, 1, 2, 3), (3,), above, state)
        from_below = shifted(rim[:, 96:128], "gz", 1)
        state = force_call(flat, key, weights, (2, 3), (1, 2), before=state, listed=listed)
        edges = jnp.concatenate([from_below, jnp.zeros((48, 64), F32), from_above], axis=1)
        force = (state[0] + edges).reshape(3, 4, 4, 128)
        change = jnp.concatenate([half * half * force, half * force], axis=0)
        return (wide_coords, wide_speed, change, force, state[2])

    first = jnp.concatenate([jnp.where(occupied, coords, UNOCCUPIED), speed], axis=0)
    first = with_halo(with_halo(first, "gx", 1), "gy", 2)
    zero = jnp.zeros((3, 4, 4, 128), F32)
    carry = (zero, zero, first, zero, jnp.zeros((16, 128), F32))
    wide_coords, wide_speed, _, force, sent = lax.fori_loop(
        0, STEPS, lambda repeat, carry: one_step(repeat, carry[0:3]), carry
    )
    work_energy = lax.all_to_all(sent, "gz", split_axis=0, concat_axis=0, tiled=True)
    force = fold(force, "gx", 1)
    below, above = both_ways(force, "gy", 2, (0, 1), (3, 4))
    own = jax.ShapeDtypeStruct((3, 2, 2, 128), F32)
    specs = [pl.BlockSpec(memory_space=pltpu.VMEM)] * 7 + [pl.BlockSpec(memory_space=pltpu.SMEM)]
    *moved, rows = pl.pallas_call(
        finish_kernel,
        out_shape=(own, own, own, jax.ShapeDtypeStruct((4, 128), F32)),
        in_specs=specs,
        name="finish",
    )(work_energy, force, below, above, wide_speed, wide_coords, coords, counts)
    return (*moved, rows.reshape(1, 1, 512))


def solution(mesh):
    split = P(None, "gx", "gy", "gz")
    cells = P("gx", "gy", "gz")
    return jax.shard_map(
        on_device,
        mesh=mesh,
        in_specs=(split, split, split, cells, split, cells, P(), P(), P(), P()),
        out_specs=(split, split, split, cells),
        check_vma=False,
    )
```

profile of v0, /device:TPU:1, one launch (start us, length us, event | category | flops | bytes accessed | tf_op | source)
XLA Modules:
  0.0 95.7 jit_solution(13162214755056058638)
XLA Ops:
  1.6 1.3 %broadcast_select_fusion = (f32[3,2,2,128]{3,2,1,0:T(2,128)S(1)}, f32[3,2,2,128]{3,2,1,0:T(2,128)}, f32[3,2,2,128]{3,2,1,0:T(2,128)S(1)}) fusion(pred[2,2,128]{2,1,0:T(4,128)(4,1)S(1)} %broadcast_compare_fusion, f32[3,2,2,128]{3,2,1,0:T(2,128)} %param.14, f32[3,2,2,128]{3,2,1,0:T(2,128)} %param.15, f32[3,2,2,128]{3,2,1,0:T(2,128)} %param.16), kind=kLoop, calls=%fused_computation.55 | loop fusion | flops 7680 | bytes 37376 | tf_op jit(solution)/shard_map/jit(_where)/select_n | solution.py:439
  3.0 3.4 %collective-permute-start.9 = (f32[6,1,2,128]{3,2,1,0:T(2,128)S(1)}, f32[6,1,2,128]{3,2,1,0:T(2,128)S(1)}, u32[]{:S(2)}, u32[]{:S(2)}) collective-permute-start(f32[6,1,2,128]{3,2,1,0:T(2,128)S(1)} %get-tuple-element.395), channel_id=1, source_target_pairs={{0,192},{64,0},{128,64},{192,128},{1,193},{65,1},{129,65},{193,129... | collective-permute-start | bytes 18440 | tf_op jit(solution)/shard_map/ppermute | solution.py:373
  6.5 1.2 %fusion.6 = s32[2,2,4,6,4,32]{5,4,2,3,1,0:T(4,128)S(1)} fusion(s32[4,6,2,2,4,32]{5,4,3,2,1,0:T(4,128)S(1)} %reshape.47), kind=kLoop, calls=%fused_computation.23 | loop fusion | flops 638976 | bytes 98304 | tf_op jit(solution)/shard_map/transpose | solution.py:367
  8.1 1.9 %collective-permute-done.8 = f32[6,1,2,128]{3,2,1,0:T(2,128)S(1)} collective-permute-done((f32[6,1,2,128]{3,2,1,0:T(2,128)S(1)}, f32[6,1,2,128]{3,2,1,0:T(2,128)S(1)}, u32[]{:S(2)}, u32[]{:S(2)}) %collective-permute-start.8) | collective-permute-done | bytes 6176 | tf_op jit(solution)/shard_map/ppermute | solution.py:373
  10.1 2.8 %collective-permute-start.11 = (f32[6,4,1,128]{3,2,1,0:T(1,128)S(1)}, f32[6,4,1,128]{3,2,1,0:T(1,128)S(1)}, u32[]{:S(2)}, u32[]{:S(2)}) collective-permute-start(f32[6,4,1,128]{3,2,1,0:T(1,128)S(1)} %get-tuple-element.391), channel_id=1, source_target_pairs={{0,48},{16,0},{32,16},{48,32},{1,49},{17,1},{33,17},{49,33},{2,50}... | collective-permute-start | bytes 36872 | tf_op jit(solution)/shard_map/ppermute | solution.py:373
  16.7 60.6 %while.28 = (s32[]{:T(128)}, f32[3,4,4,128]{3,2,1,0:T(4,128)S(1)}, f32[3,4,4,128]{3,2,1,0:T(4,128)S(1)}, f32[6,4,4,128]{3,2,1,0:T(4,128)S(1)}, f32[3,4,4,128]{3,...) while((s32[]{:T(128)}, f32[3,4,4,128]{3,2,1,0:T(4,128)S(1)}, ...), condition=%wide.region_3.4_spmd.clone, body=%wide.region_0.3_spmd.clone.sunk | while | flops 12800129024 | bytes 2820512 | solution.py:443
  17.0 5.1 %collective-permute-start.5 = (f32[48,32]{1,0:T(8,128)S(1)}, f32[48,32]{1,0:T(8,128)S(1)}, u32[]{:S(2)}, u32[]{:S(2)}) collective-permute-start(f32[48,32]{1,0:T(8,128)S(1)} %slice.144), channel_id=1, source_target_pairs={{0,1},{1,2},{2,3},{3,4},{4,5},{5,6},{6,7},{7,8},{8,9},{9,10},{10,1... | collective-permute-start | bytes 18440 | tf_op jit(solution)/shard_map/while/body/eval_jaxpr/ppermute | solution.py:373
  22.2 4.1 %force.20 = (f32[48,128]{1,0:T(8,128)S(1)}, f32[8,128]{1,0:T(8,128)S(1)}, f32[48,128]{1,0:T(8,128)S(1)}) custom-call(f32[48,128]{1,0:T(8,128)S(1)} %bitcast.29, s32[4,4,8,128]{3,2,1,0:T(8,128)S(1)} %get-tuple-element.549.refs_1_, bf16[256,64]{1,0:T(8,128)(2,1)S(1)} %get-tuple-element.550.refs_2_, bf16[128,128]{1,0:T(8,128)(2,1)S(1)} %get-tuple-element.551.refs_3_, ...), custom_call_target="tpu_custom_call" | custom-call | flops 3200000000 | bytes 300000 | tf_op jit(solution)/shard_map/while/body/eval_jaxpr/force/pallas_call | solution.py:290
  26.4 4.2 %force.21 = (f32[48,128]{1,0:T(8,128)S(1)}, f32[8,128]{1,0:T(8,128)S(1)}, f32[48,128]{1,0:T(8,128)S(1)}) custom-call(f32[48,128]{1,0:T(8,128)S(1)} %bitcast.30, s32[4,4,8,128]{3,2,1,0:T(8,128)S(1)} %get-tuple-element.549.refs_1_, bf16[256,64]{1,0:T(8,128)(2,1)S(1)} %get-tuple-element.550.refs_2_, bf16[128,128]{1,0:T(8,128)(2,1)S(1)} %get-tuple-element.551.refs_3_, ...), custom_call_target="tpu_custom_call" | custom-call | flops 3200000000 | bytes 300000 | tf_op jit(solution)/shard_map/while/body/eval_jaxpr/force/pallas_call | solution.py:290
  30.5 1.4 %collective-permute-start.6 = (f32[48,32]{1,0:T(8,128)S(1)}, f32[48,32]{1,0:T(8,128)S(1)}, u32[]{:S(2)}, u32[]{:S(2)}) collective-permute-start(f32[48,32]{1,0:T(8,128)S(1)} %bitcast.26), channel_id=1, source_target_pairs={{0,15},{1,0},{2,1},{3,2},{4,3},{5,4},{6,5},{7,6},{8,7},{9,8},{10,9... | collective-permute-start | bytes 18440 | tf_op jit(solution)/shard_map/while/body/eval_jaxpr/ppermute | solution.py:373
  32.0 4.2 %force.22 = (f32[48,128]{1,0:T(8,128)S(1)}, f32[8,128]{1,0:T(8,128)S(1)}, f32[48,128]{1,0:T(8,128)S(1)}) custom-call(f32[48,128]{1,0:T(8,128)S(1)} %bitcast.31, s32[4,4,8,128]{3,2,1,0:T(8,128)S(1)} %get-tuple-element.549.refs_1_, bf16[256,64]{1,0:T(8,128)(2,1)S(1)} %get-tuple-element.550.refs_2_, bf16[128,128]{1,0:T(8,128)(2,1)S(1)} %get-tuple-element.551.refs_3_, ...), custom_call_target="tpu_custom_call" | custom-call | flops 3200000000 | bytes 300000 | tf_op jit(solution)/shard_map/while/body/eval_jaxpr/force/pallas_call | solution.py:290
  36.6 4.6 %force.23 = (f32[48,128]{1,0:T(8,128)S(1)}, f32[8,128]{1,0:T(8,128)}, f32[16,128]{1,0:T(8,128)}) custom-call(f32[48,128]{1,0:T(8,128)S(1)} %bitcast.32, s32[4,4,8,128]{3,2,1,0:T(8,128)S(1)} %get-tuple-element.549.refs_1_, bf16[256,64]{1,0:T(8,128)(2,1)S(1)} %get-tuple-element.550.refs_2_, bf16[128,128]{1,0:T(8,128)(2,1)S(1)} %get-tuple-element.551.refs_3_, ...), custom_call_target="tpu_custom_call" | custom-call | flops 3200000000 | bytes 300000 | tf_op jit(solution)/shard_map/while/body/eval_jaxpr/force/pallas_call | solution.py:290
  41.9 9.5 %conditional.3 = (f32[6,4,4,128]{3,2,1,0:T(4,128)S(1)}) conditional(s32[]{:T(128)} %convert_element_type.50, f32[6,4,4,128]{3,2,1,0:T(4,128)S(1)} %get-tuple-element.528, f32[6,4,4,128]{3,2,1,0:T(4,128)S(1)} %get-tuple-element.528), branch_computations={%region_1.1_spmd, %region_2.2_spmd} | conditional | flops 49152 | bytes 884904 | solution.py:420
  42.0 1.5 %collective-permute-start = (f32[6,2,4,128]{3,2,1,0:T(4,128)S(1)}, f32[6,2,4,128]{3,2,1,0:T(4,128)S(1)}, u32[]{:S(2)}, u32[]{:S(2)}) collective-permute-start(f32[6,2,4,128]{3,2,1,0:T(4,128)S(1)} %get-tuple-element.378), channel_id=1, source_target_pairs={{0,64},{64,128},{128,192},{192,0},{1,65},{65,129},{129,193},{193,1... | collective-permute-start | bytes 73736 | tf_op jit(solution)/shard_map/while/body/eval_jaxpr/cond/branch_0_fun/ppermute | solution.py:373
  43.4 1.2 %collective-permute-done.1 = f32[6,2,4,128]{3,2,1,0:T(4,128)S(1)} collective-permute-done((f32[6,2,4,128]{3,2,1,0:T(4,128)S(1)}, f32[6,2,4,128]{3,2,1,0:T(4,128)S(1)}, u32[]{:S(2)}, u32[]{:S(2)}) %collective-permute-start.1) | collective-permute-done | bytes 24608 | tf_op jit(solution)/shard_map/while/body/eval_jaxpr/cond/branch_0_fun/ppermute | solution.py:373
  44.7 1.3 %collective-permute-done = f32[6,2,4,128]{3,2,1,0:T(4,128)S(1)} collective-permute-done((f32[6,2,4,128]{3,2,1,0:T(4,128)S(1)}, f32[6,2,4,128]{3,2,1,0:T(4,128)S(1)}, u32[]{:S(2)}, u32[]{:S(2)}) %collective-permute-start) | collective-permute-done | bytes 24608 | tf_op jit(solution)/shard_map/while/body/eval_jaxpr/cond/branch_0_fun/ppermute | solution.py:373
  46.0 1.4 %collective-permute-start.3 = (f32[6,4,2,128]{3,2,1,0:T(2,128)S(1)}, f32[6,4,2,128]{3,2,1,0:T(2,128)S(1)}, u32[]{:S(2)}, u32[]{:S(2)}) collective-permute-start(f32[6,4,2,128]{3,2,1,0:T(2,128)S(1)} %get-tuple-element.377), channel_id=1, source_target_pairs={{0,48},{16,0},{32,16},{48,32},{1,49},{17,1},{33,17},{49,33},{2,50}... | collective-permute-start | bytes 73736 | tf_op jit(solution)/shard_map/while/body/eval_jaxpr/cond/branch_0_fun/ppermute | solution.py:373
  47.6 1.5 %collective-permute-done.3 = f32[6,4,2,128]{3,2,1,0:T(2,128)S(1)} collective-permute-done((f32[6,4,2,128]{3,2,1,0:T(2,128)S(1)}, f32[6,4,2,128]{3,2,1,0:T(2,128)S(1)}, u32[]{:S(2)}, u32[]{:S(2)}) %collective-permute-start.3) | collective-permute-done | bytes 24608 | tf_op jit(solution)/shard_map/while/body/eval_jaxpr/cond/branch_0_fun/ppermute | solution.py:373
  49.1 2.2 %collective-permute-done.2 = f32[6,4,2,128]{3,2,1,0:T(2,128)S(1)} collective-permute-done((f32[6,4,2,128]{3,2,1,0:T(2,128)S(1)}, f32[6,4,2,128]{3,2,1,0:T(2,128)S(1)}, u32[]{:S(2)}, u32[]{:S(2)}) %collective-permute-start.2) | collective-permute-done | bytes 24608 | tf_op jit(solution)/shard_map/while/body/eval_jaxpr/cond/branch_0_fun/ppermute | solution.py:373
  51.5 2.5 %collective-permute-start.5 = (f32[48,32]{1,0:T(8,128)S(1)}, f32[48,32]{1,0:T(8,128)S(1)}, u32[]{:S(2)}, u32[]{:S(2)}) collective-permute-start(f32[48,32]{1,0:T(8,128)S(1)} %slice.144), channel_id=1, source_target_pairs={{0,1},{1,2},{2,3},{3,4},{4,5},{5,6},{6,7},{7,8},{8,9},{9,10},{10,1... | collective-permute-start | bytes 18440 | tf_op jit(solution)/shard_map/while/body/eval_jaxpr/ppermute | solution.py:373
  54.0 4.1 %force.20 = (f32[48,128]{1,0:T(8,128)S(1)}, f32[8,128]{1,0:T(8,128)S(1)}, f32[48,128]{1,0:T(8,128)S(1)}) custom-call(f32[48,128]{1,0:T(8,128)S(1)} %bitcast.29, s32[4,4,8,128]{3,2,1,0:T(8,128)S(1)} %get-tuple-element.549.refs_1_, bf16[256,64]{1,0:T(8,128)(2,1)S(1)} %get-tuple-element.550.refs_2_, bf16[128,128]{1,0:T(8,128)(2,1)S(1)} %get-tuple-element.551.refs_3_, ...), custom_call_target="tpu_custom_call" | custom-call | flops 3200000000 | bytes 300000 | tf_op jit(solution)/shard_map/while/body/eval_jaxpr/force/pallas_call | solution.py:290
  58.1 2.2 %collective-permute-start.4 = (f32[48,32]{1,0:T(8,128)S(1)}, f32[48,32]{1,0:T(8,128)S(1)}, u32[]{:S(2)}, u32[]{:S(2)}) collective-permute-start(f32[48,32]{1,0:T(8,128)S(1)} %bitcast.27), channel_id=1, source_target_pairs={{0,15},{1,0},{2,1},{3,2},{4,3},{5,4},{6,5},{7,6},{8,7},{9,8},{10,9... | collective-permute-start | bytes 18440 | tf_op jit(solution)/shard_map/while/body/eval_jaxpr/ppermute | solution.py:373
  60.4 4.2 %force.21 = (f32[48,128]{1,0:T(8,128)S(1)}, f32[8,128]{1,0:T(8,128)S(1)}, f32[48,128]{1,0:T(8,128)S(1)}) custom-call(f32[48,128]{1,0:T(8,128)S(1)} %bitcast.30, s32[4,4,8,128]{3,2,1,0:T(8,128)S(1)} %get-tuple-element.549.refs_1_, bf16[256,64]{1,0:T(8,128)(2,1)S(1)} %get-tuple-element.550.refs_2_, bf16[128,128]{1,0:T(8,128)(2,1)S(1)} %get-tuple-element.551.refs_3_, ...), custom_call_target="tpu_custom_call" | custom-call | flops 3200000000 | bytes 300000 | tf_op jit(solution)/shard_map/while/body/eval_jaxpr/force/pallas_call | solution.py:290
  64.6 3.0 %collective-permute-start.6 = (f32[48,32]{1,0:T(8,128)S(1)}, f32[48,32]{1,0:T(8,128)S(1)}, u32[]{:S(2)}, u32[]{:S(2)}) collective-permute-start(f32[48,32]{1,0:T(8,128)S(1)} %bitcast.26), channel_id=1, source_target_pairs={{0,15},{1,0},{2,1},{3,2},{4,3},{5,4},{6,5},{7,6},{8,7},{9,8},{10,9... | collective-permute-start | bytes 18440 | tf_op jit(solution)/shard_map/while/body/eval_jaxpr/ppermute | solution.py:373
  67.6 4.2 %force.22 = (f32[48,128]{1,0:T(8,128)S(1)}, f32[8,128]{1,0:T(8,128)S(1)}, f32[48,128]{1,0:T(8,128)S(1)}) custom-call(f32[48,128]{1,0:T(8,128)S(1)} %bitcast.31, s32[4,4,8,128]{3,2,1,0:T(8,128)S(1)} %get-tuple-element.549.refs_1_, bf16[256,64]{1,0:T(8,128)(2,1)S(1)} %get-tuple-element.550.refs_2_, bf16[128,128]{1,0:T(8,128)(2,1)S(1)} %get-tuple-element.551.refs_3_, ...), custom_call_target="tpu_custom_call" | custom-call | flops 3200000000 | bytes 300000 | tf_op jit(solution)/shard_map/while/body/eval_jaxpr/force/pallas_call | solution.py:290
  71.8 4.6 %force.23 = (f32[48,128]{1,0:T(8,128)S(1)}, f32[8,128]{1,0:T(8,128)}, f32[16,128]{1,0:T(8,128)}) custom-call(f32[48,128]{1,0:T(8,128)S(1)} %bitcast.32, s32[4,4,8,128]{3,2,1,0:T(8,128)S(1)} %get-tuple-element.549.refs_1_, bf16[256,64]{1,0:T(8,128)(2,1)S(1)} %get-tuple-element.550.refs_2_, bf16[128,128]{1,0:T(8,128)(2,1)S(1)} %get-tuple-element.551.refs_3_, ...), custom_call_target="tpu_custom_call" | custom-call | flops 3200000000 | bytes 300000 | tf_op jit(solution)/shard_map/while/body/eval_jaxpr/force/pallas_call | solution.py:290
  78.1 1.5 %collective-permute-start.12 = (f32[3,1,4,128]{3,2,1,0:T(4,128)S(1)}, f32[3,1,4,128]{3,2,1,0:T(4,128)S(1)}, u32[]{:S(2)}, u32[]{:S(2)}) collective-permute-start(f32[3,1,4,128]{3,2,1,0:T(4,128)S(1)} %get-tuple-element.388), channel_id=1, source_target_pairs={{0,64},{64,128},{128,192},{192,0},{1,65},{65,129},{129,193},{193,1... | collective-permute-start | bytes 18440 | tf_op jit(solution)/shard_map/ppermute | solution.py:373
  79.6 7.0 %all-to-all-start = ((f32[16,1,128]{2,1,0:T(1,128)}), f32[16,1,128]{2,1,0:T(1,128)S(1)}, u32[]{:S(2)}, u32[]{:S(2)}) async-start(f32[16,1,128]{2,1,0:T(1,128)} %bitcast.4), calls=%async_computation | async-start | bytes 16384 | tf_op jit(solution)/shard_map/all_to_all | solution.py:446
  86.8 2.7 %collective-permute-start.15 = (f32[3,2,1,128]{3,2,1,0:T(1,128)S(1)}, f32[3,2,1,128]{3,2,1,0:T(1,128)S(1)}, u32[]{:S(2)}, u32[]{:S(2)}) collective-permute-start(f32[3,2,1,128]{3,2,1,0:T(1,128)S(1)} %get-tuple-element.392), channel_id=1, source_target_pairs={{0,48},{16,0},{32,16},{48,32},{1,49},{17,1},{33,17},{49,33},{2,50}... | collective-permute-start | bytes 9224 | tf_op jit(solution)/shard_map/ppermute | solution.py:373
  89.5 1.2 %collective-permute-done.14.below_ref = f32[3,2,1,128]{3,2,1,0:T(1,128)S(1)} collective-permute-done((f32[3,2,1,128]{3,2,1,0:T(1,128)S(1)}, f32[3,2,1,128]{3,2,1,0:T(1,128)S(1)}, u32[]{:S(2)}, u32[]{:S(2)}) %collective-permute-start.14) | collective-permute-done | bytes 3104 | tf_op jit(solution)/shard_map/ppermute | solution.py:373
  90.7 3.0 %all-to-all-done = f32[16,1,128]{2,1,0:T(1,128)S(1)} async-done(((f32[16,1,128]{2,1,0:T(1,128)}), f32[16,1,128]{2,1,0:T(1,128)S(1)}, u32[]{:S(2)}, u32[]{:S(2)}) %all-to-all-start) | async-done | bytes 8224 | tf_op jit(solution)/shard_map/all_to_all | solution.py:446
  94.2 1.5 %finish.1 = (f32[3,2,2,128]{3,2,1,0:T(2,128)}, f32[3,2,2,128]{3,2,1,0:T(2,128)}, f32[3,2,2,128]{3,2,1,0:T(2,128)}, f32[4,128]{1,0:T(4,128)}) custom-call(f32[16,128]{1,0:T(8,128)} %bitcast.35, f32[3,2,4,128]{3,2,1,0:T(4,128)} %copy-done.3, f32[3,2,1,128]{3,2,1,0:T(1,128)} %copy-done.8, f32[3,2,1,128]{3,2,1,0:T(1,128)} %copy-done.9, ...), custom_call_target="tpu_custom_call" | custom-call | tf_op jit(solution)/shard_map/finish/pallas_call | solution.py:451
  (107 shorter events, 9.4 us)
Async XLA Ops:
  0.6 7.2 %copy-start = (bf16[128,128]{1,0:T(8,128)(2,1)S(1)}, bf16[128,128]{1,0:T(8,128)(2,1)}, u32[]{:S(2)}) copy-start(bf16[128,128]{1,0:T(8,128)(2,1)} %param.21) | copy-start | bytes 98308
  0.6 5.7 %copy-start.5 = (s32[24,2,2,128]{3,2,1,0:T(2,128)S(1)}, s32[24,2,2,128]{3,2,1,0:T(2,128)}, u32[]{:S(2)}) copy-start(s32[24,2,2,128]{3,2,1,0:T(2,128)} %param.18) | copy-start | bytes 147460
  3.0 5.2 %collective-permute-start.9 = (f32[6,1,2,128]{3,2,1,0:T(2,128)S(1)}, f32[6,1,2,128]{3,2,1,0:T(2,128)S(1)}, u32[]{:S(2)}, u32[]{:S(2)}) collective-permute-start(f32[6,1,2,128]{3,2,1,0:T(2,128)S(1)} %get-tuple-element.395), channel_id=1, source_target_pairs={{0,192},{64,0},{128,64},{192,128},{1,193},{65,1},{129,65},{193,129... | collective-permute-start | bytes 18440 | tf_op jit(solution)/shard_map/ppermute | solution.py:373
  6.3 3.7 %collective-permute-start.8 = (f32[6,1,2,128]{3,2,1,0:T(2,128)S(1)}, f32[6,1,2,128]{3,2,1,0:T(2,128)S(1)}, u32[]{:S(2)}, u32[]{:S(2)}) collective-permute-start(f32[6,1,2,128]{3,2,1,0:T(2,128)S(1)} %get-tuple-element.394), channel_id=1, source_target_pairs={{0,64},{64,128},{128,192},{192,0},{1,65},{65,129},{129,193},{193,1... | collective-permute-start | bytes 18440 | tf_op jit(solution)/shard_map/ppermute | solution.py:373
  6.5 1.3 %copy-start.7 = (f32[8,128]{1,0:T(8,128)S(1)}, f32[8,128]{1,0:T(8,128)}, u32[]{:S(2)}) copy-start(f32[8,128]{1,0:T(8,128)} %param.20) | copy-start | bytes 12292
  6.5 1.3 %copy-start.4 = (bf16[256,128]{1,0:T(8,128)(2,1)S(1)}, bf16[256,128]{1,0:T(8,128)(2,1)}, u32[]{:S(2)}) copy-start(bf16[256,128]{1,0:T(8,128)(2,1)} %param.22) | copy-start | bytes 196612
  10.1 5.4 %collective-permute-start.11 = (f32[6,4,1,128]{3,2,1,0:T(1,128)S(1)}, f32[6,4,1,128]{3,2,1,0:T(1,128)S(1)}, u32[]{:S(2)}, u32[]{:S(2)}) collective-permute-start(f32[6,4,1,128]{3,2,1,0:T(1,128)S(1)} %get-tuple-element.391), channel_id=1, source_target_pairs={{0,48},{16,0},{32,16},{48,32},{1,49},{17,1},{33,17},{49,33},{2,50}... | collective-permute-start | bytes 36872 | tf_op jit(solution)/shard_map/ppermute | solution.py:373
  12.9 3.8 %collective-permute-start.10 = (f32[6,4,1,128]{3,2,1,0:T(1,128)S(1)}, f32[6,4,1,128]{3,2,1,0:T(1,128)S(1)}, u32[]{:S(2)}, u32[]{:S(2)}) collective-permute-start(f32[6,4,1,128]{3,2,1,0:T(1,128)S(1)} %get-tuple-element.390), channel_id=1, source_target_pairs={{0,16},{16,32},{32,48},{48,0},{1,17},{17,33},{33,49},{49,1},{2,18}... | collective-permute-start | bytes 36872 | tf_op jit(solution)/shard_map/ppermute | solution.py:373
  13.4 0.7 copy-start.10
  14.8 0.7 copy-start.11
  17.0 9.3 %collective-permute-start.5 = (f32[48,32]{1,0:T(8,128)S(1)}, f32[48,32]{1,0:T(8,128)S(1)}, u32[]{:S(2)}, u32[]{:S(2)}) collective-permute-start(f32[48,32]{1,0:T(8,128)S(1)} %slice.144), channel_id=1, source_target_pairs={{0,1},{1,2},{2,3},{3,4},{4,5},{5,6},{6,7},{7,8},{8,9},{9,10},{10,1... | collective-permute-start | bytes 18440 | tf_op jit(solution)/shard_map/while/body/eval_jaxpr/ppermute | solution.py:373
  26.2 5.7 %collective-permute-start.4 = (f32[48,32]{1,0:T(8,128)S(1)}, f32[48,32]{1,0:T(8,128)S(1)}, u32[]{:S(2)}, u32[]{:S(2)}) collective-permute-start(f32[48,32]{1,0:T(8,128)S(1)} %bitcast.27), channel_id=1, source_target_pairs={{0,15},{1,0},{2,1},{3,2},{4,3},{5,4},{6,5},{7,6},{8,7},{9,8},{10,9... | collective-permute-start | bytes 18440 | tf_op jit(solution)/shard_map/while/body/eval_jaxpr/ppermute | solution.py:373
  30.5 10.6 %collective-permute-start.6 = (f32[48,32]{1,0:T(8,128)S(1)}, f32[48,32]{1,0:T(8,128)S(1)}, u32[]{:S(2)}, u32[]{:S(2)}) collective-permute-start(f32[48,32]{1,0:T(8,128)S(1)} %bitcast.26), channel_id=1, source_target_pairs={{0,15},{1,0},{2,1},{3,2},{4,3},{5,4},{6,5},{7,6},{8,7},{9,8},{10,9... | collective-permute-start | bytes 18440 | tf_op jit(solution)/shard_map/while/body/eval_jaxpr/ppermute | solution.py:373
  36.2 4.9 %collective-permute-start.7 = (f32[48,32]{1,0:T(8,128)S(1)}, f32[48,32]{1,0:T(8,128)S(1)}, u32[]{:S(2)}, u32[]{:S(2)}) collective-permute-start(f32[48,32]{1,0:T(8,128)S(1)} %slice.145), channel_id=1, source_target_pairs={{0,1},{1,2},{2,3},{3,4},{4,5},{5,6},{6,7},{7,8},{8,9},{9,10},{10,1... | collective-permute-start | bytes 18440 | tf_op jit(solution)/shard_map/while/body/eval_jaxpr/ppermute | solution.py:373
  41.2 0.6 copy-start.1
  41.9 2.8 %collective-permute-start.1 = (f32[6,2,4,128]{3,2,1,0:T(4,128)S(1)}, f32[6,2,4,128]{3,2,1,0:T(4,128)S(1)}, u32[]{:S(2)}, u32[]{:S(2)}) collective-permute-start(f32[6,2,4,128]{3,2,1,0:T(4,128)S(1)} %get-tuple-element.379), channel_id=1, source_target_pairs={{0,192},{64,0},{128,64},{192,128},{1,193},{65,1},{129,65},{193,129... | collective-permute-start | bytes 73736 | tf_op jit(solution)/shard_map/while/body/eval_jaxpr/cond/branch_0_fun/ppermute | solution.py:373
  42.0 4.0 %collective-permute-start = (f32[6,2,4,128]{3,2,1,0:T(4,128)S(1)}, f32[6,2,4,128]{3,2,1,0:T(4,128)S(1)}, u32[]{:S(2)}, u32[]{:S(2)}) collective-permute-start(f32[6,2,4,128]{3,2,1,0:T(4,128)S(1)} %get-tuple-element.378), channel_id=1, source_target_pairs={{0,64},{64,128},{128,192},{192,0},{1,65},{65,129},{129,193},{193,1... | collective-permute-start | bytes 73736 | tf_op jit(solution)/shard_map/while/body/eval_jaxpr/cond/branch_0_fun/ppermute | solution.py:373
  46.0 3.0 %collective-permute-start.3 = (f32[6,4,2,128]{3,2,1,0:T(2,128)S(1)}, f32[6,4,2,128]{3,2,1,0:T(2,128)S(1)}, u32[]{:S(2)}, u32[]{:S(2)}) collective-permute-start(f32[6,4,2,128]{3,2,1,0:T(2,128)S(1)} %get-tuple-element.377), channel_id=1, source_target_pairs={{0,48},{16,0},{32,16},{48,32},{1,49},{17,1},{33,17},{49,33},{2,50}... | collective-permute-start | bytes 73736 | tf_op jit(solution)/shard_map/while/body/eval_jaxpr/cond/branch_0_fun/ppermute | solution.py:373
  47.4 3.9 %collective-permute-start.2 = (f32[6,4,2,128]{3,2,1,0:T(2,128)S(1)}, f32[6,4,2,128]{3,2,1,0:T(2,128)S(1)}, u32[]{:S(2)}, u32[]{:S(2)}) collective-permute-start(f32[6,4,2,128]{3,2,1,0:T(2,128)S(1)} %get-tuple-element.376), channel_id=1, source_target_pairs={{0,16},{16,32},{32,48},{48,0},{1,17},{17,33},{33,49},{49,1},{2,18}... | collective-permute-start | bytes 73736 | tf_op jit(solution)/shard_map/while/body/eval_jaxpr/cond/branch_0_fun/ppermute | solution.py:373
  51.5 8.9 %collective-permute-start.5 = (f32[48,32]{1,0:T(8,128)S(1)}, f32[48,32]{1,0:T(8,128)S(1)}, u32[]{:S(2)}, u32[]{:S(2)}) collective-permute-start(f32[48,32]{1,0:T(8,128)S(1)} %slice.144), channel_id=1, source_target_pairs={{0,1},{1,2},{2,3},{3,4},{4,5},{5,6},{6,7},{7,8},{8,9},{9,10},{10,1... | collective-permute-start | bytes 18440 | tf_op jit(solution)/shard_map/while/body/eval_jaxpr/ppermute | solution.py:373
  58.1 9.5 %collective-permute-start.4 = (f32[48,32]{1,0:T(8,128)S(1)}, f32[48,32]{1,0:T(8,128)S(1)}, u32[]{:S(2)}, u32[]{:S(2)}) collective-permute-start(f32[48,32]{1,0:T(8,128)S(1)} %bitcast.27), channel_id=1, source_target_pairs={{0,15},{1,0},{2,1},{3,2},{4,3},{5,4},{6,5},{7,6},{8,7},{9,8},{10,9... | collective-permute-start | bytes 18440 | tf_op jit(solution)/shard_map/while/body/eval_jaxpr/ppermute | solution.py:373
  64.6 11.8 %collective-permute-start.6 = (f32[48,32]{1,0:T(8,128)S(1)}, f32[48,32]{1,0:T(8,128)S(1)}, u32[]{:S(2)}, u32[]{:S(2)}) collective-permute-start(f32[48,32]{1,0:T(8,128)S(1)} %bitcast.26), channel_id=1, source_target_pairs={{0,15},{1,0},{2,1},{3,2},{4,3},{5,4},{6,5},{7,6},{8,7},{9,8},{10,9... | collective-permute-start | bytes 18440 | tf_op jit(solution)/shard_map/while/body/eval_jaxpr/ppermute | solution.py:373
  71.8 4.6 %collective-permute-start.7 = (f32[48,32]{1,0:T(8,128)S(1)}, f32[48,32]{1,0:T(8,128)S(1)}, u32[]{:S(2)}, u32[]{:S(2)}) collective-permute-start(f32[48,32]{1,0:T(8,128)S(1)} %slice.145), channel_id=1, source_target_pairs={{0,1},{1,2},{2,3},{3,4},{4,5},{5,6},{6,7},{7,8},{8,9},{9,10},{10,1... | collective-permute-start | bytes 18440 | tf_op jit(solution)/shard_map/while/body/eval_jaxpr/ppermute | solution.py:373
  77.3 9.3 %copy-start.2 = (f32[3,4,4,128]{3,2,1,0:T(4,128)S(1)}, f32[3,4,4,128]{3,2,1,0:T(4,128)}, u32[]{:S(2)}) copy-start(f32[3,4,4,128]{3,2,1,0:T(4,128)} %get-tuple-element.237) | copy-start | bytes 73732
  78.1 8.5 %collective-permute-start.13 = (f32[3,1,4,128]{3,2,1,0:T(4,128)S(1)}, f32[3,1,4,128]{3,2,1,0:T(4,128)S(1)}, u32[]{:S(2)}, u32[]{:S(2)}) collective-permute-start(f32[3,1,4,128]{3,2,1,0:T(4,128)S(1)} %get-tuple-element.389), channel_id=1, source_target_pairs={{0,192},{64,0},{128,64},{192,128},{1,193},{65,1},{129,65},{193,129... | collective-permute-start | bytes 18440 | tf_op jit(solution)/shard_map/ppermute | solution.py:373
  78.1 8.5 %collective-permute-start.12 = (f32[3,1,4,128]{3,2,1,0:T(4,128)S(1)}, f32[3,1,4,128]{3,2,1,0:T(4,128)S(1)}, u32[]{:S(2)}, u32[]{:S(2)}) collective-permute-start(f32[3,1,4,128]{3,2,1,0:T(4,128)S(1)} %get-tuple-element.388), channel_id=1, source_target_pairs={{0,64},{64,128},{128,192},{192,0},{1,65},{65,129},{129,193},{193,1... | collective-permute-start | bytes 18440 | tf_op jit(solution)/shard_map/ppermute | solution.py:373
  79.6 14.1 %all-to-all-start = ((f32[16,1,128]{2,1,0:T(1,128)}), f32[16,1,128]{2,1,0:T(1,128)S(1)}, u32[]{:S(2)}, u32[]{:S(2)}) async-start(f32[16,1,128]{2,1,0:T(1,128)} %bitcast.4), calls=%async_computation | async-start | bytes 16384 | tf_op jit(solution)/shard_map/all_to_all | solution.py:446
  86.7 7.0 %copy-start.3 = (f32[3,2,4,128]{3,2,1,0:T(4,128)}, f32[3,2,4,128]{3,2,1,0:T(4,128)S(1)}, u32[]{:S(2)}) copy-start(f32[3,2,4,128]{3,2,1,0:T(4,128)S(1)} %maximum_add_fusion.3.x_ref) | copy-start | bytes 36868
  86.7 4.0 %collective-permute-start.14 = (f32[3,2,1,128]{3,2,1,0:T(1,128)S(1)}, f32[3,2,1,128]{3,2,1,0:T(1,128)S(1)}, u32[]{:S(2)}, u32[]{:S(2)}) collective-permute-start(f32[3,2,1,128]{3,2,1,0:T(1,128)S(1)} %get-tuple-element.393), channel_id=1, source_target_pairs={{0,16},{16,32},{32,48},{48,0},{1,17},{17,33},{33,49},{49,1},{2,18}... | collective-permute-start | bytes 9224 | tf_op jit(solution)/shard_map/ppermute | solution.py:373
  86.8 3.9 %collective-permute-start.15 = (f32[3,2,1,128]{3,2,1,0:T(1,128)S(1)}, f32[3,2,1,128]{3,2,1,0:T(1,128)S(1)}, u32[]{:S(2)}, u32[]{:S(2)}) collective-permute-start(f32[3,2,1,128]{3,2,1,0:T(1,128)S(1)} %get-tuple-element.392), channel_id=1, source_target_pairs={{0,48},{16,0},{32,16},{48,32},{1,49},{17,1},{33,17},{49,33},{2,50}... | collective-permute-start | bytes 9224 | tf_op jit(solution)/shard_map/ppermute | solution.py:373
  90.7 3.0 %copy-start.8 = (f32[3,2,1,128]{3,2,1,0:T(1,128)}, f32[3,2,1,128]{3,2,1,0:T(1,128)S(1)}, u32[]{:S(2)}) copy-start(f32[3,2,1,128]{3,2,1,0:T(1,128)S(1)} %collective-permute-done.14.below_ref) | copy-start | bytes 9220
  90.7 3.0 %copy-start.9 = (f32[3,2,1,128]{3,2,1,0:T(1,128)}, f32[3,2,1,128]{3,2,1,0:T(1,128)S(1)}, u32[]{:S(2)}) copy-start(f32[3,2,1,128]{3,2,1,0:T(1,128)S(1)} %collective-permute-done.15.above_ref) | copy-start | bytes 9220
  (2 other events, 1.2 us)
where the time goes:
time: 96.1 us; the launch traced here: 95.7 us
  Pallas kernels  35.5 us (37%)
  starting transfers between devices  35 us (36%)
  waiting for transfers between devices  13.5 us (14%)
  local copies, waits for them, and re-layouts  6.22 us (6%)
  other arithmetic  3.74 us (4%)
    pallas_call x8, Pallas kernels, force_call(): pl.pallas_call(functools.partial(force_kernel, blocks, layers, first, las...  34 us
    ppermute x20, starting transfers between devices, shifted(): lax.ppermute(array, axis, [(i, (i + step) % peers) for i in range(peers)])  28 us
    ppermute x20, waiting for transfers between devices, shifted(): lax.ppermute(array, axis, [(i, (i + step) % peers) for i in range(peers)])  10.6 us
    all_to_all x1, starting transfers between devices, on_device(): lax.all_to_all(sent, 'gz', split_axis=0, concat_axis=0, tiled=True)  7.04 us
    all_to_all x1, waiting for transfers between devices, on_device(): lax.all_to_all(sent, 'gz', split_axis=0, concat_axis=0, tiled=True)  2.98 us
    unnamed x27, local copies, waits for them, and re-layouts  2.19 us
  transfers between devices with their start and end apart: 21, of which 8 were waited for; matrix products, arithmetic and copies ran while one was open for 4% of the time, Pallas kernels for 36%

commit v1 on v0

--- a/solution.py
+++ b/solution.py
@@ -42,42 +42,43 @@
 
 def force_kernel(blocks, layers, first, last, *refs):
     refs = list(refs)
-    outer = len(layers) == 1
-    base = layers[0] // 3 * 64 if outer else 32
+    outer = layers == (0, 3)
     tab_ref, key_ref = refs[:2]
     wr_ref, wtf_ref, wtop_ref, webf_ref, web_ref, wo_ref = refs[2:8]
     refs = refs[8:]
     if outer:
-        halo_ref = refs.pop(0)
+        below_ref, above_ref = refs.pop(0), refs.pop(0)
     if not first:
         before_ref, site_before_ref = refs[:2]
         refs = refs[2:]
     if last:
         list_ref = refs.pop(0)
-    spread_ref, site_ref, extra_ref = refs[:3]
-    geo, res, acc, own_sum, table_ref = refs[3:8]
+    spread_ref, site_ref = refs[:2]
+    refs = refs[2:]
+    if outer:
+        extra_ref = refs.pop(0)
+    geo, res, acc, own_sum, table_ref = refs[:5]
     cells = [(block, layer) for block in blocks for layer in layers]
     count = len(cells)
-    works, slopes = refs[8 : 8 + count], refs[8 + count :]
+    works, slopes = refs[5 : 5 + count], refs[5 + count :]
+    lane48 = lax.broadcasted_iota(jnp.int32, (48, 128), 1)
     if outer:
-        lane48 = lax.broadcasted_iota(jnp.int32, (48, 128), 1)
-        halo = jnp.concatenate([halo_ref[...], jnp.zeros((48, 96), F32)], axis=1)
-        if base == 0:
-            table_ref[...] = jnp.where(lane48 < 32, halo, pltpu.roll(tab_ref[...], 32, 1))
-        else:
-            table_ref[...] = jnp.where(
-                lane48 < 96, pltpu.roll(tab_ref[...], 96, 1), pltpu.roll(halo, 96, 1)
-            )
+        wide = jnp.zeros((48, 96), F32)
+        below = jnp.concatenate([below_ref[...], wide], axis=1)
+        above = pltpu.roll(jnp.concatenate([above_ref[...], wide], axis=1), 96, 1)
+        table_ref[0] = jnp.where(lane48 < 32, below, pltpu.roll(tab_ref[...], 32, 1))
+        table_ref[1] = jnp.where(lane48 < 96, pltpu.roll(tab_ref[...], 96, 1), above)
     else:
-        table_ref = tab_ref
-    high = len(layers)
-    shape = (high * ROWS, 128)
+        table_ref[0] = tab_ref[...]
+    bases = {0: 0, 1: 32, 2: 32, 3: 64}
+    side = {0: 0, 1: 0, 2: 0, 3: 1}
+    shape = (ROWS, 128)
     lane = lax.broadcasted_iota(jnp.int32, shape, 1)
-    layer_of = layers[0] + lax.broadcasted_iota(jnp.int32, shape, 0) // ROWS
-    own_place = 32 * (layer_of + 1) - base + lane % 32
-    for number, block in enumerate(blocks):
+    for k, (block, layer) in enumerate(cells):
         cx, cy = block // 2, block % 2
-        key = jnp.concatenate([key_ref[block, layer] for layer in layers], axis=0)
+        base = bases[layer]
+        own_place = 32 * (layer + 1) - base + lane % 32
+        key = key_ref[block, layer]
         col = key >> 8
         place = (key & 255) - base
         own = []
@@ -87,7 +88,7 @@
             for ox in range(3):
                 for oy in range(3):
                     c = (cx + ox) * 4 + cy + oy
-                    line = table_ref[a * 16 + c : a * 16 + c + 1, :]
+                    line = table_ref[side[layer], a * 16 + c : a * 16 + c + 1, :]
                     picked = lane_pick(line, place, shape)
                     found = picked if found is None else jnp.where(col == c, picked, found)
                     if ox == 1 and oy == 1:
@@ -97,7 +98,7 @@
         shift = (
             (col >> 2) - (cx + 1),
             (col & 3) - (cy + 1),
-            (place + base) // 32 - (layer_of + 1),
+            (place + base) // 32 - (layer + 1),
         )
         far = (FAR, 0.0, 0.0)
         displace = [
@@ -110,8 +111,7 @@
         kept = [radius, root] + [displace[a] * inverse for a in range(3)] + displace
         kept.append(-4.0 * inverse * (root * root))
         for slot, value in enumerate(kept):
-            for k in range(high):
-                geo[slot, number * high + k] = value[ROWS * k : ROWS * k + ROWS]
+            geo[slot, k] = value
 
     same = lax.broadcasted_iota(jnp.int32, (32, 256), 1) % 32 == lax.broadcasted_iota(
         jnp.int32, (32, 256), 0
@@ -120,89 +120,101 @@
         F32
     )
 
-    def one_cell(k, work, slope):
-        radius8 = geo[0, k]
-        root8 = geo[1, k]
-        scale8 = geo[8, k]
-        dir8 = [geo[2 + a, k] for a in range(3)]
-        for t in range(TILES):
-            lanes = slice(256 * t, 256 * t + 256)
-            away = pair_row(radius8, t) - centre
-            radial = jnp.exp(-4.0 * away * away)
-            steep = radial * (away * pair_row(scale8, t))
-            high = radial.astype(BF16).astype(F32)
-            steep_high = steep.astype(BF16).astype(F32)
-            zero = jnp.zeros_like(high)
-            stacked = jnp.concatenate(
-                [high, radial - high, high, zero, steep_high, steep - steep_high, steep_high, zero],
+    def pair_of_cells(ks):
+        lefts, mixeds, backs = {}, {}, {}
+        for k in ks:
+            work, slope = works[k], slopes[k]
+            radius8 = geo[0, k]
+            root8 = geo[1, k]
+            scale8 = geo[8, k]
+            dir8 = [geo[2 + a, k] for a in range(3)]
+            for t in range(TILES):
+                lanes = slice(256 * t, 256 * t + 256)
+                away = pair_row(radius8, t) - centre
+                radial = jnp.exp(-4.0 * away * away)
+                steep = radial * (away * pair_row(scale8, t))
+                high = radial.astype(BF16).astype(F32)
+                steep_high = steep.astype(BF16).astype(F32)
+                zero = jnp.zeros_like(high)
+                stacked = jnp.concatenate(
+                    [high, radial - high, high, zero, steep_high, steep - steep_high, steep_high, zero],
+                    axis=0,
+                ).astype(BF16)
+                both = dot(wr_ref[...], stacked)
+                zh = both[0:128]
+                th = jnp.tanh(zh)
+                up = 1.0 + th
+                root = pair_row(root8, t)
+                work[0:128, lanes] = (zh * up * (root * root)).astype(BF16)
+                slope[:, lanes] = up * (
+                    (1.0 + zh * (1.0 - th)) * both[128:256] - zh * (0.5 * root)
+                )
+                for a in range(3):
+                    work[128 + 32 * a : 160 + 32 * a, lanes] = jnp.where(
+                        same, pair_row(dir8[a], t), 0.0
+                    ).astype(BF16)
+                work[224:256, lanes] = jnp.zeros((32, 256), BF16)
+        yield
+        gathered = [dot_nt(works[k][0:128, :], works[k][128:256, :]).astype(BF16) for k in ks]
+        mixed = dot(webf_ref[...], jnp.concatenate(gathered, axis=1))
+        for i, k in enumerate(ks):
+            part = mixed[:, 128 * i : 128 * i + 128]
+            mixeds[k] = (2.0 * part.T).astype(BF16)
+            lefts[k] = jnp.concatenate([wtf_ref[...], part.astype(BF16)], axis=1)
+        yield
+        for k in ks:
+            work, left = works[k], lefts[k]
+            root8 = geo[1, k]
+            for t in range(TILES):
+                lanes = slice(256 * t, 256 * t + 256)
+                ph = dot(left, work[0:256, lanes])
+                th = jnp.tanh(ph)
+                up = 1.0 + th
+                root = pair_row(root8, t)
+                readout = wo_ref[...]
+                energy = jnp.sum(readout * (ph * up), axis=0, keepdims=True)
+                res[4, k, 2 * t : 2 * t + 1] = energy[:, 0:128]
+                res[4, k, 2 * t + 1 : 2 * t + 2] = energy[:, 128:256]
+                work[256:384, lanes] = (
+                    (readout * (0.5 * root * root)) * (up * (1.0 + ph * (1.0 - th)))
+                ).astype(BF16)
+        yield
+        gathered = [dot_nt(works[k][256:384, :], works[k][128:256, :]).astype(BF16) for k in ks]
+        back = dot(web_ref[...], jnp.concatenate(gathered, axis=1))
+        for i, k in enumerate(ks):
+            part = back[:, 128 * i : 128 * i + 128]
+            backs[k] = part.T.astype(BF16)
+            lefts[k] = jnp.concatenate(
+                [
+                    jnp.concatenate([part.astype(BF16), wtop_ref[...]], axis=1),
+                    jnp.concatenate([jnp.zeros((96, 128), BF16), mixeds[k][0:96]], axis=1),
+                ],
                 axis=0,
-            ).astype(BF16)
-            both = dot(wr_ref[...], stacked)
-            zh = both[0:128]
-            th = jnp.tanh(zh)
-            up = 1.0 + th
-            root = pair_row(root8, t)
-            work[0:128, lanes] = (zh * up * (root * root)).astype(BF16)
-            slope[:, lanes] = up * (
-                (1.0 + zh * (1.0 - th)) * both[128:256] - zh * (0.5 * root)
             )
-            for a in range(3):
-                work[128 + 32 * a : 160 + 32 * a, lanes] = jnp.where(
-                    same, pair_row(dir8[a], t), 0.0
-                ).astype(BF16)
-            work[224:256, lanes] = jnp.zeros((32, 256), BF16)
         yield
-        gathered = dot_nt(work[0:128, :], work[128:256, :])
-        mixed = dot(webf_ref[...], gathered.astype(BF16))
-        mixed_t = (2.0 * mixed.T).astype(BF16)
-        left = jnp.concatenate([wtf_ref[...], mixed.astype(BF16)], axis=1)
-        yield
-        for t in range(TILES):
-            lanes = slice(256 * t, 256 * t + 256)
-            ph = dot(left, work[0:256, lanes])
-            th = jnp.tanh(ph)
-            up = 1.0 + th
-            root = pair_row(root8, t)
-            readout = wo_ref[...]
-            energy = jnp.sum(readout * (ph * up), axis=0, keepdims=True)
-            res[4, k, 2 * t : 2 * t + 1] = energy[:, 0:128]
-            res[4, k, 2 * t + 1 : 2 * t + 2] = energy[:, 128:256]
-            work[256:384, lanes] = (
-                (readout * (0.5 * root * root)) * (up * (1.0 + ph * (1.0 - th)))
-            ).astype(BF16)
-        yield
-        back = dot_nt(work[256:384, :], work[128:256, :])
-        back = dot(web_ref[...], back.astype(BF16))
-        back_t = back.T.astype(BF16)
-        left = jnp.concatenate(
-            [
-                jnp.concatenate([back.astype(BF16), wtop_ref[...]], axis=1),
-                jnp.concatenate([jnp.zeros((96, 128), BF16), mixed_t[0:96]], axis=1),
-            ],
-            axis=0,
-        )
-        yield
-        for t in range(TILES):
-            lanes = slice(256 * t, 256 * t + 256)
-            latent = work[0:128, lanes]
-            slant = dot(left, work[128:384, lanes])
-            turned = slant[128:224] + dot(back_t[0:96], latent)
-            outcome = [
-                jnp.sum(jnp.where(same, turned[32 * a : 32 * a + 32], 0.0), axis=0, keepdims=True)
-                for a in range(3)
-            ]
-            outcome.append(jnp.sum(slant[0:128] * slope[:, lanes], axis=0, keepdims=True))
-            for value, slot in zip(outcome, (0, 1, 2, 3)):
-                res[slot, k, 2 * t : 2 * t + 1] = value[:, 0:128]
-                res[slot, k, 2 * t + 1 : 2 * t + 2] = value[:, 128:256]
-
-    runs = [one_cell(k, works[k], slopes[k]) for k in range(count)]
+        for k in ks:
+            work, slope, left, back_t = works[k], slopes[k], lefts[k], backs[k]
+            for t in range(TILES):
+                lanes = slice(256 * t, 256 * t + 256)
+                latent = work[0:128, lanes]
+                slant = dot(left, work[128:384, lanes])
+                turned = slant[128:224] + dot(back_t[0:96], latent)
+                outcome = [
+                    jnp.sum(jnp.where(same, turned[32 * a : 32 * a + 32], 0.0), axis=0, keepdims=True)
+                    for a in range(3)
+                ]
+                outcome.append(jnp.sum(slant[0:128] * slope[:, lanes], axis=0, keepdims=True))
+                for value, slot in zip(outcome, (0, 1, 2, 3)):
+                    res[slot, k, 2 * t : 2 * t + 1] = value[:, 0:128]
+                    res[slot, k, 2 * t + 1 : 2 * t + 2] = value[:, 128:256]
+
+    runs = [pair_of_cells((k, k + 1)) for k in range(0, count, 2)]
     done = object()
-    for tick in range(6 + count):
-        for k in range(count):
-            if tick >= k and runs[k] is not None:
-                if next(runs[k], done) is done:
-                    runs[k] = None
+    for tick in range(6 + len(runs)):
+        for number in reversed(range(len(runs))):
+            if tick >= number and runs[number] is not None:
+                if next(runs[number], done) is done:
+                    runs[number] = None
 
     radius, root = geo[0], geo[1]
     direction = [geo[2 + a] for a in range(3)]
@@ -240,8 +252,8 @@
             hots.append(jnp.where(iota96 == place[r : r + 1], 1.0, 0.0).astype(BF16))
             lefts.append(spread_rows(col[r : r + 1], [-term[a][r : r + 1] for a in range(3)]))
         added = dot_nt(jnp.concatenate(hots, axis=1), jnp.concatenate(lefts, axis=1))
-        at = 32 * layer - base
-        acc[at : at + 96, 0:96] += added
+        at = 32 * layer - bases[layer]
+        acc[side[layer], at : at + 96, 0:96] += added
         term.append(res[4, k])
         for slot in range(4):
             line = jnp.sum(term[slot][0:USED], axis=0, keepdims=True)
@@ -249,14 +261,15 @@
             line = line + pltpu.roll(line, 64, 1)
             own_sum[slot, block : block + 1, :] += jnp.where(lane1 // 32 == layer, line, 0.0)
 
-    flipped = acc[...].T
+    flipped = acc[0].T
     total = flipped[0:48] + flipped[48:96]
     if outer:
-        extra_ref[...] = total
-        turn, inside = (96, lane48 < 96) if base == 0 else (32, lane48 >= 32)
-        total = jnp.where(inside, pltpu.roll(total, turn, 1), 0.0)
-    elif first:
-        extra_ref[...] = tab_ref[...]
+        flipped = acc[1].T
+        upper = flipped[0:48] + flipped[48:96]
+        extra_ref[...] = jnp.where(lane48 < 96, total, upper)
+        total = jnp.where(lane48 < 96, pltpu.roll(total, 96, 1), 0.0) + jnp.where(
+            lane48 >= 32, pltpu.roll(upper, 32, 1), 0.0
+        )
     site = own_sum[3]
     if not first:
         total = total + before_ref[...]
@@ -266,40 +279,36 @@
         for block in blocks:
             line = a * 16 + (block // 2 + 1) * 4 + block % 2 + 1
             spread_ref[line : line + 1, :] += own_sum[a, block : block + 1, :]
-    site_ref[...] = site
-    if last:
+    if not last:
+        site_ref[...] = site
+    else:
         listed = list_ref[...]
         sent = jnp.zeros((16, 128), F32)
         for block in range(4):
             table = jnp.broadcast_to(site[block : block + 1], (16, 128))
             picked = jnp.take_along_axis(table, listed & 127, axis=1, mode="promise_in_bounds")
             sent = jnp.where(listed >> 7 == block, picked, sent)
-        extra_ref[...] = sent
-
-
-def force_call(tab, key, weights, blocks, layers, halo=None, before=None, listed=None):
+        site_ref[...] = sent
+
+
+def force_call(tab, key, weights, blocks, layers, halo=(), before=None, listed=None):
     first, last = before is None, listed is not None
     count = len(blocks) * len(layers)
-    args = [tab, key, *weights]
-    if halo is not None:
-        args.append(halo)
+    args = [tab, key, *weights, *halo]
     if not first:
         args += before
     if last:
         args.append(listed)
+    outs = [48, 16 if last else 8] + [48] * len(halo[:1])
     return pl.pallas_call(
         functools.partial(force_kernel, blocks, layers, first, last),
-        out_shape=(
-            jax.ShapeDtypeStruct((48, 128), F32),
-            jax.ShapeDtypeStruct((8, 128), F32),
-            jax.ShapeDtypeStruct((16 if last else 48, 128), F32),
-        ),
+        out_shape=tuple(jax.ShapeDtypeStruct((rows, 128), F32) for rows in outs),
         scratch_shapes=[
             pltpu.VMEM((9, count, ROWS, 128), F32),
             pltpu.VMEM((5, count, ROWS, 128), F32),
-            pltpu.VMEM((128, 128), F32),
+            pltpu.VMEM((2, 128, 128), F32),
             pltpu.VMEM((4, 8, 128), F32),
-            pltpu.VMEM((48, 128), F32),
+            pltpu.VMEM((2, 48, 128), F32),
         ]
         + [pltpu.VMEM((384, 768), BF16)] * count
         + [pltpu.VMEM((128, 768), F32)] * count,
@@ -423,18 +432,18 @@
         wide_coords = wide_coords + half * wide_speed + change[0:3]
         wide_speed = wide_speed + change[3:6]
         flat = wide_coords.reshape(48, 128)
-        below = shifted(flat[:, 96:128], "gz", 1)
-        *state, again = force_call(flat, key, weights, (0, 1), (1, 2))
-        above = shifted(again[:, 0:32], "gz", -1)
-        *state, rim = force_call(flat, key, weights, (0, 1, 2, 3), (0,), below, state)
+        halo = shifted(flat[:, 96:128], "gz", 1), shifted(flat[:, 0:32], "gz", -1)
+        state = force_call(flat, key, weights, (0, 1), (1, 2))
+        *state, rim = force_call(flat, key, weights, (0, 1, 2, 3), (0, 3), halo, state)
+        from_below = shifted(rim[:, 96:128], "gz", 1)
         from_above = shifted(rim[:, 0:32], "gz", -1)
-        *state, rim = force_call(flat, key, weights, (0, 1, 2, 3), (3,), above, state)
-        from_below = shifted(rim[:, 96:128], "gz", 1)
-        state = force_call(flat, key, weights, (2, 3), (1, 2), before=state, listed=listed)
+        spread, sent = force_call(
+            flat, key, weights, (2, 3), (1, 2), before=state, listed=listed
+        )
         edges = jnp.concatenate([from_below, jnp.zeros((48, 64), F32), from_above], axis=1)
-        force = (state[0] + edges).reshape(3, 4, 4, 128)
+        force = (spread + edges).reshape(3, 4, 4, 128)
         change = jnp.concatenate([half * half * force, half * force], axis=0)
-        return (wide_coords, wide_speed, change, force, state[2])
+        return (wide_coords, wide_speed, change, force, sent)
 
     first = jnp.concatenate([jnp.where(occupied, coords, UNOCCUPIED), speed], axis=0)
     first = with_halo(with_halo(first, "gx", 1), "gy", 2)

time: 96.1 us -> 90.6 us (0.943)
  Pallas kernels: 35.5 us -> 27.7 us
  starting transfers between devices: 35 us -> 37.4 us
    pallas_call x8 -> x6, Pallas kernels: 34 us -> 26.2 us  [force_call(): pl.pallas_call(functools.partial(force_kernel, blocks, layers, first, las...]
    all_to_all x1, starting transfers between devices: 7.04 us -> 8.73 us  [on_device(): lax.all_to_all(sent, 'gz', split_axis=0, concat_axis=0, tiled=True)]
  transfers between devices with their start and end apart: 21 -> 21, of which waited for: 8 -> 8; matrix products, arithmetic and copies ran while one was open for 4% -> 4% of each run, Pallas kernels for 36% -> 16%
where the time goes in v1:
time: 90.6 us; the launch traced here: 90.3 us
  starting transfers between devices  37.4 us (41%)
  Pallas kernels  27.7 us (31%)
  waiting for transfers between devices  13.6 us (15%)
  local copies, waits for them, and re-layouts  6.2 us (7%)
  other arithmetic  3.74 us (4%)
  between operations  0.91 us (1%)
    ppermute x20, starting transfers between devices, shifted(): lax.ppermute(array, axis, [(i, (i + step) % peers) for i in range(peers)])  28.7 us
    pallas_call x6, Pallas kernels, force_call(): pl.pallas_call(functools.partial(force_kernel, blocks, layers, first, las...  26.2 us
    ppermute x20, waiting for transfers between devices, shifted(): lax.ppermute(array, axis, [(i, (i + step) % peers) for i in range(peers)])  10.4 us
    all_to_all x1, starting transfers between devices, on_device(): lax.all_to_all(sent, 'gz', split_axis=0, concat_axis=0, tiled=True)  8.73 us
    all_to_all x1, waiting for transfers between devices, on_device(): lax.all_to_all(sent, 'gz', split_axis=0, concat_axis=0, tiled=True)  3.14 us
    unnamed x27, local copies, waits for them, and re-layouts  2.2 us
  transfers between devices with their start and end apart: 21, of which 8 were waited for; matrix products, arithmetic and copies ran while one was open for 4% of the time, Pallas kernels for 16%

profile of v1, /device:TPU:1, one launch (start us, length us, event | category | flops | bytes accessed | tf_op | source)
XLA Modules:
  0.0 90.3 jit_solution(14845648762477766164)
XLA Ops:
  0.7 0.8 lt.45
  1.6 1.3 %broadcast_select_fusion = (f32[3,2,2,128]{3,2,1,0:T(2,128)S(1)}, f32[3,2,2,128]{3,2,1,0:T(2,128)}, f32[3,2,2,128]{3,2,1,0:T(2,128)S(1)}) fusion(pred[2,2,128]{2,1,0:T(4,128)(4,1)S(1)} %broadcast_compare_fusion, f32[3,2,2,128]{3,2,1,0:T(2,128)} %param.14, f32[3,2,2,128]{3,2,1,0:T(2,128)} %param.15, f32[3,2,2,128]{3,2,1,0:T(2,128)} %param.16), kind=kLoop, calls=%fused_computation.55 | loop fusion | flops 7680 | bytes 37376 | tf_op jit(solution)/shard_map/jit(_where)/select_n | solution.py:448
  2.9 3.4 %collective-permute-start.9 = (f32[6,1,2,128]{3,2,1,0:T(2,128)S(1)}, f32[6,1,2,128]{3,2,1,0:T(2,128)S(1)}, u32[]{:S(2)}, u32[]{:S(2)}) collective-permute-start(f32[6,1,2,128]{3,2,1,0:T(2,128)S(1)} %get-tuple-element.391), channel_id=1, source_target_pairs={{0,192},{64,0},{128,64},{192,128},{1,193},{65,1},{129,65},{193,129... | collective-permute-start | bytes 18440 | tf_op jit(solution)/shard_map/ppermute | solution.py:382
  6.5 1.2 %fusion.6 = s32[2,2,4,6,4,32]{5,4,2,3,1,0:T(4,128)S(1)} fusion(s32[4,6,2,2,4,32]{5,4,3,2,1,0:T(4,128)S(1)} %reshape.47), kind=kLoop, calls=%fused_computation.23 | loop fusion | flops 638976 | bytes 98304 | tf_op jit(solution)/shard_map/transpose | solution.py:376
  8.1 1.9 %collective-permute-done.8 = f32[6,1,2,128]{3,2,1,0:T(2,128)S(1)} collective-permute-done((f32[6,1,2,128]{3,2,1,0:T(2,128)S(1)}, f32[6,1,2,128]{3,2,1,0:T(2,128)S(1)}, u32[]{:S(2)}, u32[]{:S(2)}) %collective-permute-start.8) | collective-permute-done | bytes 6176 | tf_op jit(solution)/shard_map/ppermute | solution.py:382
  10.1 2.8 %collective-permute-start.11 = (f32[6,4,1,128]{3,2,1,0:T(1,128)S(1)}, f32[6,4,1,128]{3,2,1,0:T(1,128)S(1)}, u32[]{:S(2)}, u32[]{:S(2)}) collective-permute-start(f32[6,4,1,128]{3,2,1,0:T(1,128)S(1)} %get-tuple-element.387), channel_id=1, source_target_pairs={{0,48},{16,0},{32,16},{48,32},{1,49},{17,1},{33,17},{49,33},{2,50}... | collective-permute-start | bytes 36872 | tf_op jit(solution)/shard_map/ppermute | solution.py:382
  15.5 1.2 %collective-permute-done.10 = f32[6,4,1,128]{3,2,1,0:T(1,128)S(1)} collective-permute-done((f32[6,4,1,128]{3,2,1,0:T(1,128)S(1)}, f32[6,4,1,128]{3,2,1,0:T(1,128)S(1)}, u32[]{:S(2)}, u32[]{:S(2)}) %collective-permute-start.10) | collective-permute-done | bytes 12320 | tf_op jit(solution)/shard_map/ppermute | solution.py:382
  16.7 53.5 %while.28 = (s32[]{:T(128)}, f32[3,4,4,128]{3,2,1,0:T(4,128)S(1)}, f32[3,4,4,128]{3,2,1,0:T(4,128)S(1)}, f32[6,4,4,128]{3,2,1,0:T(4,128)S(1)}, f32[3,4,4,128]{3,...) while((s32[]{:T(128)}, f32[3,4,4,128]{3,2,1,0:T(4,128)S(1)}, ...), condition=%wide.region_3.4_spmd.clone, body=%wide.region_0.3_spmd.clone.sunk | while | flops 12800129024 | bytes 2545088 | solution.py:452
  17.0 5.1 %collective-permute-start.4 = (f32[48,32]{1,0:T(8,128)S(1)}, f32[48,32]{1,0:T(8,128)S(1)}, u32[]{:S(2)}, u32[]{:S(2)}) collective-permute-start(f32[48,32]{1,0:T(8,128)S(1)} %get-tuple-element.490), channel_id=1, source_target_pairs={{0,1},{1,2},{2,3},{3,4},{4,5},{5,6},{6,7},{7,8},{8,9},{9,10},{10,1... | collective-permute-start | bytes 18440 | tf_op jit(solution)/shard_map/while/body/eval_jaxpr/ppermute | solution.py:382
  22.2 3.3 %force.15 = (f32[48,128]{1,0:T(8,128)S(1)}, f32[8,128]{1,0:T(8,128)S(1)}) custom-call(f32[48,128]{1,0:T(8,128)S(1)} %bitcast.21, s32[4,4,8,128]{3,2,1,0:T(8,128)S(1)} %get-tuple-element.545.refs_1_, bf16[256,64]{1,0:T(8,128)(2,1)S(1)} %get-tuple-element.546.refs_2_, bf16[128,128]{1,0:T(8,128)(2,1)S(1)} %get-tuple-element.547.refs_3_, ...), custom_call_target="tpu_custom_call" | custom-call | flops 3200000000 | bytes 300000 | tf_op jit(solution)/shard_map/while/body/eval_jaxpr/force/pallas_call | solution.py:303
  25.5 6.1 %force.16 = (f32[48,128]{1,0:T(8,128)S(1)}, f32[8,128]{1,0:T(8,128)S(1)}, f32[48,128]{1,0:T(8,128)S(1)}) custom-call(f32[48,128]{1,0:T(8,128)S(1)} %bitcast.22, s32[4,4,8,128]{3,2,1,0:T(8,128)S(1)} %get-tuple-element.545.refs_1_, bf16[256,64]{1,0:T(8,128)(2,1)S(1)} %get-tuple-element.546.refs_2_, bf16[128,128]{1,0:T(8,128)(2,1)S(1)} %get-tuple-element.547.refs_3_, ...), custom_call_target="tpu_custom_call" | custom-call | flops 6400000000 | bytes 300000 | tf_op jit(solution)/shard_map/while/body/eval_jaxpr/force/pallas_call | solution.py:303
  31.7 1.4 %collective-permute-start.6 = (f32[48,32]{1,0:T(8,128)S(1)}, f32[48,32]{1,0:T(8,128)S(1)}, u32[]{:S(2)}, u32[]{:S(2)}) collective-permute-start(f32[48,32]{1,0:T(8,128)S(1)} %get-tuple-element.498), channel_id=1, source_target_pairs={{0,15},{1,0},{2,1},{3,2},{4,3},{5,4},{6,5},{7,6},{8,7},{9,8},{10,9... | collective-permute-start | bytes 18440 | tf_op jit(solution)/shard_map/while/body/eval_jaxpr/ppermute | solution.py:382
  33.5 3.7 %force.17 = (f32[48,128]{1,0:T(8,128)S(1)}, f32[16,128]{1,0:T(8,128)}) custom-call(f32[48,128]{1,0:T(8,128)S(1)} %bitcast.23, s32[4,4,8,128]{3,2,1,0:T(8,128)S(1)} %get-tuple-element.545.refs_1_, bf16[256,64]{1,0:T(8,128)(2,1)S(1)} %get-tuple-element.546.refs_2_, bf16[128,128]{1,0:T(8,128)(2,1)S(1)} %get-tuple-element.547.refs_3_, ...), custom_call_target="tpu_custom_call" | custom-call | flops 3200000000 | bytes 300000 | tf_op jit(solution)/shard_map/while/body/eval_jaxpr/force/pallas_call | solution.py:303
  37.9 9.5 %conditional.3 = (f32[6,4,4,128]{3,2,1,0:T(4,128)S(1)}) conditional(s32[]{:T(128)} %convert_element_type.50, f32[6,4,4,128]{3,2,1,0:T(4,128)S(1)} %get-tuple-element.524, f32[6,4,4,128]{3,2,1,0:T(4,128)S(1)} %get-tuple-element.524), branch_computations={%region_1.1_spmd, %region_2.2_spmd} | conditional | flops 49152 | bytes 884904 | solution.py:429
  38.0 1.5 %collective-permute-start = (f32[6,2,4,128]{3,2,1,0:T(4,128)S(1)}, f32[6,2,4,128]{3,2,1,0:T(4,128)S(1)}, u32[]{:S(2)}, u32[]{:S(2)}) collective-permute-start(f32[6,2,4,128]{3,2,1,0:T(4,128)S(1)} %get-tuple-element.370), channel_id=1, source_target_pairs={{0,64},{64,128},{128,192},{192,0},{1,65},{65,129},{129,193},{193,1... | collective-permute-start | bytes 73736 | tf_op jit(solution)/shard_map/while/body/eval_jaxpr/cond/branch_0_fun/ppermute | solution.py:382
  39.5 1.2 %collective-permute-done.1 = f32[6,2,4,128]{3,2,1,0:T(4,128)S(1)} collective-permute-done((f32[6,2,4,128]{3,2,1,0:T(4,128)S(1)}, f32[6,2,4,128]{3,2,1,0:T(4,128)S(1)}, u32[]{:S(2)}, u32[]{:S(2)}) %collective-permute-start.1) | collective-permute-done | bytes 24608 | tf_op jit(solution)/shard_map/while/body/eval_jaxpr/cond/branch_0_fun/ppermute | solution.py:382
  40.7 1.3 %collective-permute-done = f32[6,2,4,128]{3,2,1,0:T(4,128)S(1)} collective-permute-done((f32[6,2,4,128]{3,2,1,0:T(4,128)S(1)}, f32[6,2,4,128]{3,2,1,0:T(4,128)S(1)}, u32[]{:S(2)}, u32[]{:S(2)}) %collective-permute-start) | collective-permute-done | bytes 24608 | tf_op jit(solution)/shard_map/while/body/eval_jaxpr/cond/branch_0_fun/ppermute | solution.py:382
  42.1 1.4 %collective-permute-start.3 = (f32[6,4,2,128]{3,2,1,0:T(2,128)S(1)}, f32[6,4,2,128]{3,2,1,0:T(2,128)S(1)}, u32[]{:S(2)}, u32[]{:S(2)}) collective-permute-start(f32[6,4,2,128]{3,2,1,0:T(2,128)S(1)} %get-tuple-element.369), channel_id=1, source_target_pairs={{0,48},{16,0},{32,16},{48,32},{1,49},{17,1},{33,17},{49,33},{2,50}... | collective-permute-start | bytes 73736 | tf_op jit(solution)/shard_map/while/body/eval_jaxpr/cond/branch_0_fun/ppermute | solution.py:382
  43.6 1.3 %collective-permute-done.3 = f32[6,4,2,128]{3,2,1,0:T(2,128)S(1)} collective-permute-done((f32[6,4,2,128]{3,2,1,0:T(2,128)S(1)}, f32[6,4,2,128]{3,2,1,0:T(2,128)S(1)}, u32[]{:S(2)}, u32[]{:S(2)}) %collective-permute-start.3) | collective-permute-done | bytes 24608 | tf_op jit(solution)/shard_map/while/body/eval_jaxpr/cond/branch_0_fun/ppermute | solution.py:382
  44.9 2.5 %collective-permute-done.2 = f32[6,4,2,128]{3,2,1,0:T(2,128)S(1)} collective-permute-done((f32[6,4,2,128]{3,2,1,0:T(2,128)S(1)}, f32[6,4,2,128]{3,2,1,0:T(2,128)S(1)}, u32[]{:S(2)}, u32[]{:S(2)}) %collective-permute-start.2) | collective-permute-done | bytes 24608 | tf_op jit(solution)/shard_map/while/body/eval_jaxpr/cond/branch_0_fun/ppermute | solution.py:382
  47.5 2.5 %collective-permute-start.4 = (f32[48,32]{1,0:T(8,128)S(1)}, f32[48,32]{1,0:T(8,128)S(1)}, u32[]{:S(2)}, u32[]{:S(2)}) collective-permute-start(f32[48,32]{1,0:T(8,128)S(1)} %get-tuple-element.490), channel_id=1, source_target_pairs={{0,1},{1,2},{2,3},{3,4},{4,5},{5,6},{6,7},{7,8},{8,9},{9,10},{10,1... | collective-permute-start | bytes 18440 | tf_op jit(solution)/shard_map/while/body/eval_jaxpr/ppermute | solution.py:382
  50.0 2.9 %collective-permute-start.5 = (f32[48,32]{1,0:T(8,128)S(1)}, f32[48,32]{1,0:T(8,128)S(1)}, u32[]{:S(2)}, u32[]{:S(2)}) collective-permute-start(f32[48,32]{1,0:T(8,128)S(1)} %get-tuple-element.491), channel_id=1, source_target_pairs={{0,15},{1,0},{2,1},{3,2},{4,3},{5,4},{6,5},{7,6},{8,7},{9,8},{10,9... | collective-permute-start | bytes 18440 | tf_op jit(solution)/shard_map/while/body/eval_jaxpr/ppermute | solution.py:382
  53.0 3.3 %force.15 = (f32[48,128]{1,0:T(8,128)S(1)}, f32[8,128]{1,0:T(8,128)S(1)}) custom-call(f32[48,128]{1,0:T(8,128)S(1)} %bitcast.21, s32[4,4,8,128]{3,2,1,0:T(8,128)S(1)} %get-tuple-element.545.refs_1_, bf16[256,64]{1,0:T(8,128)(2,1)S(1)} %get-tuple-element.546.refs_2_, bf16[128,128]{1,0:T(8,128)(2,1)S(1)} %get-tuple-element.547.refs_3_, ...), custom_call_target="tpu_custom_call" | custom-call | flops 3200000000 | bytes 300000 | tf_op jit(solution)/shard_map/while/body/eval_jaxpr/force/pallas_call | solution.py:303
  56.4 6.1 %force.16 = (f32[48,128]{1,0:T(8,128)S(1)}, f32[8,128]{1,0:T(8,128)S(1)}, f32[48,128]{1,0:T(8,128)S(1)}) custom-call(f32[48,128]{1,0:T(8,128)S(1)} %bitcast.22, s32[4,4,8,128]{3,2,1,0:T(8,128)S(1)} %get-tuple-element.545.refs_1_, bf16[256,64]{1,0:T(8,128)(2,1)S(1)} %get-tuple-element.546.refs_2_, bf16[128,128]{1,0:T(8,128)(2,1)S(1)} %get-tuple-element.547.refs_3_, ...), custom_call_target="tpu_custom_call" | custom-call | flops 6400000000 | bytes 300000 | tf_op jit(solution)/shard_map/while/body/eval_jaxpr/force/pallas_call | solution.py:303
  62.5 3.0 %collective-permute-start.6 = (f32[48,32]{1,0:T(8,128)S(1)}, f32[48,32]{1,0:T(8,128)S(1)}, u32[]{:S(2)}, u32[]{:S(2)}) collective-permute-start(f32[48,32]{1,0:T(8,128)S(1)} %get-tuple-element.498), channel_id=1, source_target_pairs={{0,15},{1,0},{2,1},{3,2},{4,3},{5,4},{6,5},{7,6},{8,7},{9,8},{10,9... | collective-permute-start | bytes 18440 | tf_op jit(solution)/shard_map/while/body/eval_jaxpr/ppermute | solution.py:382
  65.5 3.7 %force.17 = (f32[48,128]{1,0:T(8,128)S(1)}, f32[16,128]{1,0:T(8,128)}) custom-call(f32[48,128]{1,0:T(8,128)S(1)} %bitcast.23, s32[4,4,8,128]{3,2,1,0:T(8,128)S(1)} %get-tuple-element.545.refs_1_, bf16[256,64]{1,0:T(8,128)(2,1)S(1)} %get-tuple-element.546.refs_2_, bf16[128,128]{1,0:T(8,128)(2,1)S(1)} %get-tuple-element.547.refs_3_, ...), custom_call_target="tpu_custom_call" | custom-call | flops 3200000000 | bytes 300000 | tf_op jit(solution)/shard_map/while/body/eval_jaxpr/force/pallas_call | solution.py:303
  71.0 1.5 %collective-permute-start.12 = (f32[3,1,4,128]{3,2,1,0:T(4,128)S(1)}, f32[3,1,4,128]{3,2,1,0:T(4,128)S(1)}, u32[]{:S(2)}, u32[]{:S(2)}) collective-permute-start(f32[3,1,4,128]{3,2,1,0:T(4,128)S(1)} %get-tuple-element.384), channel_id=1, source_target_pairs={{0,64},{64,128},{128,192},{192,0},{1,65},{65,129},{129,193},{193,1... | collective-permute-start | bytes 18440 | tf_op jit(solution)/shard_map/ppermute | solution.py:382
  72.4 8.7 %all-to-all-start = ((f32[16,1,128]{2,1,0:T(1,128)}), f32[16,1,128]{2,1,0:T(1,128)S(1)}, u32[]{:S(2)}, u32[]{:S(2)}) async-start(f32[16,1,128]{2,1,0:T(1,128)} %bitcast.4), calls=%async_computation | async-start | bytes 16384 | tf_op jit(solution)/shard_map/all_to_all | solution.py:455
  81.3 2.7 %collective-permute-start.15 = (f32[3,2,1,128]{3,2,1,0:T(1,128)S(1)}, f32[3,2,1,128]{3,2,1,0:T(1,128)S(1)}, u32[]{:S(2)}, u32[]{:S(2)}) collective-permute-start(f32[3,2,1,128]{3,2,1,0:T(1,128)S(1)} %get-tuple-element.388), channel_id=1, source_target_pairs={{0,48},{16,0},{32,16},{48,32},{1,49},{17,1},{33,17},{49,33},{2,50}... | collective-permute-start | bytes 9224 | tf_op jit(solution)/shard_map/ppermute | solution.py:382
  84.0 1.0 %collective-permute-done.14.below_ref = f32[3,2,1,128]{3,2,1,0:T(1,128)S(1)} collective-permute-done((f32[3,2,1,128]{3,2,1,0:T(1,128)S(1)}, f32[3,2,1,128]{3,2,1,0:T(1,128)S(1)}, u32[]{:S(2)}, u32[]{:S(2)}) %collective-permute-start.14) | collective-permute-done | bytes 3104 | tf_op jit(solution)/shard_map/ppermute | solution.py:382
  85.0 3.1 %all-to-all-done = f32[16,1,128]{2,1,0:T(1,128)S(1)} async-done(((f32[16,1,128]{2,1,0:T(1,128)}), f32[16,1,128]{2,1,0:T(1,128)S(1)}, u32[]{:S(2)}, u32[]{:S(2)}) %all-to-all-start) | async-done | bytes 8224 | tf_op jit(solution)/shard_map/all_to_all | solution.py:455
  88.8 1.5 %finish.1 = (f32[3,2,2,128]{3,2,1,0:T(2,128)}, f32[3,2,2,128]{3,2,1,0:T(2,128)}, f32[3,2,2,128]{3,2,1,0:T(2,128)}, f32[4,128]{1,0:T(4,128)}) custom-call(f32[16,128]{1,0:T(8,128)} %bitcast.26, f32[3,2,4,128]{3,2,1,0:T(4,128)} %copy-done.3, f32[3,2,1,128]{3,2,1,0:T(1,128)} %copy-done.8, f32[3,2,1,128]{3,2,1,0:T(1,128)} %copy-done.9, ...), custom_call_target="tpu_custom_call" | custom-call | tf_op jit(solution)/shard_map/finish/pallas_call | solution.py:460
  (105 shorter events, 7.4 us)
Async XLA Ops:
  0.6 7.2 %copy-start = (bf16[128,128]{1,0:T(8,128)(2,1)S(1)}, bf16[128,128]{1,0:T(8,128)(2,1)}, u32[]{:S(2)}) copy-start(bf16[128,128]{1,0:T(8,128)(2,1)} %param.21) | copy-start | bytes 98308
  0.6 5.7 %copy-start.5 = (s32[24,2,2,128]{3,2,1,0:T(2,128)S(1)}, s32[24,2,2,128]{3,2,1,0:T(2,128)}, u32[]{:S(2)}) copy-start(s32[24,2,2,128]{3,2,1,0:T(2,128)} %param.18) | copy-start | bytes 147460
  2.9 5.2 %collective-permute-start.9 = (f32[6,1,2,128]{3,2,1,0:T(2,128)S(1)}, f32[6,1,2,128]{3,2,1,0:T(2,128)S(1)}, u32[]{:S(2)}, u32[]{:S(2)}) collective-permute-start(f32[6,1,2,128]{3,2,1,0:T(2,128)S(1)} %get-tuple-element.391), channel_id=1, source_target_pairs={{0,192},{64,0},{128,64},{192,128},{1,193},{65,1},{129,65},{193,129... | collective-permute-start | bytes 18440 | tf_op jit(solution)/shard_map/ppermute | solution.py:382
  6.3 3.7 %collective-permute-start.8 = (f32[6,1,2,128]{3,2,1,0:T(2,128)S(1)}, f32[6,1,2,128]{3,2,1,0:T(2,128)S(1)}, u32[]{:S(2)}, u32[]{:S(2)}) collective-permute-start(f32[6,1,2,128]{3,2,1,0:T(2,128)S(1)} %get-tuple-element.390), channel_id=1, source_target_pairs={{0,64},{64,128},{128,192},{192,0},{1,65},{65,129},{129,193},{193,1... | collective-permute-start | bytes 18440 | tf_op jit(solution)/shard_map/ppermute | solution.py:382
  6.5 1.3 %copy-start.7 = (f32[8,128]{1,0:T(8,128)S(1)}, f32[8,128]{1,0:T(8,128)}, u32[]{:S(2)}) copy-start(f32[8,128]{1,0:T(8,128)} %param.20) | copy-start | bytes 12292
  6.5 1.3 %copy-start.4 = (bf16[256,128]{1,0:T(8,128)(2,1)S(1)}, bf16[256,128]{1,0:T(8,128)(2,1)}, u32[]{:S(2)}) copy-start(bf16[256,128]{1,0:T(8,128)(2,1)} %param.22) | copy-start | bytes 196612
  10.1 5.4 %collective-permute-start.11 = (f32[6,4,1,128]{3,2,1,0:T(1,128)S(1)}, f32[6,4,1,128]{3,2,1,0:T(1,128)S(1)}, u32[]{:S(2)}, u32[]{:S(2)}) collective-permute-start(f32[6,4,1,128]{3,2,1,0:T(1,128)S(1)} %get-tuple-element.387), channel_id=1, source_target_pairs={{0,48},{16,0},{32,16},{48,32},{1,49},{17,1},{33,17},{49,33},{2,50}... | collective-permute-start | bytes 36872 | tf_op jit(solution)/shard_map/ppermute | solution.py:382
  12.9 3.8 %collective-permute-start.10 = (f32[6,4,1,128]{3,2,1,0:T(1,128)S(1)}, f32[6,4,1,128]{3,2,1,0:T(1,128)S(1)}, u32[]{:S(2)}, u32[]{:S(2)}) collective-permute-start(f32[6,4,1,128]{3,2,1,0:T(1,128)S(1)} %get-tuple-element.386), channel_id=1, source_target_pairs={{0,16},{16,32},{32,48},{48,0},{1,17},{17,33},{33,49},{49,1},{2,18}... | collective-permute-start | bytes 36872 | tf_op jit(solution)/shard_map/ppermute | solution.py:382
  13.4 0.7 copy-start.10
  14.8 0.7 copy-start.11
  17.0 8.5 %collective-permute-start.4 = (f32[48,32]{1,0:T(8,128)S(1)}, f32[48,32]{1,0:T(8,128)S(1)}, u32[]{:S(2)}, u32[]{:S(2)}) collective-permute-start(f32[48,32]{1,0:T(8,128)S(1)} %get-tuple-element.490), channel_id=1, source_target_pairs={{0,1},{1,2},{2,3},{3,4},{4,5},{5,6},{6,7},{7,8},{8,9},{9,10},{10,1... | collective-permute-start | bytes 18440 | tf_op jit(solution)/shard_map/while/body/eval_jaxpr/ppermute | solution.py:382
  22.1 3.5 %collective-permute-start.5 = (f32[48,32]{1,0:T(8,128)S(1)}, f32[48,32]{1,0:T(8,128)S(1)}, u32[]{:S(2)}, u32[]{:S(2)}) collective-permute-start(f32[48,32]{1,0:T(8,128)S(1)} %get-tuple-element.491), channel_id=1, source_target_pairs={{0,15},{1,0},{2,1},{3,2},{4,3},{5,4},{6,5},{7,6},{8,7},{9,8},{10,9... | collective-permute-start | bytes 18440 | tf_op jit(solution)/shard_map/while/body/eval_jaxpr/ppermute | solution.py:382
  31.7 5.5 %collective-permute-start.6 = (f32[48,32]{1,0:T(8,128)S(1)}, f32[48,32]{1,0:T(8,128)S(1)}, u32[]{:S(2)}, u32[]{:S(2)}) collective-permute-start(f32[48,32]{1,0:T(8,128)S(1)} %get-tuple-element.498), channel_id=1, source_target_pairs={{0,15},{1,0},{2,1},{3,2},{4,3},{5,4},{6,5},{7,6},{8,7},{9,8},{10,9... | collective-permute-start | bytes 18440 | tf_op jit(solution)/shard_map/while/body/eval_jaxpr/ppermute | solution.py:382
  33.1 4.1 %collective-permute-start.7 = (f32[48,32]{1,0:T(8,128)S(1)}, f32[48,32]{1,0:T(8,128)S(1)}, u32[]{:S(2)}, u32[]{:S(2)}) collective-permute-start(f32[48,32]{1,0:T(8,128)S(1)} %get-tuple-element.499), channel_id=1, source_target_pairs={{0,1},{1,2},{2,3},{3,4},{4,5},{5,6},{6,7},{7,8},{8,9},{9,10},{10,1... | collective-permute-start | bytes 18440 | tf_op jit(solution)/shard_map/while/body/eval_jaxpr/ppermute | solution.py:382
  37.3 0.6 copy-start.1
  38.0 2.8 %collective-permute-start.1 = (f32[6,2,4,128]{3,2,1,0:T(4,128)S(1)}, f32[6,2,4,128]{3,2,1,0:T(4,128)S(1)}, u32[]{:S(2)}, u32[]{:S(2)}) collective-permute-start(f32[6,2,4,128]{3,2,1,0:T(4,128)S(1)} %get-tuple-element.371), channel_id=1, source_target_pairs={{0,192},{64,0},{128,64},{192,128},{1,193},{65,1},{129,65},{193,129... | collective-permute-start | bytes 73736 | tf_op jit(solution)/shard_map/while/body/eval_jaxpr/cond/branch_0_fun/ppermute | solution.py:382
  38.0 4.0 %collective-permute-start = (f32[6,2,4,128]{3,2,1,0:T(4,128)S(1)}, f32[6,2,4,128]{3,2,1,0:T(4,128)S(1)}, u32[]{:S(2)}, u32[]{:S(2)}) collective-permute-start(f32[6,2,4,128]{3,2,1,0:T(4,128)S(1)} %get-tuple-element.370), channel_id=1, source_target_pairs={{0,64},{64,128},{128,192},{192,0},{1,65},{65,129},{129,193},{193,1... | collective-permute-start | bytes 73736 | tf_op jit(solution)/shard_map/while/body/eval_jaxpr/cond/branch_0_fun/ppermute | solution.py:382
  42.1 2.8 %collective-permute-start.3 = (f32[6,4,2,128]{3,2,1,0:T(2,128)S(1)}, f32[6,4,2,128]{3,2,1,0:T(2,128)S(1)}, u32[]{:S(2)}, u32[]{:S(2)}) collective-permute-start(f32[6,4,2,128]{3,2,1,0:T(2,128)S(1)} %get-tuple-element.369), channel_id=1, source_target_pairs={{0,48},{16,0},{32,16},{48,32},{1,49},{17,1},{33,17},{49,33},{2,50}... | collective-permute-start | bytes 73736 | tf_op jit(solution)/shard_map/while/body/eval_jaxpr/cond/branch_0_fun/ppermute | solution.py:382
  43.5 3.9 %collective-permute-start.2 = (f32[6,4,2,128]{3,2,1,0:T(2,128)S(1)}, f32[6,4,2,128]{3,2,1,0:T(2,128)S(1)}, u32[]{:S(2)}, u32[]{:S(2)}) collective-permute-start(f32[6,4,2,128]{3,2,1,0:T(2,128)S(1)} %get-tuple-element.368), channel_id=1, source_target_pairs={{0,16},{16,32},{32,48},{48,0},{1,17},{17,33},{33,49},{49,1},{2,18}... | collective-permute-start | bytes 73736 | tf_op jit(solution)/shard_map/while/body/eval_jaxpr/cond/branch_0_fun/ppermute | solution.py:382
  47.5 8.8 %collective-permute-start.4 = (f32[48,32]{1,0:T(8,128)S(1)}, f32[48,32]{1,0:T(8,128)S(1)}, u32[]{:S(2)}, u32[]{:S(2)}) collective-permute-start(f32[48,32]{1,0:T(8,128)S(1)} %get-tuple-element.490), channel_id=1, source_target_pairs={{0,1},{1,2},{2,3},{3,4},{4,5},{5,6},{6,7},{7,8},{8,9},{9,10},{10,1... | collective-permute-start | bytes 18440 | tf_op jit(solution)/shard_map/while/body/eval_jaxpr/ppermute | solution.py:382
  50.0 6.4 %collective-permute-start.5 = (f32[48,32]{1,0:T(8,128)S(1)}, f32[48,32]{1,0:T(8,128)S(1)}, u32[]{:S(2)}, u32[]{:S(2)}) collective-permute-start(f32[48,32]{1,0:T(8,128)S(1)} %get-tuple-element.491), channel_id=1, source_target_pairs={{0,15},{1,0},{2,1},{3,2},{4,3},{5,4},{6,5},{7,6},{8,7},{9,8},{10,9... | collective-permute-start | bytes 18440 | tf_op jit(solution)/shard_map/while/body/eval_jaxpr/ppermute | solution.py:382
  62.5 6.7 %collective-permute-start.6 = (f32[48,32]{1,0:T(8,128)S(1)}, f32[48,32]{1,0:T(8,128)S(1)}, u32[]{:S(2)}, u32[]{:S(2)}) collective-permute-start(f32[48,32]{1,0:T(8,128)S(1)} %get-tuple-element.498), channel_id=1, source_target_pairs={{0,15},{1,0},{2,1},{3,2},{4,3},{5,4},{6,5},{7,6},{8,7},{9,8},{10,9... | collective-permute-start | bytes 18440 | tf_op jit(solution)/shard_map/while/body/eval_jaxpr/ppermute | solution.py:382
  65.5 3.8 %collective-permute-start.7 = (f32[48,32]{1,0:T(8,128)S(1)}, f32[48,32]{1,0:T(8,128)S(1)}, u32[]{:S(2)}, u32[]{:S(2)}) collective-permute-start(f32[48,32]{1,0:T(8,128)S(1)} %get-tuple-element.499), channel_id=1, source_target_pairs={{0,1},{1,2},{2,3},{3,4},{4,5},{5,6},{6,7},{7,8},{8,9},{9,10},{10,1... | collective-permute-start | bytes 18440 | tf_op jit(solution)/shard_map/while/body/eval_jaxpr/ppermute | solution.py:382
  70.2 11.0 %copy-start.2 = (f32[3,4,4,128]{3,2,1,0:T(4,128)S(1)}, f32[3,4,4,128]{3,2,1,0:T(4,128)}, u32[]{:S(2)}) copy-start(f32[3,4,4,128]{3,2,1,0:T(4,128)} %get-tuple-element.233) | copy-start | bytes 73732
  71.0 10.2 %collective-permute-start.13 = (f32[3,1,4,128]{3,2,1,0:T(4,128)S(1)}, f32[3,1,4,128]{3,2,1,0:T(4,128)S(1)}, u32[]{:S(2)}, u32[]{:S(2)}) collective-permute-start(f32[3,1,4,128]{3,2,1,0:T(4,128)S(1)} %get-tuple-element.385), channel_id=1, source_target_pairs={{0,192},{64,0},{128,64},{192,128},{1,193},{65,1},{129,65},{193,129... | collective-permute-start | bytes 18440 | tf_op jit(solution)/shard_map/ppermute | solution.py:382
  71.0 10.2 %collective-permute-start.12 = (f32[3,1,4,128]{3,2,1,0:T(4,128)S(1)}, f32[3,1,4,128]{3,2,1,0:T(4,128)S(1)}, u32[]{:S(2)}, u32[]{:S(2)}) collective-permute-start(f32[3,1,4,128]{3,2,1,0:T(4,128)S(1)} %get-tuple-element.384), channel_id=1, source_target_pairs={{0,64},{64,128},{128,192},{192,0},{1,65},{65,129},{129,193},{193,1... | collective-permute-start | bytes 18440 | tf_op jit(solution)/shard_map/ppermute | solution.py:382
  72.4 15.8 %all-to-all-start = ((f32[16,1,128]{2,1,0:T(1,128)}), f32[16,1,128]{2,1,0:T(1,128)S(1)}, u32[]{:S(2)}, u32[]{:S(2)}) async-start(f32[16,1,128]{2,1,0:T(1,128)} %bitcast.4), calls=%async_computation | async-start | bytes 16384 | tf_op jit(solution)/shard_map/all_to_all | solution.py:455
  81.2 7.0 %copy-start.3 = (f32[3,2,4,128]{3,2,1,0:T(4,128)}, f32[3,2,4,128]{3,2,1,0:T(4,128)S(1)}, u32[]{:S(2)}) copy-start(f32[3,2,4,128]{3,2,1,0:T(4,128)S(1)} %maximum_add_fusion.3.x_ref) | copy-start | bytes 36868
  81.2 3.8 %collective-permute-start.14 = (f32[3,2,1,128]{3,2,1,0:T(1,128)S(1)}, f32[3,2,1,128]{3,2,1,0:T(1,128)S(1)}, u32[]{:S(2)}, u32[]{:S(2)}) collective-permute-start(f32[3,2,1,128]{3,2,1,0:T(1,128)S(1)} %get-tuple-element.389), channel_id=1, source_target_pairs={{0,16},{16,32},{32,48},{48,0},{1,17},{17,33},{33,49},{49,1},{2,18}... | collective-permute-start | bytes 9224 | tf_op jit(solution)/shard_map/ppermute | solution.py:382
  81.3 3.7 %collective-permute-start.15 = (f32[3,2,1,128]{3,2,1,0:T(1,128)S(1)}, f32[3,2,1,128]{3,2,1,0:T(1,128)S(1)}, u32[]{:S(2)}, u32[]{:S(2)}) collective-permute-start(f32[3,2,1,128]{3,2,1,0:T(1,128)S(1)} %get-tuple-element.388), channel_id=1, source_target_pairs={{0,48},{16,0},{32,16},{48,32},{1,49},{17,1},{33,17},{49,33},{2,50}... | collective-permute-start | bytes 9224 | tf_op jit(solution)/shard_map/ppermute | solution.py:382
  85.0 3.2 %copy-start.8 = (f32[3,2,1,128]{3,2,1,0:T(1,128)}, f32[3,2,1,128]{3,2,1,0:T(1,128)S(1)}, u32[]{:S(2)}) copy-start(f32[3,2,1,128]{3,2,1,0:T(1,128)S(1)} %collective-permute-done.14.below_ref) | copy-start | bytes 9220
  85.0 3.2 %copy-start.9 = (f32[3,2,1,128]{3,2,1,0:T(1,128)}, f32[3,2,1,128]{3,2,1,0:T(1,128)S(1)}, u32[]{:S(2)}) copy-start(f32[3,2,1,128]{3,2,1,0:T(1,128)S(1)} %collective-permute-done.15.above_ref) | copy-start | bytes 9220
  (2 other events, 1.2 us)

commit v2 on v1

--- a/solution.py
+++ b/solution.py
@@ -320,23 +320,39 @@
     )(*args)
 
 
+def lanes_below(count_ref, cx, cy):
+    lane = lax.broadcasted_iota(jnp.int32, (1, 128), 1)
+    limit = jnp.zeros((1, 128), jnp.int32)
+    for cz in range(4):
+        limit = jnp.where(lane // 32 == cz, count_ref[cx, cy, cz], limit)
+    return lane % 32 < limit
+
+
+def begin_kernel(
+    positions_ref, velocities_ref, forces_ref, count_ref, low_ref, high_ref, coords_ref
+):
+    speed = velocities_ref[...] + 0.5 * TIME_STEP * forces_ref[...]
+    coords = positions_ref[...] + TIME_STEP * speed
+    coords_ref[...] = coords + TIME_STEP * speed
+    for cx, first_ref in enumerate((low_ref, high_ref)):
+        first_ref[3:6, 0] = speed[:, cx]
+        for cy in range(2):
+            occupied = lanes_below(count_ref, cx, cy)
+            for a in range(3):
+                first_ref[a, 0, cy : cy + 1, :] = jnp.where(
+                    occupied, coords[a, cx, cy : cy + 1, :], UNOCCUPIED
+                )
+
+
 def finish_kernel(
-    arrived_ref, x_ref, below_ref, above_ref, pace_ref, place_ref, drift_ref, count_ref, *outs
+    source_ref, x_ref, below_ref, above_ref, pace_ref, place_ref, drift_ref, count_ref, *outs
 ):
-    coords_ref, speed_ref, force_ref, rows_ref = outs
-    lane = lax.broadcasted_iota(jnp.int32, (1, 128), 1)
-    for row in range(4):
-        line = arrived_ref[4 * row : 4 * row + 1, :]
-        for part in range(1, 4):
-            moved = pltpu.roll(arrived_ref[4 * row + part : 4 * row + part + 1, :], 32 * part, 1)
-            line = jnp.where(lane // 32 == part, moved, line)
-        rows_ref[row : row + 1, :] = line
+    coords_ref, speed_ref, force_ref, rows_ref, arrived_ref, semaphore = outs
+    copy = pltpu.make_async_copy(source_ref, arrived_ref, semaphore)
+    copy.start()
     for cx in range(2):
         for cy in range(2):
-            limit = jnp.zeros((1, 128), jnp.int32)
-            for cz in range(4):
-                limit = jnp.where(lane // 32 == cz, count_ref[cx, cy, cz], limit)
-            occupied = lane % 32 < limit
+            occupied = lanes_below(count_ref, cx, cy)
             for a in range(3):
                 beside = below_ref if cy == 0 else above_ref
                 force = x_ref[a, cx, cy + 1 : cy + 2, :] + beside[a, cx]
@@ -346,8 +362,16 @@
                 coords_ref[a, cx, cy : cy + 1, :] = jnp.where(
                     occupied,
                     place_ref[a, cx + 1, cy + 1 : cy + 2, :],
-                    drift_ref[a, cx, cy : cy + 1, :] + TIME_STEP * speed,
+                    drift_ref[a, cx, cy : cy + 1, :],
                 )
+    copy.wait()
+    lane = lax.broadcasted_iota(jnp.int32, (1, 128), 1)
+    for row in range(4):
+        line = arrived_ref[4 * row : 4 * row + 1, :]
+        for part in range(1, 4):
+            moved = pltpu.roll(arrived_ref[4 * row + part : 4 * row + part + 1, :], 32 * part, 1)
+            line = jnp.where(lane // 32 == part, moved, line)
+        rows_ref[row : row + 1, :] = line
 
 
 def prepare_weights(w_radial, w_env, w_latent, w_out):
@@ -396,11 +420,6 @@
 def share(padded, axis, dim):
     below, above = both_ways(padded, axis, dim, (0, 2), (2, 4))
     return padded + jnp.concatenate([below, above], axis=dim)
-
-
-def fold(padded, axis, dim):
-    below, above = both_ways(padded, axis, dim, (0, 1), (3, 4))
-    return lax.slice_in_dim(padded, 1, 3, axis=dim) + jnp.concatenate([below, above], axis=dim)
 
 
 def on_device(
@@ -418,17 +437,27 @@
     weights = prepare_weights(w_radial, w_env, w_latent, w_out)
     key = neighbour_keys(neighbours)
     listed = jnp.pad(send_list.reshape(16, 32), ((0, 0), (0, 96)))
-    occupied = jnp.arange(32, dtype=jnp.int32).reshape(1, 1, 1, 32) < counts[:, :, :, None]
-    occupied = occupied.reshape(1, 2, 2, 128)
-    half, quarter = TIME_STEP, 0.5 * TIME_STEP
-    speed = velocities + quarter * forces_in
-    coords = positions + half * speed
+    half = TIME_STEP
+    own = jax.ShapeDtypeStruct((3, 2, 2, 128), F32)
+    vmem, smem = (pl.BlockSpec(memory_space=space) for space in (pltpu.VMEM, pltpu.SMEM))
+    face = jax.ShapeDtypeStruct((6, 1, 2, 128), F32)
+    low, high, drift = pl.pallas_call(
+        begin_kernel,
+        out_shape=(face, face, own),
+        in_specs=[vmem] * 3 + [smem],
+        name="begin",
+    )(positions, velocities, forces_in, counts)
+    first = jnp.concatenate([shifted(high, "gx", 1), low, high, shifted(low, "gx", -1)], axis=1)
+    first = with_halo(first, "gy", 2)
 
     def one_step(repeat, carry):
-        wide_coords, wide_speed, change = carry
-        change = lax.cond(
-            repeat == 0, lambda part: part, lambda part: share(share(part, "gx", 1), "gy", 2), change
-        )
+        wide_coords, wide_speed, force = carry[0:3]
+
+        def from_force(part):
+            part = share(share(part, "gx", 1), "gy", 2)
+            return jnp.concatenate([half * half * part, half * part], axis=0)
+
+        change = lax.cond(repeat == 0, lambda part: first, from_force, force)
         wide_coords = wide_coords + half * wide_speed + change[0:3]
         wide_speed = wide_speed + change[3:6]
         flat = wide_coords.reshape(48, 128)
@@ -442,27 +471,23 @@
         )
         edges = jnp.concatenate([from_below, jnp.zeros((48, 64), F32), from_above], axis=1)
         force = (spread + edges).reshape(3, 4, 4, 128)
-        change = jnp.concatenate([half * half * force, half * force], axis=0)
-        return (wide_coords, wide_speed, change, force, sent)
-
-    first = jnp.concatenate([jnp.where(occupied, coords, UNOCCUPIED), speed], axis=0)
-    first = with_halo(with_halo(first, "gx", 1), "gy", 2)
+        return (wide_coords, wide_speed, force, force[:, 0:1], force[:, 3:4], sent)
+
     zero = jnp.zeros((3, 4, 4, 128), F32)
-    carry = (zero, zero, first, zero, jnp.zeros((16, 128), F32))
-    wide_coords, wide_speed, _, force, sent = lax.fori_loop(
-        0, STEPS, lambda repeat, carry: one_step(repeat, carry[0:3]), carry
+    carry = (zero, zero, zero, zero[:, 0:1], zero[:, 0:1], jnp.zeros((16, 128), F32))
+    wide_coords, wide_speed, force, low, high, sent = lax.fori_loop(0, STEPS, one_step, carry)
+    work_energy = lax.all_to_all(sent, "gz", split_axis=0, concat_axis=0, tiled=True)
+    force = force[:, 1:3] + jnp.concatenate(
+        [shifted(high, "gx", 1), shifted(low, "gx", -1)], axis=1
     )
-    work_energy = lax.all_to_all(sent, "gz", split_axis=0, concat_axis=0, tiled=True)
-    force = fold(force, "gx", 1)
     below, above = both_ways(force, "gy", 2, (0, 1), (3, 4))
-    own = jax.ShapeDtypeStruct((3, 2, 2, 128), F32)
-    specs = [pl.BlockSpec(memory_space=pltpu.VMEM)] * 7 + [pl.BlockSpec(memory_space=pltpu.SMEM)]
     *moved, rows = pl.pallas_call(
         finish_kernel,
         out_shape=(own, own, own, jax.ShapeDtypeStruct((4, 128), F32)),
-        in_specs=specs,
+        in_specs=[pl.BlockSpec(memory_space=pltpu.HBM)] + [vmem] * 6 + [smem],
+        scratch_shapes=[pltpu.VMEM((16, 128), F32), pltpu.SemaphoreType.DMA(())],
         name="finish",
-    )(work_energy, force, below, above, wide_speed, wide_coords, coords, counts)
+    )(work_energy, force, below, above, wide_speed, wide_coords, drift, counts)
     return (*moved, rows.reshape(1, 1, 512))
 
 

time: 90.6 us -> 90.3 us (level)
  Pallas kernels: 27.7 us -> 30 us
  other arithmetic: 3.74 us -> 2.32 us
    pallas_call x0 -> x1, Pallas kernels: none -> 1.44 us  [on_device(): pl.pallas_call(begin_kernel, out_shape=(face, face, own), in_specs=[vmem]...]
    unnamed x27 -> x30, local copies, waits for them, and re-layouts: 2.2 us -> 3.57 us
    select_n x1 -> x0, other arithmetic: 1.33 us -> none  [on_device(): jnp.where(occupied, coords, UNOCCUPIED)]
    slice x0 -> x2, local copies, waits for them, and re-layouts: none -> 1.21 us  [one_step(): return (wide_coords, wide_speed, force, force[:, 0:1], force[:, 3:4], sent)]
    while x4 -> x0, local copies, waits for them, and re-layouts: 1.16 us -> none
    lt x4 -> x0, local copies, waits for them, and re-layouts: 0.94 us -> none  [on_device(): jnp.arange(32, dtype=jnp.int32).reshape(1, 1, 1, 32) < counts[:, :, :, None]]
  transfers between devices with their start and end apart: 21 -> 21, of which waited for: 8 -> 7; matrix products, arithmetic and copies ran while one was open for 4% -> 5% of each run, Pallas kernels for 16% -> 16%
where the time goes in v2:
time: 90.3 us; the launch traced here: 89.8 us
  starting transfers between devices  36.6 us (41%)
  Pallas kernels  30 us (33%)
  waiting for transfers between devices  12.7 us (14%)
  local copies, waits for them, and re-layouts  6.73 us (7%)
  other arithmetic  2.32 us (3%)
  between operations  1.07 us (1%)
    ppermute x20, starting transfers between devices, shifted(): lax.ppermute(array, axis, [(i, (i + step) % peers) for i in range(peers)])  27.9 us
    pallas_call x6, Pallas kernels, force_call(): pl.pallas_call(functools.partial(force_kernel, blocks, layers, first, las...  26.4 us
    ppermute x20, waiting for transfers between devices, shifted(): lax.ppermute(array, axis, [(i, (i + step) % peers) for i in range(peers)])  9.71 us
    all_to_all x1, starting transfers between devices, on_device(): lax.all_to_all(sent, 'gz', split_axis=0, concat_axis=0, tiled=True)  8.67 us
    unnamed x30, local copies, waits for them, and re-layouts  3.57 us
    all_to_all x1, waiting for transfers between devices, on_device(): lax.all_to_all(sent, 'gz', split_axis=0, concat_axis=0, tiled=True)  2.97 us
    pallas_call x1, Pallas kernels, on_device(): pl.pallas_call(finish_kernel, out_shape=(own, own, own, jax.ShapeDtypeStr...  2.19 us
  transfers between devices with their start and end apart: 21, of which 7 were waited for; matrix products, arithmetic and copies ran while one was open for 5% of the time, Pallas kernels for 16%

profile of v2, /device:TPU:1, one launch (start us, length us, event | category | flops | bytes accessed | tf_op | source)
XLA Modules:
  0.0 89.8 jit_solution(12581230289639931409)
XLA Ops:
  0.6 1.4 %begin.1 = (f32[6,1,2,128]{3,2,1,0:T(2,128)}, f32[6,1,2,128]{3,2,1,0:T(2,128)}, f32[3,2,2,128]{3,2,1,0:T(2,128)}) custom-call(f32[3,2,2,128]{3,2,1,0:T(2,128)} %positions_ref.1, f32[3,2,2,128]{3,2,1,0:T(2,128)} %velocities_ref.1, f32[3,2,2,128]{3,2,1,0:T(2,128)} %forces_ref.1, s32[2,2,4]{2,1,0:T(2,128)} %count_ref.3), custom_call_target="tpu_custom_call" | custom-call | tf_op jit(solution)/shard_map/begin/pallas_call | solution.py:444
  2.1 2.0 %collective-permute-start.8 = (f32[6,1,2,128]{3,2,1,0:T(2,128)}, f32[6,1,2,128]{3,2,1,0:T(2,128)S(1)}, u32[]{:S(2)}, u32[]{:S(2)}) collective-permute-start(f32[6,1,2,128]{3,2,1,0:T(2,128)} %get-tuple-element.262), channel_id=1, source_target_pairs={{0,64},{64,128},{128,192},{192,0},{1,65},{65,129},{129,193},{193,1... | collective-permute-start | bytes 18440 | tf_op jit(solution)/shard_map/ppermute | solution.py:406
  4.1 1.3 %collective-permute-start.9 = (f32[6,1,2,128]{3,2,1,0:T(2,128)}, f32[6,1,2,128]{3,2,1,0:T(2,128)S(1)}, u32[]{:S(2)}, u32[]{:S(2)}) collective-permute-start(f32[6,1,2,128]{3,2,1,0:T(2,128)} %get-tuple-element.263), channel_id=1, source_target_pairs={{0,192},{64,0},{128,64},{192,128},{1,193},{65,1},{129,65},{193,129... | collective-permute-start | bytes 18440 | tf_op jit(solution)/shard_map/ppermute | solution.py:406
  5.4 1.0 %reshape.36 = s32[4,6,2,2,4,32]{5,4,3,2,1,0:T(4,128)S(1)} reshape(s32[24,2,2,128]{3,2,1,0:T(2,128)} %param.18) | data formatting | bytes 98304 | tf_op jit(solution)/shard_map/reshape | solution.py:392
  6.4 1.2 %fusion.6 = s32[2,2,4,6,4,32]{5,4,2,3,1,0:T(4,128)S(1)} fusion(s32[4,6,2,2,4,32]{5,4,3,2,1,0:T(4,128)S(1)} %reshape.36), kind=kLoop, calls=%fused_computation.23 | loop fusion | flops 638976 | bytes 98304 | tf_op jit(solution)/shard_map/transpose | solution.py:400
  9.4 3.0 %collective-permute-start.11 = (f32[6,4,1,128]{3,2,1,0:T(1,128)S(1)}, f32[6,4,1,128]{3,2,1,0:T(1,128)S(1)}, u32[]{:S(2)}, u32[]{:S(2)}) collective-permute-start(f32[6,4,1,128]{3,2,1,0:T(1,128)S(1)} %get-tuple-element.434), channel_id=1, source_target_pairs={{0,48},{16,0},{32,16},{48,32},{1,49},{17,1},{33,17},{49,33},{2,50}... | collective-permute-start | bytes 36872 | tf_op jit(solution)/shard_map/ppermute | solution.py:406
  15.0 1.2 %collective-permute-done.10 = f32[6,4,1,128]{3,2,1,0:T(1,128)S(1)} collective-permute-done((f32[6,4,1,128]{3,2,1,0:T(1,128)S(1)}, f32[6,4,1,128]{3,2,1,0:T(1,128)S(1)}, u32[]{:S(2)}, u32[]{:S(2)}) %collective-permute-start.10) | collective-permute-done | bytes 12320 | tf_op jit(solution)/shard_map/ppermute | solution.py:406
  16.2 53.5 %while.27 = (s32[]{:T(128)}, f32[3,4,4,128]{3,2,1,0:T(4,128)S(1)}, f32[3,4,4,128]{3,2,1,0:T(4,128)S(1)}, f32[3,4,4,128]{3,2,1,0:T(4,128)S(1)}, f32[3,1,4,128]{3,...) while((s32[]{:T(128)}, f32[3,4,4,128]{3,2,1,0:T(4,128)S(1)}, ...), condition=%wide.region_3.4_spmd.clone, body=%wide.region_0.3_spmd.clone.sunk | while | flops 12800104448 | bytes 1979828 | solution.py:478
  16.6 4.2 %collective-permute-start.4 = (f32[48,32]{1,0:T(8,128)S(1)}, f32[48,32]{1,0:T(8,128)S(1)}, u32[]{:S(2)}, u32[]{:S(2)}) collective-permute-start(f32[48,32]{1,0:T(8,128)S(1)} %get-tuple-element.545), channel_id=1, source_target_pairs={{0,1},{1,2},{2,3},{3,4},{4,5},{5,6},{6,7},{7,8},{8,9},{9,10},{10,1... | collective-permute-start | bytes 18440 | tf_op jit(solution)/shard_map/while/body/eval_jaxpr/ppermute | solution.py:406
  20.9 3.3 %force.15 = (f32[48,128]{1,0:T(8,128)S(1)}, f32[8,128]{1,0:T(8,128)S(1)}) custom-call(f32[48,128]{1,0:T(8,128)S(1)} %bitcast.21, s32[4,4,8,128]{3,2,1,0:T(8,128)S(1)} %get-tuple-element.606.refs_1_, bf16[256,64]{1,0:T(8,128)(2,1)S(1)} %get-tuple-element.607.refs_2_, bf16[128,128]{1,0:T(8,128)(2,1)S(1)} %get-tuple-element.608.refs_3_, ...), custom_call_target="tpu_custom_call" | custom-call | flops 3200000000 | bytes 300000 | tf_op jit(solution)/shard_map/while/body/eval_jaxpr/force/pallas_call | solution.py:303
  24.3 6.1 %force.16 = (f32[48,128]{1,0:T(8,128)S(1)}, f32[8,128]{1,0:T(8,128)S(1)}, f32[48,128]{1,0:T(8,128)S(1)}) custom-call(f32[48,128]{1,0:T(8,128)S(1)} %bitcast.22, s32[4,4,8,128]{3,2,1,0:T(8,128)S(1)} %get-tuple-element.606.refs_1_, bf16[256,64]{1,0:T(8,128)(2,1)S(1)} %get-tuple-element.607.refs_2_, bf16[128,128]{1,0:T(8,128)(2,1)S(1)} %get-tuple-element.608.refs_3_, ...), custom_call_target="tpu_custom_call" | custom-call | flops 6400000000 | bytes 300000 | tf_op jit(solution)/shard_map/while/body/eval_jaxpr/force/pallas_call | solution.py:303
  30.5 1.8 %collective-permute-start.6 = (f32[48,32]{1,0:T(8,128)S(1)}, f32[48,32]{1,0:T(8,128)S(1)}, u32[]{:S(2)}, u32[]{:S(2)}) collective-permute-start(f32[48,32]{1,0:T(8,128)S(1)} %get-tuple-element.553), channel_id=1, source_target_pairs={{0,15},{1,0},{2,1},{3,2},{4,3},{5,4},{6,5},{7,6},{8,7},{9,8},{10,9... | collective-permute-start | bytes 18440 | tf_op jit(solution)/shard_map/while/body/eval_jaxpr/ppermute | solution.py:406
  32.3 3.8 %force.17 = (f32[48,128]{1,0:T(8,128)S(1)}, f32[16,128]{1,0:T(8,128)}) custom-call(f32[48,128]{1,0:T(8,128)S(1)} %bitcast.23, s32[4,4,8,128]{3,2,1,0:T(8,128)S(1)} %get-tuple-element.606.refs_1_, bf16[256,64]{1,0:T(8,128)(2,1)S(1)} %get-tuple-element.607.refs_2_, bf16[128,128]{1,0:T(8,128)(2,1)S(1)} %get-tuple-element.608.refs_3_, ...), custom_call_target="tpu_custom_call" | custom-call | flops 3200000000 | bytes 300000 | tf_op jit(solution)/shard_map/while/body/eval_jaxpr/force/pallas_call | solution.py:303
  36.7 10.4 %conditional.3 = (f32[6,4,4,128]{3,2,1,0:T(4,128)S(1)}) conditional(s32[]{:T(128)} %convert_element_type.50, f32[3,4,4,128]{3,2,1,0:T(4,128)S(1)} %get-tuple-element.581, f32[6,4,4,128]{3,2,1,0:T(4,128)S(1)} %get-tuple-element.605), branch_computations={%region_1.1_spmd, %region_2.2_spmd} | conditional | flops 49152 | bytes 565416 | solution.py:460
  36.7 1.3 %collective-permute-start.1 = (f32[3,2,4,128]{3,2,1,0:T(4,128)S(1)}, f32[3,2,4,128]{3,2,1,0:T(4,128)S(1)}, u32[]{:S(2)}, u32[]{:S(2)}) collective-permute-start(f32[3,2,4,128]{3,2,1,0:T(4,128)S(1)} %get-tuple-element.420), channel_id=1, source_target_pairs={{0,192},{64,0},{128,64},{192,128},{1,193},{65,1},{129,65},{193,129... | collective-permute-start | bytes 36872 | tf_op jit(solution)/shard_map/while/body/eval_jaxpr/cond/branch_0_fun/ppermute | solution.py:406
  38.2 1.1 %collective-permute-done.1 = f32[3,2,4,128]{3,2,1,0:T(4,128)S(1)} collective-permute-done((f32[3,2,4,128]{3,2,1,0:T(4,128)S(1)}, f32[3,2,4,128]{3,2,1,0:T(4,128)S(1)}, u32[]{:S(2)}, u32[]{:S(2)}) %collective-permute-start.1) | collective-permute-done | bytes 12320 | tf_op jit(solution)/shard_map/while/body/eval_jaxpr/cond/branch_0_fun/ppermute | solution.py:406
  39.3 2.5 %collective-permute-done = f32[3,2,4,128]{3,2,1,0:T(4,128)S(1)} collective-permute-done((f32[3,2,4,128]{3,2,1,0:T(4,128)S(1)}, f32[3,2,4,128]{3,2,1,0:T(4,128)S(1)}, u32[]{:S(2)}, u32[]{:S(2)}) %collective-permute-start) | collective-permute-done | bytes 12320 | tf_op jit(solution)/shard_map/while/body/eval_jaxpr/cond/branch_0_fun/ppermute | solution.py:406
  41.8 1.6 %collective-permute-start.3 = (f32[3,4,2,128]{3,2,1,0:T(2,128)S(1)}, f32[3,4,2,128]{3,2,1,0:T(2,128)S(1)}, u32[]{:S(2)}, u32[]{:S(2)}) collective-permute-start(f32[3,4,2,128]{3,2,1,0:T(2,128)S(1)} %get-tuple-element.418), channel_id=1, source_target_pairs={{0,48},{16,0},{32,16},{48,32},{1,49},{17,1},{33,17},{49,33},{2,50}... | collective-permute-start | bytes 36872 | tf_op jit(solution)/shard_map/while/body/eval_jaxpr/cond/branch_0_fun/ppermute | solution.py:406
  43.3 1.1 %collective-permute-done.3 = f32[3,4,2,128]{3,2,1,0:T(2,128)S(1)} collective-permute-done((f32[3,4,2,128]{3,2,1,0:T(2,128)S(1)}, f32[3,4,2,128]{3,2,1,0:T(2,128)S(1)}, u32[]{:S(2)}, u32[]{:S(2)}) %collective-permute-start.3) | collective-permute-done | bytes 12320 | tf_op jit(solution)/shard_map/while/body/eval_jaxpr/cond/branch_0_fun/ppermute | solution.py:406
  44.4 2.7 %collective-permute-done.2 = f32[3,4,2,128]{3,2,1,0:T(2,128)S(1)} collective-permute-done((f32[3,4,2,128]{3,2,1,0:T(2,128)S(1)}, f32[3,4,2,128]{3,2,1,0:T(2,128)S(1)}, u32[]{:S(2)}, u32[]{:S(2)}) %collective-permute-start.2) | collective-permute-done | bytes 12320 | tf_op jit(solution)/shard_map/while/body/eval_jaxpr/cond/branch_0_fun/ppermute | solution.py:406
  47.3 2.5 %collective-permute-start.4 = (f32[48,32]{1,0:T(8,128)S(1)}, f32[48,32]{1,0:T(8,128)S(1)}, u32[]{:S(2)}, u32[]{:S(2)}) collective-permute-start(f32[48,32]{1,0:T(8,128)S(1)} %get-tuple-element.545), channel_id=1, source_target_pairs={{0,1},{1,2},{2,3},{3,4},{4,5},{5,6},{6,7},{7,8},{8,9},{9,10},{10,1... | collective-permute-start | bytes 18440 | tf_op jit(solution)/shard_map/while/body/eval_jaxpr/ppermute | solution.py:406
  49.7 2.9 %collective-permute-start.5 = (f32[48,32]{1,0:T(8,128)S(1)}, f32[48,32]{1,0:T(8,128)S(1)}, u32[]{:S(2)}, u32[]{:S(2)}) collective-permute-start(f32[48,32]{1,0:T(8,128)S(1)} %get-tuple-element.546), channel_id=1, source_target_pairs={{0,15},{1,0},{2,1},{3,2},{4,3},{5,4},{6,5},{7,6},{8,7},{9,8},{10,9... | collective-permute-start | bytes 18440 | tf_op jit(solution)/shard_map/while/body/eval_jaxpr/ppermute | solution.py:406
  52.7 3.3 %force.15 = (f32[48,128]{1,0:T(8,128)S(1)}, f32[8,128]{1,0:T(8,128)S(1)}) custom-call(f32[48,128]{1,0:T(8,128)S(1)} %bitcast.21, s32[4,4,8,128]{3,2,1,0:T(8,128)S(1)} %get-tuple-element.606.refs_1_, bf16[256,64]{1,0:T(8,128)(2,1)S(1)} %get-tuple-element.607.refs_2_, bf16[128,128]{1,0:T(8,128)(2,1)S(1)} %get-tuple-element.608.refs_3_, ...), custom_call_target="tpu_custom_call" | custom-call | flops 3200000000 | bytes 300000 | tf_op jit(solution)/shard_map/while/body/eval_jaxpr/force/pallas_call | solution.py:303
  56.1 6.1 %force.16 = (f32[48,128]{1,0:T(8,128)S(1)}, f32[8,128]{1,0:T(8,128)S(1)}, f32[48,128]{1,0:T(8,128)S(1)}) custom-call(f32[48,128]{1,0:T(8,128)S(1)} %bitcast.22, s32[4,4,8,128]{3,2,1,0:T(8,128)S(1)} %get-tuple-element.606.refs_1_, bf16[256,64]{1,0:T(8,128)(2,1)S(1)} %get-tuple-element.607.refs_2_, bf16[128,128]{1,0:T(8,128)(2,1)S(1)} %get-tuple-element.608.refs_3_, ...), custom_call_target="tpu_custom_call" | custom-call | flops 6400000000 | bytes 300000 | tf_op jit(solution)/shard_map/while/body/eval_jaxpr/force/pallas_call | solution.py:303
  62.3 3.0 %collective-permute-start.6 = (f32[48,32]{1,0:T(8,128)S(1)}, f32[48,32]{1,0:T(8,128)S(1)}, u32[]{:S(2)}, u32[]{:S(2)}) collective-permute-start(f32[48,32]{1,0:T(8,128)S(1)} %get-tuple-element.553), channel_id=1, source_target_pairs={{0,15},{1,0},{2,1},{3,2},{4,3},{5,4},{6,5},{7,6},{8,7},{9,8},{10,9... | collective-permute-start | bytes 18440 | tf_op jit(solution)/shard_map/while/body/eval_jaxpr/ppermute | solution.py:406
  65.3 3.8 %force.17 = (f32[48,128]{1,0:T(8,128)S(1)}, f32[16,128]{1,0:T(8,128)}) custom-call(f32[48,128]{1,0:T(8,128)S(1)} %bitcast.23, s32[4,4,8,128]{3,2,1,0:T(8,128)S(1)} %get-tuple-element.606.refs_1_, bf16[256,64]{1,0:T(8,128)(2,1)S(1)} %get-tuple-element.607.refs_2_, bf16[128,128]{1,0:T(8,128)(2,1)S(1)} %get-tuple-element.608.refs_3_, ...), custom_call_target="tpu_custom_call" | custom-call | flops 3200000000 | bytes 300000 | tf_op jit(solution)/shard_map/while/body/eval_jaxpr/force/pallas_call | solution.py:303
  69.7 1.5 %collective-permute-start.12 = (f32[3,1,4,128]{3,2,1,0:T(4,128)}, f32[3,1,4,128]{3,2,1,0:T(4,128)S(1)}, u32[]{:S(2)}, u32[]{:S(2)}) collective-permute-start(f32[3,1,4,128]{3,2,1,0:T(4,128)} %get-tuple-element.266), channel_id=1, source_target_pairs={{0,64},{64,128},{128,192},{192,0},{1,65},{65,129},{129,193},{193,1... | collective-permute-start | bytes 18440 | tf_op jit(solution)/shard_map/ppermute | solution.py:406
  71.2 8.7 %all-to-all-start = ((f32[16,1,128]{2,1,0:T(1,128)}), f32[16,1,128]{2,1,0:T(1,128)S(1)}, u32[]{:S(2)}, u32[]{:S(2)}) async-start(f32[16,1,128]{2,1,0:T(1,128)} %bitcast.27), calls=%async_computation | async-start | bytes 16384 | tf_op jit(solution)/shard_map/all_to_all | solution.py:479
  80.0 2.7 %collective-permute-start.15 = (f32[3,2,1,128]{3,2,1,0:T(1,128)S(1)}, f32[3,2,1,128]{3,2,1,0:T(1,128)S(1)}, u32[]{:S(2)}, u32[]{:S(2)}) collective-permute-start(f32[3,2,1,128]{3,2,1,0:T(1,128)S(1)} %get-tuple-element.435), channel_id=1, source_target_pairs={{0,48},{16,0},{32,16},{48,32},{1,49},{17,1},{33,17},{49,33},{2,50}... | collective-permute-start | bytes 9224 | tf_op jit(solution)/shard_map/ppermute | solution.py:406
  82.7 1.2 %collective-permute-done.14.below_ref = f32[3,2,1,128]{3,2,1,0:T(1,128)S(1)} collective-permute-done((f32[3,2,1,128]{3,2,1,0:T(1,128)S(1)}, f32[3,2,1,128]{3,2,1,0:T(1,128)S(1)}, u32[]{:S(2)}, u32[]{:S(2)}) %collective-permute-start.14) | collective-permute-done | bytes 3104 | tf_op jit(solution)/shard_map/ppermute | solution.py:406
  83.9 3.0 %all-to-all-done = f32[16,1,128]{2,1,0:T(1,128)S(1)} async-done(((f32[16,1,128]{2,1,0:T(1,128)}), f32[16,1,128]{2,1,0:T(1,128)S(1)}, u32[]{:S(2)}, u32[]{:S(2)}) %all-to-all-start) | async-done | bytes 8224 | tf_op jit(solution)/shard_map/all_to_all | solution.py:479
  87.5 2.2 %finish.1 = (f32[3,2,2,128]{3,2,1,0:T(2,128)}, f32[3,2,2,128]{3,2,1,0:T(2,128)}, f32[3,2,2,128]{3,2,1,0:T(2,128)}, f32[4,128]{1,0:T(4,128)}) custom-call(f32[16,128]{1,0:T(8,128)} %bitcast.26, f32[3,2,4,128]{3,2,1,0:T(4,128)} %copy-done.1, f32[3,2,1,128]{3,2,1,0:T(1,128)} %copy-done.7, f32[3,2,1,128]{3,2,1,0:T(1,128)} %copy-done.8, ...), custom_call_target="tpu_custom_call" | custom-call | tf_op jit(solution)/shard_map/finish/pallas_call | solution.py:484
  (99 shorter events, 7.4 us)
Async XLA Ops:
  0.6 7.0 %copy-start = (bf16[128,128]{1,0:T(8,128)(2,1)S(1)}, bf16[128,128]{1,0:T(8,128)(2,1)}, u32[]{:S(2)}) copy-start(bf16[128,128]{1,0:T(8,128)(2,1)} %param.21) | copy-start | bytes 98308
  2.1 5.9 %collective-permute-start.8 = (f32[6,1,2,128]{3,2,1,0:T(2,128)}, f32[6,1,2,128]{3,2,1,0:T(2,128)S(1)}, u32[]{:S(2)}, u32[]{:S(2)}) collective-permute-start(f32[6,1,2,128]{3,2,1,0:T(2,128)} %get-tuple-element.262), channel_id=1, source_target_pairs={{0,64},{64,128},{128,192},{192,0},{1,65},{65,129},{129,193},{193,1... | collective-permute-start | bytes 18440 | tf_op jit(solution)/shard_map/ppermute | solution.py:406
  4.1 5.3 %collective-permute-start.9 = (f32[6,1,2,128]{3,2,1,0:T(2,128)}, f32[6,1,2,128]{3,2,1,0:T(2,128)S(1)}, u32[]{:S(2)}, u32[]{:S(2)}) collective-permute-start(f32[6,1,2,128]{3,2,1,0:T(2,128)} %get-tuple-element.263), channel_id=1, source_target_pairs={{0,192},{64,0},{128,64},{192,128},{1,193},{65,1},{129,65},{193,129... | collective-permute-start | bytes 18440 | tf_op jit(solution)/shard_map/ppermute | solution.py:406
  6.4 1.3 %copy-start.6 = (f32[8,128]{1,0:T(8,128)S(1)}, f32[8,128]{1,0:T(8,128)}, u32[]{:S(2)}) copy-start(f32[8,128]{1,0:T(8,128)} %param.20) | copy-start | bytes 12292
  6.4 1.3 %copy-start.2 = (bf16[256,128]{1,0:T(8,128)(2,1)S(1)}, bf16[256,128]{1,0:T(8,128)(2,1)}, u32[]{:S(2)}) copy-start(bf16[256,128]{1,0:T(8,128)(2,1)} %param.22) | copy-start | bytes 196612
  8.0 0.7 copy-start.4
  8.7 0.7 copy-start.5
  9.4 5.6 %collective-permute-start.11 = (f32[6,4,1,128]{3,2,1,0:T(1,128)S(1)}, f32[6,4,1,128]{3,2,1,0:T(1,128)S(1)}, u32[]{:S(2)}, u32[]{:S(2)}) collective-permute-start(f32[6,4,1,128]{3,2,1,0:T(1,128)S(1)} %get-tuple-element.434), channel_id=1, source_target_pairs={{0,48},{16,0},{32,16},{48,32},{1,49},{17,1},{33,17},{49,33},{2,50}... | collective-permute-start | bytes 36872 | tf_op jit(solution)/shard_map/ppermute | solution.py:406
  12.4 3.8 %collective-permute-start.10 = (f32[6,4,1,128]{3,2,1,0:T(1,128)S(1)}, f32[6,4,1,128]{3,2,1,0:T(1,128)S(1)}, u32[]{:S(2)}, u32[]{:S(2)}) collective-permute-start(f32[6,4,1,128]{3,2,1,0:T(1,128)S(1)} %get-tuple-element.433), channel_id=1, source_target_pairs={{0,16},{16,32},{32,48},{48,0},{1,17},{17,33},{33,49},{49,1},{2,18}... | collective-permute-start | bytes 36872 | tf_op jit(solution)/shard_map/ppermute | solution.py:406
  12.9 0.7 copy-start.9
  14.3 0.7 copy-start.10
  16.6 7.7 %collective-permute-start.4 = (f32[48,32]{1,0:T(8,128)S(1)}, f32[48,32]{1,0:T(8,128)S(1)}, u32[]{:S(2)}, u32[]{:S(2)}) collective-permute-start(f32[48,32]{1,0:T(8,128)S(1)} %get-tuple-element.545), channel_id=1, source_target_pairs={{0,1},{1,2},{2,3},{3,4},{4,5},{5,6},{6,7},{7,8},{8,9},{9,10},{10,1... | collective-permute-start | bytes 18440 | tf_op jit(solution)/shard_map/while/body/eval_jaxpr/ppermute | solution.py:406
  20.8 3.5 %collective-permute-start.5 = (f32[48,32]{1,0:T(8,128)S(1)}, f32[48,32]{1,0:T(8,128)S(1)}, u32[]{:S(2)}, u32[]{:S(2)}) collective-permute-start(f32[48,32]{1,0:T(8,128)S(1)} %get-tuple-element.546), channel_id=1, source_target_pairs={{0,15},{1,0},{2,1},{3,2},{4,3},{5,4},{6,5},{7,6},{8,7},{9,8},{10,9... | collective-permute-start | bytes 18440 | tf_op jit(solution)/shard_map/while/body/eval_jaxpr/ppermute | solution.py:406
  30.5 5.6 %collective-permute-start.6 = (f32[48,32]{1,0:T(8,128)S(1)}, f32[48,32]{1,0:T(8,128)S(1)}, u32[]{:S(2)}, u32[]{:S(2)}) collective-permute-start(f32[48,32]{1,0:T(8,128)S(1)} %get-tuple-element.553), channel_id=1, source_target_pairs={{0,15},{1,0},{2,1},{3,2},{4,3},{5,4},{6,5},{7,6},{8,7},{9,8},{10,9... | collective-permute-start | bytes 18440 | tf_op jit(solution)/shard_map/while/body/eval_jaxpr/ppermute | solution.py:406
  32.3 3.8 %collective-permute-start.7 = (f32[48,32]{1,0:T(8,128)S(1)}, f32[48,32]{1,0:T(8,128)S(1)}, u32[]{:S(2)}, u32[]{:S(2)}) collective-permute-start(f32[48,32]{1,0:T(8,128)S(1)} %get-tuple-element.554), channel_id=1, source_target_pairs={{0,1},{1,2},{2,3},{3,4},{4,5},{5,6},{6,7},{7,8},{8,9},{9,10},{10,1... | collective-permute-start | bytes 18440 | tf_op jit(solution)/shard_map/while/body/eval_jaxpr/ppermute | solution.py:406
  36.7 2.5 %collective-permute-start.1 = (f32[3,2,4,128]{3,2,1,0:T(4,128)S(1)}, f32[3,2,4,128]{3,2,1,0:T(4,128)S(1)}, u32[]{:S(2)}, u32[]{:S(2)}) collective-permute-start(f32[3,2,4,128]{3,2,1,0:T(4,128)S(1)} %get-tuple-element.420), channel_id=1, source_target_pairs={{0,192},{64,0},{128,64},{192,128},{1,193},{65,1},{129,65},{193,129... | collective-permute-start | bytes 36872 | tf_op jit(solution)/shard_map/while/body/eval_jaxpr/cond/branch_0_fun/ppermute | solution.py:406
  38.0 3.8 %collective-permute-start = (f32[3,2,4,128]{3,2,1,0:T(4,128)S(1)}, f32[3,2,4,128]{3,2,1,0:T(4,128)S(1)}, u32[]{:S(2)}, u32[]{:S(2)}) collective-permute-start(f32[3,2,4,128]{3,2,1,0:T(4,128)S(1)} %get-tuple-element.419), channel_id=1, source_target_pairs={{0,64},{64,128},{128,192},{192,0},{1,65},{65,129},{129,193},{193,1... | collective-permute-start | bytes 36872 | tf_op jit(solution)/shard_map/while/body/eval_jaxpr/cond/branch_0_fun/ppermute | solution.py:406
  41.8 2.6 %collective-permute-start.3 = (f32[3,4,2,128]{3,2,1,0:T(2,128)S(1)}, f32[3,4,2,128]{3,2,1,0:T(2,128)S(1)}, u32[]{:S(2)}, u32[]{:S(2)}) collective-permute-start(f32[3,4,2,128]{3,2,1,0:T(2,128)S(1)} %get-tuple-element.418), channel_id=1, source_target_pairs={{0,48},{16,0},{32,16},{48,32},{1,49},{17,1},{33,17},{49,33},{2,50}... | collective-permute-start | bytes 36872 | tf_op jit(solution)/shard_map/while/body/eval_jaxpr/cond/branch_0_fun/ppermute | solution.py:406
  43.3 3.8 %collective-permute-start.2 = (f32[3,4,2,128]{3,2,1,0:T(2,128)S(1)}, f32[3,4,2,128]{3,2,1,0:T(2,128)S(1)}, u32[]{:S(2)}, u32[]{:S(2)}) collective-permute-start(f32[3,4,2,128]{3,2,1,0:T(2,128)S(1)} %get-tuple-element.417), channel_id=1, source_target_pairs={{0,16},{16,32},{32,48},{48,0},{1,17},{17,33},{33,49},{49,1},{2,18}... | collective-permute-start | bytes 36872 | tf_op jit(solution)/shard_map/while/body/eval_jaxpr/cond/branch_0_fun/ppermute | solution.py:406
  47.3 8.8 %collective-permute-start.4 = (f32[48,32]{1,0:T(8,128)S(1)}, f32[48,32]{1,0:T(8,128)S(1)}, u32[]{:S(2)}, u32[]{:S(2)}) collective-permute-start(f32[48,32]{1,0:T(8,128)S(1)} %get-tuple-element.545), channel_id=1, source_target_pairs={{0,1},{1,2},{2,3},{3,4},{4,5},{5,6},{6,7},{7,8},{8,9},{9,10},{10,1... | collective-permute-start | bytes 18440 | tf_op jit(solution)/shard_map/while/body/eval_jaxpr/ppermute | solution.py:406
  49.7 6.4 %collective-permute-start.5 = (f32[48,32]{1,0:T(8,128)S(1)}, f32[48,32]{1,0:T(8,128)S(1)}, u32[]{:S(2)}, u32[]{:S(2)}) collective-permute-start(f32[48,32]{1,0:T(8,128)S(1)} %get-tuple-element.546), channel_id=1, source_target_pairs={{0,15},{1,0},{2,1},{3,2},{4,3},{5,4},{6,5},{7,6},{8,7},{9,8},{10,9... | collective-permute-start | bytes 18440 | tf_op jit(solution)/shard_map/while/body/eval_jaxpr/ppermute | solution.py:406
  62.3 6.7 %collective-permute-start.6 = (f32[48,32]{1,0:T(8,128)S(1)}, f32[48,32]{1,0:T(8,128)S(1)}, u32[]{:S(2)}, u32[]{:S(2)}) collective-permute-start(f32[48,32]{1,0:T(8,128)S(1)} %get-tuple-element.553), channel_id=1, source_target_pairs={{0,15},{1,0},{2,1},{3,2},{4,3},{5,4},{6,5},{7,6},{8,7},{9,8},{10,9... | collective-permute-start | bytes 18440 | tf_op jit(solution)/shard_map/while/body/eval_jaxpr/ppermute | solution.py:406
  65.3 3.8 %collective-permute-start.7 = (f32[48,32]{1,0:T(8,128)S(1)}, f32[48,32]{1,0:T(8,128)S(1)}, u32[]{:S(2)}, u32[]{:S(2)}) collective-permute-start(f32[48,32]{1,0:T(8,128)S(1)} %get-tuple-element.554), channel_id=1, source_target_pairs={{0,1},{1,2},{2,3},{3,4},{4,5},{5,6},{6,7},{7,8},{8,9},{9,10},{10,1... | collective-permute-start | bytes 18440 | tf_op jit(solution)/shard_map/while/body/eval_jaxpr/ppermute | solution.py:406
  69.7 10.1 %collective-permute-start.13 = (f32[3,1,4,128]{3,2,1,0:T(4,128)}, f32[3,1,4,128]{3,2,1,0:T(4,128)S(1)}, u32[]{:S(2)}, u32[]{:S(2)}) collective-permute-start(f32[3,1,4,128]{3,2,1,0:T(4,128)} %get-tuple-element.267), channel_id=1, source_target_pairs={{0,192},{64,0},{128,64},{192,128},{1,193},{65,1},{129,65},{193,129... | collective-permute-start | bytes 18440 | tf_op jit(solution)/shard_map/ppermute | solution.py:406
  69.7 10.1 %collective-permute-start.12 = (f32[3,1,4,128]{3,2,1,0:T(4,128)}, f32[3,1,4,128]{3,2,1,0:T(4,128)S(1)}, u32[]{:S(2)}, u32[]{:S(2)}) collective-permute-start(f32[3,1,4,128]{3,2,1,0:T(4,128)} %get-tuple-element.266), channel_id=1, source_target_pairs={{0,64},{64,128},{128,192},{192,0},{1,65},{65,129},{129,193},{193,1... | collective-permute-start | bytes 18440 | tf_op jit(solution)/shard_map/ppermute | solution.py:406
  71.2 15.7 %all-to-all-start = ((f32[16,1,128]{2,1,0:T(1,128)}), f32[16,1,128]{2,1,0:T(1,128)S(1)}, u32[]{:S(2)}, u32[]{:S(2)}) async-start(f32[16,1,128]{2,1,0:T(1,128)} %bitcast.27), calls=%async_computation | async-start | bytes 16384 | tf_op jit(solution)/shard_map/all_to_all | solution.py:479
  79.9 7.0 %copy-start.1 = (f32[3,2,4,128]{3,2,1,0:T(4,128)}, f32[3,2,4,128]{3,2,1,0:T(4,128)S(1)}, u32[]{:S(2)}) copy-start(f32[3,2,4,128]{3,2,1,0:T(4,128)S(1)} %maximum_add_fusion.3.x_ref) | copy-start | bytes 36868
  79.9 4.0 %collective-permute-start.14 = (f32[3,2,1,128]{3,2,1,0:T(1,128)S(1)}, f32[3,2,1,128]{3,2,1,0:T(1,128)S(1)}, u32[]{:S(2)}, u32[]{:S(2)}) collective-permute-start(f32[3,2,1,128]{3,2,1,0:T(1,128)S(1)} %get-tuple-element.436), channel_id=1, source_target_pairs={{0,16},{16,32},{32,48},{48,0},{1,17},{17,33},{33,49},{49,1},{2,18}... | collective-permute-start | bytes 9224 | tf_op jit(solution)/shard_map/ppermute | solution.py:406
  80.0 3.9 %collective-permute-start.15 = (f32[3,2,1,128]{3,2,1,0:T(1,128)S(1)}, f32[3,2,1,128]{3,2,1,0:T(1,128)S(1)}, u32[]{:S(2)}, u32[]{:S(2)}) collective-permute-start(f32[3,2,1,128]{3,2,1,0:T(1,128)S(1)} %get-tuple-element.435), channel_id=1, source_target_pairs={{0,48},{16,0},{32,16},{48,32},{1,49},{17,1},{33,17},{49,33},{2,50}... | collective-permute-start | bytes 9224 | tf_op jit(solution)/shard_map/ppermute | solution.py:406
  83.9 3.0 %copy-start.7 = (f32[3,2,1,128]{3,2,1,0:T(1,128)}, f32[3,2,1,128]{3,2,1,0:T(1,128)S(1)}, u32[]{:S(2)}) copy-start(f32[3,2,1,128]{3,2,1,0:T(1,128)S(1)} %collective-permute-done.14.below_ref) | copy-start | bytes 9220
  83.9 3.0 %copy-start.8 = (f32[3,2,1,128]{3,2,1,0:T(1,128)}, f32[3,2,1,128]{3,2,1,0:T(1,128)S(1)}, u32[]{:S(2)}) copy-start(f32[3,2,1,128]{3,2,1,0:T(1,128)S(1)} %collective-permute-done.15.above_ref) | copy-start | bytes 9220
  86.9 0.6 copy-start.3

commit v3 on v2

--- a/solution.py
+++ b/solution.py
@@ -374,31 +374,68 @@
         rows_ref[row : row + 1, :] = line
 
 
-def prepare_weights(w_radial, w_env, w_latent, w_out):
-    top = w_latent[0:128]
-    both = jnp.dot(
-        w_env.astype(F32), w_latent[128:256].astype(F32), precision=lax.Precision.HIGHEST
+def prepare_kernel(
+    near_ref, list_ref, radial_ref, env_ref, latent_ref, out_ref,
+    key_ref, listed_ref, wr_ref, wtf_ref, wtop_ref, webf_ref, web_ref, wo_ref,
+):
+    lane = lax.broadcasted_iota(jnp.int32, (USED, 128), 1)
+    for block in range(4):
+        cx, cy = block // 2, block % 2
+        codes = [near_ref[USED * part : USED * part + USED, cx, cy, :] for part in range(4)]
+        for layer in range(4):
+            code = codes[0] if layer == 0 else pltpu.roll(codes[0], 128 - 32 * layer, 1)
+            for part in range(1, 4):
+                turn = 32 * (part - layer) % 128
+                moved = pltpu.roll(codes[part], turn, 1) if turn else codes[part]
+                code = jnp.where(lane // 32 == part, moved, code)
+            offset = code >> 5
+            third = (offset * 43) >> 7
+            ninth = (third * 43) >> 7
+            col = (cx + ninth) * 4 + cy + third - 3 * ninth
+            place = (layer + offset - 3 * third) * 32 + (code & 31)
+            key_ref[block, layer] = jnp.concatenate(
+                [col * 256 + place, jnp.zeros((ROWS - USED, 128), jnp.int32)], axis=0
+            )
+    for row in range(16):
+        line = list_ref[0, :, 128 * (row // 4) : 128 * (row // 4) + 128]
+        turn = 32 * (-row % 4)
+        listed_ref[row : row + 1, :] = pltpu.roll(line, turn, 1) if turn else line
+    radial = 0.5 * radial_ref[...]
+    high = radial.astype(BF16).astype(F32)
+    zero = jnp.zeros_like(high)
+    parts = [high, high, radial - high, zero]
+    wr_ref[0:128, :] = jnp.concatenate(parts + [zero] * 12, axis=0).T[:, 0:64].astype(BF16)
+    wr_ref[128:256, :] = (
+        jnp.concatenate([zero] * 4 + parts + [zero] * 8, axis=0).T[:, 0:64].astype(BF16)
     )
-    high = w_radial.astype(BF16)
-    low = (w_radial - high.astype(F32)).astype(BF16)
-    half = BF16(0.5)
-    wr = jnp.concatenate([high, high, low, jnp.zeros_like(low)], axis=0).T * half
-    wr = jnp.concatenate([jnp.pad(wr, ((0, 0), (0, 32))), jnp.pad(wr, ((0, 0), (32, 0)))], axis=0)
-    wo = jnp.broadcast_to(w_out.astype(F32)[:, None], (128, 256))
-    return (wr, top.T * half, top, (0.5 * both).T.astype(BF16), both.astype(BF16), wo)
-
-
-def neighbour_keys(neighbours):
-    code = neighbours.reshape(4, 6, 2, 2, 4, 32)
-    offset = code // 32
-    slot = code % 32
-    grid = lambda n, dim: jnp.arange(n, dtype=jnp.int32).reshape(
-        tuple(n if d == dim else 1 for d in range(6))
-    )
-    col = (grid(2, 2) + offset // 9) * 4 + grid(2, 3) + offset // 3 % 3
-    place = (grid(4, 4) + offset % 3) * 32 + slot
-    key = (col * 256 + place).transpose(2, 3, 4, 1, 0, 5).reshape(4, 4, USED, 128)
-    return jnp.pad(key, ((0, 0), (0, 0), (0, ROWS - USED), (0, 0)))
+    top = latent_ref[0:128, :]
+    wtop_ref[...] = top
+    wtf_ref[...] = (0.5 * top.astype(F32)).T.astype(BF16)
+    both = dot(env_ref[...], latent_ref[128:256, :])
+    web_ref[...] = both.astype(BF16)
+    webf_ref[...] = (0.5 * both).T.astype(BF16)
+    readout = jnp.broadcast_to(out_ref[...].astype(F32), (128, 128)).T
+    wo_ref[:, 0:128] = readout
+    wo_ref[:, 128:256] = readout
+
+
+def prepare(neighbours, send_list, w_radial, w_env, w_latent, w_out):
+    square = jax.ShapeDtypeStruct((128, 128), BF16)
+    key, listed, *weights = pl.pallas_call(
+        prepare_kernel,
+        out_shape=(
+            jax.ShapeDtypeStruct((4, 4, ROWS, 128), jnp.int32),
+            jax.ShapeDtypeStruct((16, 128), jnp.int32),
+            jax.ShapeDtypeStruct((256, 64), BF16),
+            square,
+            square,
+            square,
+            square,
+            jax.ShapeDtypeStruct((128, 256), F32),
+        ),
+        name="prepare",
+    )(neighbours, send_list, w_radial, w_env, w_latent, w_out.reshape(1, 128))
+    return key, listed, weights
 
 
 def shifted(array, axis, step):
@@ -434,9 +471,7 @@
     w_latent,
     w_out,
 ):
-    weights = prepare_weights(w_radial, w_env, w_latent, w_out)
-    key = neighbour_keys(neighbours)
-    listed = jnp.pad(send_list.reshape(16, 32), ((0, 0), (0, 96)))
+    key, listed, weights = prepare(neighbours, send_list, w_radial, w_env, w_latent, w_out)
     half = TIME_STEP
     own = jax.ShapeDtypeStruct((3, 2, 2, 128), F32)
     vmem, smem = (pl.BlockSpec(memory_space=space) for space in (pltpu.VMEM, pltpu.SMEM))

time: 90.3 us -> 85.3 us (0.945)
  waiting for transfers between devices: 12.7 us -> 7.66 us
  starting transfers between devices: 36.6 us -> 41.4 us
  local copies, waits for them, and re-layouts: 6.73 us -> 3.02 us
  other arithmetic: 2.32 us -> 0.34 us
  Pallas kernels: 30 us -> 31.3 us
    ppermute x20, starting transfers between devices: 27.9 us -> 32.9 us  [shifted(): lax.ppermute(array, axis, [(i, (i + step) % peers) for i in range(peers)])]
    all_to_all x1, waiting for transfers between devices: 2.97 us -> 0.31 us  [on_device(): lax.all_to_all(sent, 'gz', split_axis=0, concat_axis=0, tiled=True)]
    ppermute x20, waiting for transfers between devices: 9.71 us -> 7.35 us  [shifted(): lax.ppermute(array, axis, [(i, (i + step) % peers) for i in range(peers)])]
    unnamed x30 -> x15, local copies, waits for them, and re-layouts: 3.57 us -> 1.3 us
    transpose x1 -> x0, other arithmetic: 1.22 us -> none  [neighbour_keys(): (col * 256 + place).transpose(2, 3, 4, 1, 0, 5).reshape(4, 4, USED, 128)]
    reshape x3 -> x0, local copies, waits for them, and re-layouts: 1.19 us -> none  [the longest x1 0.95 us: neighbour_keys(): code = neighbours.reshape(4, 6, 2, 2, 4, 32)]
    pallas_call x0 -> x1, Pallas kernels: none -> 1.16 us  [prepare(): pl.pallas_call(prepare_kernel, out_shape=(jax.ShapeDtypeStruct((4, 4, ROW...]
  transfers between devices with their start and end apart: 21 -> 21, of which waited for: 7 -> 7; matrix products, arithmetic and copies ran while one was open for 5% -> 0% of each run, Pallas kernels for 16% -> 18%
where the time goes in v3:
time: 85.3 us; the launch traced here: 84.9 us
  starting transfers between devices  41.4 us (49%)
  Pallas kernels  31.3 us (37%)
  waiting for transfers between devices  7.66 us (9%)
  local copies, waits for them, and re-layouts  3.02 us (4%)
  between operations  0.91 us (1%)
    ppermute x20, starting transfers between devices, shifted(): lax.ppermute(array, axis, [(i, (i + step) % peers) for i in range(peers)])  32.9 us
    pallas_call x6, Pallas kernels, force_call(): pl.pallas_call(functools.partial(force_kernel, blocks, layers, first, las...  26.5 us
    all_to_all x1, starting transfers between devices, on_device(): lax.all_to_all(sent, 'gz', split_axis=0, concat_axis=0, tiled=True)  8.55 us
    ppermute x20, waiting for transfers between devices, shifted(): lax.ppermute(array, axis, [(i, (i + step) % peers) for i in range(peers)])  7.35 us
    pallas_call x1, Pallas kernels, on_device(): pl.pallas_call(finish_kernel, out_shape=(own, own, own, jax.ShapeDtypeStr...  2.19 us
  transfers between devices with their start and end apart: 21, of which 7 were waited for; matrix products, arithmetic and copies ran while one was open for 0% of the time, Pallas kernels for 18%

profile of v3, /device:TPU:1, one launch (start us, length us, event | category | flops | bytes accessed | tf_op | source)
XLA Modules:
  0.0 84.9 jit_solution(15264670920462499807)
XLA Ops:
  0.6 1.4 %begin.1 = (f32[6,1,2,128]{3,2,1,0:T(2,128)}, f32[6,1,2,128]{3,2,1,0:T(2,128)}, f32[3,2,2,128]{3,2,1,0:T(2,128)}) custom-call(f32[3,2,2,128]{3,2,1,0:T(2,128)} %positions_ref.1, f32[3,2,2,128]{3,2,1,0:T(2,128)} %velocities_ref.1, f32[3,2,2,128]{3,2,1,0:T(2,128)} %forces_ref.1, s32[2,2,4]{2,1,0:T(2,128)} %count_ref.3), custom_call_target="tpu_custom_call" | custom-call | tf_op jit(solution)/shard_map/begin/pallas_call | solution.py:479
  2.1 2.0 %collective-permute-start.8 = (f32[6,1,2,128]{3,2,1,0:T(2,128)}, f32[6,1,2,128]{3,2,1,0:T(2,128)S(1)}, u32[]{:S(2)}, u32[]{:S(2)}) collective-permute-start(f32[6,1,2,128]{3,2,1,0:T(2,128)} %get-tuple-element.270), channel_id=1, source_target_pairs={{0,64},{64,128},{128,192},{192,0},{1,65},{65,129},{129,193},{193,1... | collective-permute-start | bytes 18440 | tf_op jit(solution)/shard_map/ppermute | solution.py:443
  4.1 1.4 %collective-permute-start.9 = (f32[6,1,2,128]{3,2,1,0:T(2,128)}, f32[6,1,2,128]{3,2,1,0:T(2,128)S(1)}, u32[]{:S(2)}, u32[]{:S(2)}) collective-permute-start(f32[6,1,2,128]{3,2,1,0:T(2,128)} %get-tuple-element.271), channel_id=1, source_target_pairs={{0,192},{64,0},{128,64},{192,128},{1,193},{65,1},{129,65},{193,129... | collective-permute-start | bytes 18440 | tf_op jit(solution)/shard_map/ppermute | solution.py:443
  5.5 1.1 %collective-permute-done.8 = f32[6,1,2,128]{3,2,1,0:T(2,128)S(1)} collective-permute-done((f32[6,1,2,128]{3,2,1,0:T(2,128)}, f32[6,1,2,128]{3,2,1,0:T(2,128)S(1)}, u32[]{:S(2)}, u32[]{:S(2)}) %collective-permute-start.8) | collective-permute-done | bytes 6176 | tf_op jit(solution)/shard_map/ppermute | solution.py:443
  6.6 0.7 copy-done.3
  7.4 1.6 %collective-permute-start.10 = (f32[6,4,1,128]{3,2,1,0:T(1,128)S(1)}, f32[6,4,1,128]{3,2,1,0:T(1,128)S(1)}, u32[]{:S(2)}, u32[]{:S(2)}) collective-permute-start(f32[6,4,1,128]{3,2,1,0:T(1,128)S(1)} %get-tuple-element.392), channel_id=1, source_target_pairs={{0,16},{16,32},{32,48},{48,0},{1,17},{17,33},{33,49},{49,1},{2,18}... | collective-permute-start | bytes 36872 | tf_op jit(solution)/shard_map/ppermute | solution.py:443
  8.9 1.5 %collective-permute-start.11 = (f32[6,4,1,128]{3,2,1,0:T(1,128)S(1)}, f32[6,4,1,128]{3,2,1,0:T(1,128)S(1)}, u32[]{:S(2)}, u32[]{:S(2)}) collective-permute-start(f32[6,4,1,128]{3,2,1,0:T(1,128)S(1)} %get-tuple-element.393), channel_id=1, source_target_pairs={{0,48},{16,0},{32,16},{48,32},{1,49},{17,1},{33,17},{49,33},{2,50}... | collective-permute-start | bytes 36872 | tf_op jit(solution)/shard_map/ppermute | solution.py:443
  10.5 1.2 %prepare.1 = (s32[4,4,8,128]{3,2,1,0:T(8,128)S(1)}, s32[16,128]{1,0:T(8,128)S(1)}, bf16[256,64]{1,0:T(8,128)(2,1)S(1)}, bf16[128,128]{1,0:T(8,128)(2,1)S(1)}, bf...) custom-call(s32[24,2,2,128]{3,2,1,0:T(2,128)} %near_ref.1, ...), custom_call_target="tpu_custom_call" | custom-call | tf_op jit(solution)/shard_map/prepare/pallas_call | solution.py:424
  11.7 51.8 %while.27 = (s32[]{:T(128)}, f32[3,4,4,128]{3,2,1,0:T(4,128)S(1)}, f32[3,4,4,128]{3,2,1,0:T(4,128)S(1)}, f32[3,4,4,128]{3,2,1,0:T(4,128)S(1)}, f32[3,1,4,128]{3,...) while((s32[]{:T(128)}, f32[3,4,4,128]{3,2,1,0:T(4,128)S(1)}, ...), condition=%wide.region_3.0_spmd.clone, body=%wide.region_0.0_spmd.clone.sunk | while | flops 12800104448 | bytes 1848244 | solution.py:513
  12.1 4.6 %collective-permute-start.4 = (f32[48,32]{1,0:T(8,128)S(1)}, f32[48,32]{1,0:T(8,128)S(1)}, u32[]{:S(2)}, u32[]{:S(2)}) collective-permute-start(f32[48,32]{1,0:T(8,128)S(1)} %get-tuple-element.504), channel_id=1, source_target_pairs={{0,1},{1,2},{2,3},{3,4},{4,5},{5,6},{6,7},{7,8},{8,9},{9,10},{10,1... | collective-permute-start | bytes 18440 | tf_op jit(solution)/shard_map/while/body/eval_jaxpr/ppermute | solution.py:443
  16.7 3.3 %force.15 = (f32[48,128]{1,0:T(8,128)S(1)}, f32[8,128]{1,0:T(8,128)S(1)}) custom-call(f32[48,128]{1,0:T(8,128)S(1)} %bitcast.11, s32[4,4,8,128]{3,2,1,0:T(8,128)S(1)} %get-tuple-element.565.refs_1_, bf16[256,64]{1,0:T(8,128)(2,1)S(1)} %get-tuple-element.566.refs_2_, bf16[128,128]{1,0:T(8,128)(2,1)S(1)} %get-tuple-element.567.refs_3_, ...), custom_call_target="tpu_custom_call" | custom-call | flops 3200000000 | bytes 300000 | tf_op jit(solution)/shard_map/while/body/eval_jaxpr/force/pallas_call | solution.py:303
  20.2 6.2 %force.16 = (f32[48,128]{1,0:T(8,128)S(1)}, f32[8,128]{1,0:T(8,128)S(1)}, f32[48,128]{1,0:T(8,128)S(1)}) custom-call(f32[48,128]{1,0:T(8,128)S(1)} %bitcast.12, s32[4,4,8,128]{3,2,1,0:T(8,128)S(1)} %get-tuple-element.565.refs_1_, bf16[256,64]{1,0:T(8,128)(2,1)S(1)} %get-tuple-element.566.refs_2_, bf16[128,128]{1,0:T(8,128)(2,1)S(1)} %get-tuple-element.567.refs_3_, ...), custom_call_target="tpu_custom_call" | custom-call | flops 6400000000 | bytes 300000 | tf_op jit(solution)/shard_map/while/body/eval_jaxpr/force/pallas_call | solution.py:303
  26.5 2.7 %collective-permute-start.6 = (f32[48,32]{1,0:T(8,128)S(1)}, f32[48,32]{1,0:T(8,128)S(1)}, u32[]{:S(2)}, u32[]{:S(2)}) collective-permute-start(f32[48,32]{1,0:T(8,128)S(1)} %get-tuple-element.512), channel_id=1, source_target_pairs={{0,15},{1,0},{2,1},{3,2},{4,3},{5,4},{6,5},{7,6},{8,7},{9,8},{10,9... | collective-permute-start | bytes 18440 | tf_op jit(solution)/shard_map/while/body/eval_jaxpr/ppermute | solution.py:443
  29.1 3.8 %force.17 = (f32[48,128]{1,0:T(8,128)S(1)}, f32[16,128]{1,0:T(8,128)}) custom-call(f32[48,128]{1,0:T(8,128)S(1)} %bitcast.13, s32[4,4,8,128]{3,2,1,0:T(8,128)S(1)} %get-tuple-element.565.refs_1_, bf16[256,64]{1,0:T(8,128)(2,1)S(1)} %get-tuple-element.566.refs_2_, bf16[128,128]{1,0:T(8,128)(2,1)S(1)} %get-tuple-element.567.refs_3_, ...), custom_call_target="tpu_custom_call" | custom-call | flops 3200000000 | bytes 300000 | tf_op jit(solution)/shard_map/while/body/eval_jaxpr/force/pallas_call | solution.py:303
  33.0 0.6 fusion.12
  33.6 8.0 %conditional.3 = (f32[6,4,4,128]{3,2,1,0:T(4,128)S(1)}) conditional(s32[]{:T(128)} %convert_element_type.9, f32[3,4,4,128]{3,2,1,0:T(4,128)S(1)} %get-tuple-element.540, f32[6,4,4,128]{3,2,1,0:T(4,128)S(1)} %get-tuple-element.564), branch_computations={%region_1.0_spmd, %region_2.0_spmd} | conditional | flops 49152 | bytes 565416 | solution.py:495
  33.6 2.7 %collective-permute-start.1 = (f32[3,2,4,128]{3,2,1,0:T(4,128)S(1)}, f32[3,2,4,128]{3,2,1,0:T(4,128)S(1)}, u32[]{:S(2)}, u32[]{:S(2)}) collective-permute-start(f32[3,2,4,128]{3,2,1,0:T(4,128)S(1)} %get-tuple-element.383), channel_id=1, source_target_pairs={{0,192},{64,0},{128,64},{192,128},{1,193},{65,1},{129,65},{193,129... | collective-permute-start | bytes 36872 | tf_op jit(solution)/shard_map/while/body/eval_jaxpr/cond/branch_0_fun/ppermute | solution.py:443
  36.3 1.1 %collective-permute-done = f32[3,2,4,128]{3,2,1,0:T(4,128)S(1)} collective-permute-done((f32[3,2,4,128]{3,2,1,0:T(4,128)S(1)}, f32[3,2,4,128]{3,2,1,0:T(4,128)S(1)}, u32[]{:S(2)}, u32[]{:S(2)}) %collective-permute-start) | collective-permute-done | bytes 12320 | tf_op jit(solution)/shard_map/while/body/eval_jaxpr/cond/branch_0_fun/ppermute | solution.py:443
  37.7 2.8 %collective-permute-start.3 = (f32[3,4,2,128]{3,2,1,0:T(2,128)S(1)}, f32[3,4,2,128]{3,2,1,0:T(2,128)S(1)}, u32[]{:S(2)}, u32[]{:S(2)}) collective-permute-start(f32[3,4,2,128]{3,2,1,0:T(2,128)S(1)} %get-tuple-element.381), channel_id=1, source_target_pairs={{0,48},{16,0},{32,16},{48,32},{1,49},{17,1},{33,17},{49,33},{2,50}... | collective-permute-start | bytes 36872 | tf_op jit(solution)/shard_map/while/body/eval_jaxpr/cond/branch_0_fun/ppermute | solution.py:443
  40.5 1.0 %collective-permute-done.2 = f32[3,4,2,128]{3,2,1,0:T(2,128)S(1)} collective-permute-done((f32[3,4,2,128]{3,2,1,0:T(2,128)S(1)}, f32[3,4,2,128]{3,2,1,0:T(2,128)S(1)}, u32[]{:S(2)}, u32[]{:S(2)}) %collective-permute-start.2) | collective-permute-done | bytes 12320 | tf_op jit(solution)/shard_map/while/body/eval_jaxpr/cond/branch_0_fun/ppermute | solution.py:443
  41.7 1.8 %collective-permute-start.4 = (f32[48,32]{1,0:T(8,128)S(1)}, f32[48,32]{1,0:T(8,128)S(1)}, u32[]{:S(2)}, u32[]{:S(2)}) collective-permute-start(f32[48,32]{1,0:T(8,128)S(1)} %get-tuple-element.504), channel_id=1, source_target_pairs={{0,1},{1,2},{2,3},{3,4},{4,5},{5,6},{6,7},{7,8},{8,9},{9,10},{10,1... | collective-permute-start | bytes 18440 | tf_op jit(solution)/shard_map/while/body/eval_jaxpr/ppermute | solution.py:443
  43.5 2.9 %collective-permute-start.5 = (f32[48,32]{1,0:T(8,128)S(1)}, f32[48,32]{1,0:T(8,128)S(1)}, u32[]{:S(2)}, u32[]{:S(2)}) collective-permute-start(f32[48,32]{1,0:T(8,128)S(1)} %get-tuple-element.505), channel_id=1, source_target_pairs={{0,15},{1,0},{2,1},{3,2},{4,3},{5,4},{6,5},{7,6},{8,7},{9,8},{10,9... | collective-permute-start | bytes 18440 | tf_op jit(solution)/shard_map/while/body/eval_jaxpr/ppermute | solution.py:443
  46.4 3.3 %force.15 = (f32[48,128]{1,0:T(8,128)S(1)}, f32[8,128]{1,0:T(8,128)S(1)}) custom-call(f32[48,128]{1,0:T(8,128)S(1)} %bitcast.11, s32[4,4,8,128]{3,2,1,0:T(8,128)S(1)} %get-tuple-element.565.refs_1_, bf16[256,64]{1,0:T(8,128)(2,1)S(1)} %get-tuple-element.566.refs_2_, bf16[128,128]{1,0:T(8,128)(2,1)S(1)} %get-tuple-element.567.refs_3_, ...), custom_call_target="tpu_custom_call" | custom-call | flops 3200000000 | bytes 300000 | tf_op jit(solution)/shard_map/while/body/eval_jaxpr/force/pallas_call | solution.py:303
  49.8 6.2 %force.16 = (f32[48,128]{1,0:T(8,128)S(1)}, f32[8,128]{1,0:T(8,128)S(1)}, f32[48,128]{1,0:T(8,128)S(1)}) custom-call(f32[48,128]{1,0:T(8,128)S(1)} %bitcast.12, s32[4,4,8,128]{3,2,1,0:T(8,128)S(1)} %get-tuple-element.565.refs_1_, bf16[256,64]{1,0:T(8,128)(2,1)S(1)} %get-tuple-element.566.refs_2_, bf16[128,128]{1,0:T(8,128)(2,1)S(1)} %get-tuple-element.567.refs_3_, ...), custom_call_target="tpu_custom_call" | custom-call | flops 6400000000 | bytes 300000 | tf_op jit(solution)/shard_map/while/body/eval_jaxpr/force/pallas_call | solution.py:303
  56.0 3.0 %collective-permute-start.6 = (f32[48,32]{1,0:T(8,128)S(1)}, f32[48,32]{1,0:T(8,128)S(1)}, u32[]{:S(2)}, u32[]{:S(2)}) collective-permute-start(f32[48,32]{1,0:T(8,128)S(1)} %get-tuple-element.512), channel_id=1, source_target_pairs={{0,15},{1,0},{2,1},{3,2},{4,3},{5,4},{6,5},{7,6},{8,7},{9,8},{10,9... | collective-permute-start | bytes 18440 | tf_op jit(solution)/shard_map/while/body/eval_jaxpr/ppermute | solution.py:443
  59.0 3.8 %force.17 = (f32[48,128]{1,0:T(8,128)S(1)}, f32[16,128]{1,0:T(8,128)}) custom-call(f32[48,128]{1,0:T(8,128)S(1)} %bitcast.13, s32[4,4,8,128]{3,2,1,0:T(8,128)S(1)} %get-tuple-element.565.refs_1_, bf16[256,64]{1,0:T(8,128)(2,1)S(1)} %get-tuple-element.566.refs_2_, bf16[128,128]{1,0:T(8,128)(2,1)S(1)} %get-tuple-element.567.refs_3_, ...), custom_call_target="tpu_custom_call" | custom-call | flops 3200000000 | bytes 300000 | tf_op jit(solution)/shard_map/while/body/eval_jaxpr/force/pallas_call | solution.py:303
  63.5 3.0 %collective-permute-start.13 = (f32[3,1,4,128]{3,2,1,0:T(4,128)}, f32[3,1,4,128]{3,2,1,0:T(4,128)S(1)}, u32[]{:S(2)}, u32[]{:S(2)}) collective-permute-start(f32[3,1,4,128]{3,2,1,0:T(4,128)} %get-tuple-element.283), channel_id=1, source_target_pairs={{0,192},{64,0},{128,64},{192,128},{1,193},{65,1},{129,65},{193,129... | collective-permute-start | bytes 18440 | tf_op jit(solution)/shard_map/ppermute | solution.py:443
  66.4 8.5 %all-to-all-start = ((f32[16,1,128]{2,1,0:T(1,128)}), f32[16,1,128]{2,1,0:T(1,128)S(1)}, u32[]{:S(2)}, u32[]{:S(2)}) async-start(f32[16,1,128]{2,1,0:T(1,128)} %bitcast.17), calls=%async_computation | async-start | bytes 16384 | tf_op jit(solution)/shard_map/all_to_all | solution.py:514
  75.0 2.7 %collective-permute-start.15 = (f32[3,2,1,128]{3,2,1,0:T(1,128)S(1)}, f32[3,2,1,128]{3,2,1,0:T(1,128)S(1)}, u32[]{:S(2)}, u32[]{:S(2)}) collective-permute-start(f32[3,2,1,128]{3,2,1,0:T(1,128)S(1)} %get-tuple-element.394), channel_id=1, source_target_pairs={{0,48},{16,0},{32,16},{48,32},{1,49},{17,1},{33,17},{49,33},{2,50}... | collective-permute-start | bytes 9224 | tf_op jit(solution)/shard_map/ppermute | solution.py:443
  77.7 0.7 collective-permute-done.15.above_ref
  78.5 3.2 %collective-permute-done.14.below_ref = f32[3,2,1,128]{3,2,1,0:T(1,128)S(1)} collective-permute-done((f32[3,2,1,128]{3,2,1,0:T(1,128)S(1)}, f32[3,2,1,128]{3,2,1,0:T(1,128)S(1)}, u32[]{:S(2)}, u32[]{:S(2)}) %collective-permute-start.14) | collective-permute-done | bytes 3104 | tf_op jit(solution)/shard_map/ppermute | solution.py:443
  82.6 2.2 %finish.1 = (f32[3,2,2,128]{3,2,1,0:T(2,128)}, f32[3,2,2,128]{3,2,1,0:T(2,128)}, f32[3,2,2,128]{3,2,1,0:T(2,128)}, f32[4,128]{1,0:T(4,128)}) custom-call(f32[16,128]{1,0:T(8,128)} %bitcast.16, f32[3,2,4,128]{3,2,1,0:T(4,128)} %copy-done, f32[3,2,1,128]{3,2,1,0:T(1,128)} %copy-done.5, f32[3,2,1,128]{3,2,1,0:T(1,128)} %copy-done.4, ...), custom_call_target="tpu_custom_call" | custom-call | tf_op jit(solution)/shard_map/finish/pallas_call | solution.py:519
  (68 shorter events, 2.9 us)
Async XLA Ops:
  2.1 4.5 %collective-permute-start.8 = (f32[6,1,2,128]{3,2,1,0:T(2,128)}, f32[6,1,2,128]{3,2,1,0:T(2,128)S(1)}, u32[]{:S(2)}, u32[]{:S(2)}) collective-permute-start(f32[6,1,2,128]{3,2,1,0:T(2,128)} %get-tuple-element.270), channel_id=1, source_target_pairs={{0,64},{64,128},{128,192},{192,0},{1,65},{65,129},{129,193},{193,1... | collective-permute-start | bytes 18440 | tf_op jit(solution)/shard_map/ppermute | solution.py:443
  4.1 2.5 %copy-start.2 = (f32[6,1,2,128]{3,2,1,0:T(2,128)S(1)}, f32[6,1,2,128]{3,2,1,0:T(2,128)}, u32[]{:S(2)}) copy-start(f32[6,1,2,128]{3,2,1,0:T(2,128)} %get-tuple-element.271) | copy-start | bytes 18436
  4.1 3.2 %collective-permute-start.9 = (f32[6,1,2,128]{3,2,1,0:T(2,128)}, f32[6,1,2,128]{3,2,1,0:T(2,128)S(1)}, u32[]{:S(2)}, u32[]{:S(2)}) collective-permute-start(f32[6,1,2,128]{3,2,1,0:T(2,128)} %get-tuple-element.271), channel_id=1, source_target_pairs={{0,192},{64,0},{128,64},{192,128},{1,193},{65,1},{129,65},{193,129... | collective-permute-start | bytes 18440 | tf_op jit(solution)/shard_map/ppermute | solution.py:443
  6.6 0.7 copy-start.3
  7.4 4.3 %collective-permute-start.10 = (f32[6,4,1,128]{3,2,1,0:T(1,128)S(1)}, f32[6,4,1,128]{3,2,1,0:T(1,128)S(1)}, u32[]{:S(2)}, u32[]{:S(2)}) collective-permute-start(f32[6,4,1,128]{3,2,1,0:T(1,128)S(1)} %get-tuple-element.392), channel_id=1, source_target_pairs={{0,16},{16,32},{32,48},{48,0},{1,17},{17,33},{33,49},{49,1},{2,18}... | collective-permute-start | bytes 36872 | tf_op jit(solution)/shard_map/ppermute | solution.py:443
  8.9 2.7 %collective-permute-start.11 = (f32[6,4,1,128]{3,2,1,0:T(1,128)S(1)}, f32[6,4,1,128]{3,2,1,0:T(1,128)S(1)}, u32[]{:S(2)}, u32[]{:S(2)}) collective-permute-start(f32[6,4,1,128]{3,2,1,0:T(1,128)S(1)} %get-tuple-element.393), channel_id=1, source_target_pairs={{0,48},{16,0},{32,16},{48,32},{1,49},{17,1},{33,17},{49,33},{2,50}... | collective-permute-start | bytes 36872 | tf_op jit(solution)/shard_map/ppermute | solution.py:443
  12.1 8.0 %collective-permute-start.4 = (f32[48,32]{1,0:T(8,128)S(1)}, f32[48,32]{1,0:T(8,128)S(1)}, u32[]{:S(2)}, u32[]{:S(2)}) collective-permute-start(f32[48,32]{1,0:T(8,128)S(1)} %get-tuple-element.504), channel_id=1, source_target_pairs={{0,1},{1,2},{2,3},{3,4},{4,5},{5,6},{6,7},{7,8},{8,9},{9,10},{10,1... | collective-permute-start | bytes 18440 | tf_op jit(solution)/shard_map/while/body/eval_jaxpr/ppermute | solution.py:443
  16.7 3.5 %collective-permute-start.5 = (f32[48,32]{1,0:T(8,128)S(1)}, f32[48,32]{1,0:T(8,128)S(1)}, u32[]{:S(2)}, u32[]{:S(2)}) collective-permute-start(f32[48,32]{1,0:T(8,128)S(1)} %get-tuple-element.505), channel_id=1, source_target_pairs={{0,15},{1,0},{2,1},{3,2},{4,3},{5,4},{6,5},{7,6},{8,7},{9,8},{10,9... | collective-permute-start | bytes 18440 | tf_op jit(solution)/shard_map/while/body/eval_jaxpr/ppermute | solution.py:443
  26.5 6.4 %collective-permute-start.6 = (f32[48,32]{1,0:T(8,128)S(1)}, f32[48,32]{1,0:T(8,128)S(1)}, u32[]{:S(2)}, u32[]{:S(2)}) collective-permute-start(f32[48,32]{1,0:T(8,128)S(1)} %get-tuple-element.512), channel_id=1, source_target_pairs={{0,15},{1,0},{2,1},{3,2},{4,3},{5,4},{6,5},{7,6},{8,7},{9,8},{10,9... | collective-permute-start | bytes 18440 | tf_op jit(solution)/shard_map/while/body/eval_jaxpr/ppermute | solution.py:443
  29.1 3.8 %collective-permute-start.7 = (f32[48,32]{1,0:T(8,128)S(1)}, f32[48,32]{1,0:T(8,128)S(1)}, u32[]{:S(2)}, u32[]{:S(2)}) collective-permute-start(f32[48,32]{1,0:T(8,128)S(1)} %get-tuple-element.513), channel_id=1, source_target_pairs={{0,1},{1,2},{2,3},{3,4},{4,5},{5,6},{6,7},{7,8},{8,9},{9,10},{10,1... | collective-permute-start | bytes 18440 | tf_op jit(solution)/shard_map/while/body/eval_jaxpr/ppermute | solution.py:443
  33.6 3.8 %collective-permute-start = (f32[3,2,4,128]{3,2,1,0:T(4,128)S(1)}, f32[3,2,4,128]{3,2,1,0:T(4,128)S(1)}, u32[]{:S(2)}, u32[]{:S(2)}) collective-permute-start(f32[3,2,4,128]{3,2,1,0:T(4,128)S(1)} %get-tuple-element.382), channel_id=1, source_target_pairs={{0,64},{64,128},{128,192},{192,0},{1,65},{65,129},{129,193},{193,1... | collective-permute-start | bytes 36872 | tf_op jit(solution)/shard_map/while/body/eval_jaxpr/cond/branch_0_fun/ppermute | solution.py:443
  33.6 3.8 %collective-permute-start.1 = (f32[3,2,4,128]{3,2,1,0:T(4,128)S(1)}, f32[3,2,4,128]{3,2,1,0:T(4,128)S(1)}, u32[]{:S(2)}, u32[]{:S(2)}) collective-permute-start(f32[3,2,4,128]{3,2,1,0:T(4,128)S(1)} %get-tuple-element.383), channel_id=1, source_target_pairs={{0,192},{64,0},{128,64},{192,128},{1,193},{65,1},{129,65},{193,129... | collective-permute-start | bytes 36872 | tf_op jit(solution)/shard_map/while/body/eval_jaxpr/cond/branch_0_fun/ppermute | solution.py:443
  37.4 4.1 %collective-permute-start.2 = (f32[3,4,2,128]{3,2,1,0:T(2,128)S(1)}, f32[3,4,2,128]{3,2,1,0:T(2,128)S(1)}, u32[]{:S(2)}, u32[]{:S(2)}) collective-permute-start(f32[3,4,2,128]{3,2,1,0:T(2,128)S(1)} %get-tuple-element.380), channel_id=1, source_target_pairs={{0,16},{16,32},{32,48},{48,0},{1,17},{17,33},{33,49},{49,1},{2,18}... | collective-permute-start | bytes 36872 | tf_op jit(solution)/shard_map/while/body/eval_jaxpr/cond/branch_0_fun/ppermute | solution.py:443
  37.7 3.8 %collective-permute-start.3 = (f32[3,4,2,128]{3,2,1,0:T(2,128)S(1)}, f32[3,4,2,128]{3,2,1,0:T(2,128)S(1)}, u32[]{:S(2)}, u32[]{:S(2)}) collective-permute-start(f32[3,4,2,128]{3,2,1,0:T(2,128)S(1)} %get-tuple-element.381), channel_id=1, source_target_pairs={{0,48},{16,0},{32,16},{48,32},{1,49},{17,1},{33,17},{49,33},{2,50}... | collective-permute-start | bytes 36872 | tf_op jit(solution)/shard_map/while/body/eval_jaxpr/cond/branch_0_fun/ppermute | solution.py:443
  41.7 8.1 %collective-permute-start.4 = (f32[48,32]{1,0:T(8,128)S(1)}, f32[48,32]{1,0:T(8,128)S(1)}, u32[]{:S(2)}, u32[]{:S(2)}) collective-permute-start(f32[48,32]{1,0:T(8,128)S(1)} %get-tuple-element.504), channel_id=1, source_target_pairs={{0,1},{1,2},{2,3},{3,4},{4,5},{5,6},{6,7},{7,8},{8,9},{9,10},{10,1... | collective-permute-start | bytes 18440 | tf_op jit(solution)/shard_map/while/body/eval_jaxpr/ppermute | solution.py:443
  43.5 6.3 %collective-permute-start.5 = (f32[48,32]{1,0:T(8,128)S(1)}, f32[48,32]{1,0:T(8,128)S(1)}, u32[]{:S(2)}, u32[]{:S(2)}) collective-permute-start(f32[48,32]{1,0:T(8,128)S(1)} %get-tuple-element.505), channel_id=1, source_target_pairs={{0,15},{1,0},{2,1},{3,2},{4,3},{5,4},{6,5},{7,6},{8,7},{9,8},{10,9... | collective-permute-start | bytes 18440 | tf_op jit(solution)/shard_map/while/body/eval_jaxpr/ppermute | solution.py:443
  56.0 6.7 %collective-permute-start.6 = (f32[48,32]{1,0:T(8,128)S(1)}, f32[48,32]{1,0:T(8,128)S(1)}, u32[]{:S(2)}, u32[]{:S(2)}) collective-permute-start(f32[48,32]{1,0:T(8,128)S(1)} %get-tuple-element.512), channel_id=1, source_target_pairs={{0,15},{1,0},{2,1},{3,2},{4,3},{5,4},{6,5},{7,6},{8,7},{9,8},{10,9... | collective-permute-start | bytes 18440 | tf_op jit(solution)/shard_map/while/body/eval_jaxpr/ppermute | solution.py:443
  59.0 3.8 %collective-permute-start.7 = (f32[48,32]{1,0:T(8,128)S(1)}, f32[48,32]{1,0:T(8,128)S(1)}, u32[]{:S(2)}, u32[]{:S(2)}) collective-permute-start(f32[48,32]{1,0:T(8,128)S(1)} %get-tuple-element.513), channel_id=1, source_target_pairs={{0,1},{1,2},{2,3},{3,4},{4,5},{5,6},{6,7},{7,8},{8,9},{9,10},{10,1... | collective-permute-start | bytes 18440 | tf_op jit(solution)/shard_map/while/body/eval_jaxpr/ppermute | solution.py:443
  63.5 11.5 %collective-permute-start.13 = (f32[3,1,4,128]{3,2,1,0:T(4,128)}, f32[3,1,4,128]{3,2,1,0:T(4,128)S(1)}, u32[]{:S(2)}, u32[]{:S(2)}) collective-permute-start(f32[3,1,4,128]{3,2,1,0:T(4,128)} %get-tuple-element.283), channel_id=1, source_target_pairs={{0,192},{64,0},{128,64},{192,128},{1,193},{65,1},{129,65},{193,129... | collective-permute-start | bytes 18440 | tf_op jit(solution)/shard_map/ppermute | solution.py:443
  66.4 8.6 %collective-permute-start.12 = (f32[3,1,4,128]{3,2,1,0:T(4,128)}, f32[3,1,4,128]{3,2,1,0:T(4,128)S(1)}, u32[]{:S(2)}, u32[]{:S(2)}) collective-permute-start(f32[3,1,4,128]{3,2,1,0:T(4,128)} %get-tuple-element.282), channel_id=1, source_target_pairs={{0,64},{64,128},{128,192},{192,0},{1,65},{65,129},{129,193},{193,1... | collective-permute-start | bytes 18440 | tf_op jit(solution)/shard_map/ppermute | solution.py:443
  66.4 15.6 %all-to-all-start = ((f32[16,1,128]{2,1,0:T(1,128)}), f32[16,1,128]{2,1,0:T(1,128)S(1)}, u32[]{:S(2)}, u32[]{:S(2)}) async-start(f32[16,1,128]{2,1,0:T(1,128)} %bitcast.17), calls=%async_computation | async-start | bytes 16384 | tf_op jit(solution)/shard_map/all_to_all | solution.py:514
  75.0 7.0 %copy-start = (f32[3,2,4,128]{3,2,1,0:T(4,128)}, f32[3,2,4,128]{3,2,1,0:T(4,128)S(1)}, u32[]{:S(2)}) copy-start(f32[3,2,4,128]{3,2,1,0:T(4,128)S(1)} %maximum_add_fusion.3.x_ref) | copy-start | bytes 36868
  75.0 3.4 %collective-permute-start.15 = (f32[3,2,1,128]{3,2,1,0:T(1,128)S(1)}, f32[3,2,1,128]{3,2,1,0:T(1,128)S(1)}, u32[]{:S(2)}, u32[]{:S(2)}) collective-permute-start(f32[3,2,1,128]{3,2,1,0:T(1,128)S(1)} %get-tuple-element.394), channel_id=1, source_target_pairs={{0,48},{16,0},{32,16},{48,32},{1,49},{17,1},{33,17},{49,33},{2,50}... | collective-permute-start | bytes 9224 | tf_op jit(solution)/shard_map/ppermute | solution.py:443
  77.7 4.0 %collective-permute-start.14 = (f32[3,2,1,128]{3,2,1,0:T(1,128)S(1)}, f32[3,2,1,128]{3,2,1,0:T(1,128)S(1)}, u32[]{:S(2)}, u32[]{:S(2)}) collective-permute-start(f32[3,2,1,128]{3,2,1,0:T(1,128)S(1)} %get-tuple-element.395), channel_id=1, source_target_pairs={{0,16},{16,32},{32,48},{48,0},{1,17},{17,33},{33,49},{49,1},{2,18}... | collective-permute-start | bytes 9224 | tf_op jit(solution)/shard_map/ppermute | solution.py:443
  78.5 3.5 %copy-start.4 = (f32[3,2,1,128]{3,2,1,0:T(1,128)}, f32[3,2,1,128]{3,2,1,0:T(1,128)S(1)}, u32[]{:S(2)}) copy-start(f32[3,2,1,128]{3,2,1,0:T(1,128)S(1)} %collective-permute-done.15.above_ref) | copy-start | bytes 9220
  81.7 0.6 copy-start.5
  82.0 0.6 copy-start.1
